TPU v7x, 32 devices: a whole 2x2x4 slice. The times are simulated.
32 devices in a mesh: parts: 2 (over y), gx: 4 (over z), gy: 2 (over x), gz: 2 (over core).
Axes of the slice: x: 2, y: 2, z: 4, core: 2. Of those that a mesh axis runs over, the one named last changes fastest.
Arguments:
- electric: float32 [4, 4, 2, 3, 65536], P(('parts', 'gy'), 'gx', 'gz'), parts along dimension 0, may hold values from -6 to 6
- magnetic: float32 [4, 4, 2, 3, 65536], P(('parts', 'gy'), 'gx', 'gz'), parts along dimension 0, may hold values from -6 to 6
- material: int32 [4, 4, 2, 65536], P(('parts', 'gy'), 'gx', 'gz'), parts along dimension 0, may hold values from 0 to 3
- permittivity: float32 [4], replicated, may hold values from 1 to 12
Outputs:
- electric_next: float32 [4, 4, 2, 3, 65536], P(('parts', 'gy'), 'gx', 'gz'), parts along dimension 0
- magnetic_next: float32 [4, 4, 2, 3, 65536], P(('parts', 'gy'), 'gx', 'gz'), parts along dimension 0
There are 2 independent parts, one for each index of `parts`. A program takes and returns all parts, laid end to end along the dimension named above; an argument that names none is the same for every part. Nothing has to cross between parts.
All inputs are finite; a program needn't handle non-finite values.
Results may differ from a plain program's by a relative error of at most 0.0003.
Values sent between devices are 32-bit elements; how exact they have to be, the bound alone decides.
No kernel may reach another device: no remote copies, remote signals or barrier semaphores. Data moves between devices by JAX's collectives and lax.ppermute only.
A program may use at most 64 MiB of HBM per device.

v0:
```python
from functools import partial

import jax
import jax.numpy as jnp
from jax import lax
from jax.experimental import pallas as pl
from jax.experimental.pallas import tpu as pltpu
from jax.sharding import PartitionSpec as P

CZ = 4
CX = 32
CY = 512
MATS = 4


courant = 0.5


def passed_along(x, axis, by):
    devices = lax.axis_size(axis)
    return lax.ppermute(x, axis, [(i, (i + by) % devices) for i in range(devices)])


def from_behind(x, axis, by):
    devices = lax.axis_size(axis)
    pairs = [(i, i + by) for i in range(devices) if 0 <= i + by < devices]
    return lax.ppermute(x, axis, pairs)


def forward_diff(values, dim_axis, ghost_plane):
    shifted = jnp.concatenate(
        [
            lax.slice_in_dim(values, 1, values.shape[dim_axis], axis=dim_axis),
            jnp.expand_dims(ghost_plane, dim_axis),
        ],
        axis=dim_axis,
    )
    return shifted - values


def backward_diff(values, dim_axis, ghost_plane):
    shifted = jnp.concatenate(
        [
            jnp.expand_dims(ghost_plane, dim_axis),
            lax.slice_in_dim(values, 0, values.shape[dim_axis] - 1, axis=dim_axis),
        ],
        axis=dim_axis,
    )
    return values - shifted


def curl_with(differ, vectors, ghost_depth, ghost_width, ghost_height):
    ghosts = (ghost_depth, ghost_width, ghost_height)

    def along_axis(component, dim_axis):
        return differ(vectors[component], dim_axis, ghosts[dim_axis][component])

    curl_x = along_axis(2, 2) - along_axis(1, 0)
    curl_y = along_axis(0, 0) - along_axis(2, 1)
    curl_z = along_axis(1, 1) - along_axis(0, 2)
    return jnp.stack([curl_x, curl_y, curl_z])


def restrict(face_plane):
    quads = face_plane.reshape(3, face_plane.shape[1] // 2, 2, face_plane.shape[2] // 2, 2)
    return (
        quads[:, :, 0, :, 0] + quads[:, :, 0, :, 1] + (quads[:, :, 1, :, 0] + quads[:, :, 1, :, 1])
    ) * 0.25


def enlarge(face_plane):
    return jnp.repeat(jnp.repeat(face_plane, 2, axis=1), 2, axis=2)


def lookup(material, permittivity):
    permit_sum = jnp.zeros(material.shape, jnp.float32)
    for material_id in range(MATS):
        permit_sum = permit_sum + jnp.where(material == material_id, permittivity[material_id], 0.0)
    return courant / permit_sum


def pack_face(face_plane, length):
    flat_face = face_plane.reshape(3, -1)
    if flat_face.shape[1] < length:
        flat_face = jnp.concatenate(
            [flat_face, jnp.zeros((3, length - flat_face.shape[1]), flat_face.dtype)], axis=1
        )
    return flat_face


def unpack_face(flat_face, row_count, col_count):
    return flat_face[:, : row_count * col_count].reshape(3, row_count, col_count)


def level_height(got_height, is_fine):
    return got_height if is_fine else restrict(got_height)


def low_faces(grid_shape, is_fine, flat_field):
    vectors = flat_field.reshape((3,) + grid_shape)
    face_plane = vectors[:, :, :, 0]
    if not is_fine:
        face_plane = enlarge(face_plane)
    return (
        pack_face(vectors[:, :, 0, :], CZ * CY),
        pack_face(vectors[:, 0, :, :], CX * CY),
        face_plane,
    )


def high_faces(grid_shape, is_fine, flat_field):
    vectors = flat_field.reshape((3,) + grid_shape)
    face_plane = vectors[:, :, :, -1]
    if not is_fine:
        face_plane = enlarge(face_plane)
    return (
        pack_face(vectors[:, :, -1, :], CZ * CY),
        pack_face(vectors[:, -1, :, :], CX * CY),
        face_plane,
    )


def advance_magnetic(
    grid_shape, is_fine, does_move, e_flat, h_flat, got_width, got_depth, got_height
):
    if not does_move:
        return h_flat
    deep_cells, wide_cells, tall_cells = grid_shape
    vectors = e_flat.reshape((3,) + grid_shape)
    curl_term = curl_with(
        forward_diff,
        vectors,
        unpack_face(got_depth, wide_cells, tall_cells),
        unpack_face(got_width, deep_cells, tall_cells),
        level_height(got_height, is_fine),
    )
    return (h_flat.reshape((3,) + grid_shape) - courant * curl_term).reshape(3, -1)


def advance_electric(
    grid_shape, is_fine, does_move, e_flat, h_flat, coefficient, got_width, got_depth, got_height
):
    if not does_move:
        return e_flat
    deep_cells, wide_cells, tall_cells = grid_shape
    magnetic = h_flat.reshape((3,) + grid_shape)
    curl_term = curl_with(
        backward_diff,
        magnetic,
        unpack_face(got_depth, wide_cells, tall_cells),
        unpack_face(got_width, deep_cells, tall_cells),
        level_height(got_height, is_fine),
    )
    return (
        e_flat.reshape((3,) + grid_shape) + coefficient.reshape(grid_shape) * curl_term
    ).reshape(3, -1)


def pass_width(face_plane, offset):
    return passed_along(face_plane, "gx", offset)


def pass_depth(face_plane, offset):
    return from_behind(face_plane, "gz", offset)


def pass_height(face_plane, offset):
    return from_behind(face_plane, "gy", offset)


def general_shards(electric, magnetic, material, permittivity):
    cell_count = electric.shape[-1]
    e_flat = electric.reshape(3, cell_count)
    h_flat = magnetic.reshape(3, cell_count)
    coefficient = lookup(material.reshape(cell_count), permittivity)
    is_fine = lax.axis_index("gy") >= lax.axis_size("gy") // 2
    coarse_shape = (CZ, CX, CY)
    fine_shape = (2 * CZ, 2 * CX, CY // 4)
    for substep in range(2):
        coarse_moves = substep == 0
        face_width, face_depth, face_height = lax.cond(
            is_fine,
            partial(low_faces, fine_shape, True),
            partial(low_faces, coarse_shape, False),
            e_flat,
        )
        got_depth = pass_depth(face_depth, -1)
        got_height = pass_height(face_height, -1)
        got_width = pass_width(face_width, -1)
        h_flat = lax.cond(
            is_fine,
            partial(advance_magnetic, fine_shape, True, True),
            partial(advance_magnetic, coarse_shape, False, coarse_moves),
            e_flat,
            h_flat,
            got_width,
            got_depth,
            got_height,
        )
        rim_width, rim_depth, rim_height = lax.cond(
            is_fine,
            partial(high_faces, fine_shape, True),
            partial(high_faces, coarse_shape, False),
            h_flat,
        )
        rim_depth = pass_depth(rim_depth, 1)
        rim_height = pass_height(rim_height, 1)
        rim_width = pass_width(rim_width, 1)
        e_flat = lax.cond(
            is_fine,
            partial(advance_electric, fine_shape, True, True),
            partial(advance_electric, coarse_shape, False, coarse_moves),
            e_flat,
            h_flat,
            coefficient,
            rim_width,
            rim_depth,
            rim_height,
        )
    return (e_flat.reshape(electric.shape), h_flat.reshape(magnetic.shape))


ROWS = 512
HALO = 128
EXT = 1296
LIMIT = 40 * 1024 * 1024
F32 = jnp.float32
VM = pl.BlockSpec(memory_space=pltpu.VMEM)
HBM = pl.BlockSpec(memory_space=pltpu.HBM)
CHUNK = 32


class Fine:
    depth, stride, count, own, step, used, height, parts, last = 64, 72, 10, 8, 1, 10, 16, 1, 63


class Coarse:
    depth, stride, count, own, step, used, height, parts, last = 128, 144, 5, 4, 4, 5, 8, 4, 31


def vmem(*shape, dtype=F32):
    return pltpu.VMEM(shape, dtype)


def held(x):
    return pltpu.with_memory_space_constraint(x, pltpu.VMEM)


def far(x):
    return pltpu.with_memory_space_constraint(x, pltpu.HBM)


def kernel_call(body, out_shape, in_specs, out_specs, scratch=(), aliases=None):
    return pl.pallas_call(
        body,
        out_shape=out_shape,
        in_specs=in_specs,
        out_specs=out_specs,
        scratch_shapes=list(scratch),
        input_output_aliases=aliases or {},
        compiler_params=pltpu.CompilerParams(vmem_limit_bytes=LIMIT),
    )


def by_level(body):
    is_fine = lax.axis_index("gy") >= lax.axis_size("gy") // 2
    gz = lax.axis_index("gz")
    pl.when(is_fine)(lambda: body(Fine, gz))
    pl.when(jnp.logical_not(is_fine))(lambda: body(Coarse, gz))


def lanes_of(shape):
    return lax.broadcasted_iota(jnp.int32, shape, len(shape) - 1)


def rows_of(shape):
    return lax.broadcasted_iota(jnp.int32, shape, len(shape) - 2)


def roll_lanes(x, by):
    return pltpu.roll(x, by % 128, 1)


def roll_rows(x, by):
    return pltpu.roll(x, by % x.shape[0], 0)


def layer_row(grid, index):
    return pl.multiple_of(grid.stride * (index + 1), 8)


def own_first(grid, gz):
    return (grid.count - grid.own) * gz


def halo_first(grid, gz):
    return grid.own * (1 - gz)


def clear_pads(grid, ref, *zero_layers):
    for comp in range(3):
        for index in range(grid.count + 2):
            start, size = grid.stride * index, grid.stride
            if index not in zero_layers:
                start, size = start + grid.depth, size - grid.depth
            ref[comp, pl.ds(start, size), :] = jnp.zeros((size, 128), F32)


def own_layers(grid, ref, gz):
    view = ref.reshape(3, EXT // grid.stride, grid.stride, 128)
    return view.at[:, pl.ds(1 + own_first(grid, gz), grid.own), pl.ds(0, grid.depth), :]


def block_layers(grid, ref):
    return ref.reshape(3, grid.own, grid.depth, 128)


def at_lane(tile, lane_from, lane_to, value):
    lane = lanes_of(value.shape)
    return jnp.where(lane == lane_to, roll_lanes(value, lane_to - lane_from), tile)


def average(ref, lead, row, stride):
    steps = (0, 1, stride, stride + 1)
    quad = [ref[lead, pl.ds(row + step, 32, stride=2), :] for step in steps]
    return ((quad[0] + quad[1]) + (quad[2] + quad[3])) * 0.25


def put_column(tile, lane_from, slot, column):
    for block in range(4):
        tile = at_lane(tile, lane_from, 32 * block + slot, column[8 * block : 8 * block + 8])
    return tile


def gather(e_hbm, h_hbm, m_hbm, e_ext, zmsg, ytile, h_top, m_edge, sems):
    def body(grid, gz):
        edge = pl.ds((1 - gz) * (ROWS - HALO), HALO)
        source, target = block_layers(grid, e_hbm), own_layers(grid, e_ext, gz)
        first = [0, 2] if grid is Fine else [0, 1, 2]
        e_loads = {
            comp: pltpu.make_async_copy(source.at[comp], target.at[comp], sems.at[comp])
            for comp in (0, 2, 1)
        }
        h_loads = [] if grid is Fine else [
            pltpu.make_async_copy(h_hbm.at[comp], h_top.at[comp], sems.at[3 + comp]) for comp in (0, 2)
        ]
        loads = [
            pltpu.make_async_copy(h_hbm.at[:, edge], zmsg.at[pl.ds(3, 3)], sems.at[6]),
            pltpu.make_async_copy(m_hbm.at[edge], m_edge, sems.at[7]),
        ]
        for load in list(e_loads.values()) + h_loads + loads:
            load.start()
        clear_pads(grid, e_ext, grid.count + 1)
        for comp in first:
            e_loads[comp].wait()
        for load in h_loads:
            load.wait()
        begin = layer_row(grid, own_first(grid, gz))
        tile = jnp.zeros((8, 128), F32)
        for layer in range(4):
            if grid is Fine:
                row = begin + 2 * grid.stride * layer
                tile = put_column(tile, 0, layer, average(e_ext, 0, row, grid.stride))
                tile = put_column(tile, 0, 8 + layer, average(e_ext, 2, row, grid.stride))
            else:
                top = pl.ds(begin + grid.stride * layer + 3, 32, stride=4)
                h_row = pl.ds(grid.depth * layer + 3, 32, stride=4)
                ex, ey, ez = (e_ext[comp, top, :] for comp in range(3))
                tile = put_column(tile, 127, layer, h_top[0, h_row, :] + 0.5 * ez)
                tile = put_column(tile, 127, 8 + layer, h_top[2, h_row, :] - 0.5 * ex)
                tile = put_column(tile, 127, 16 + layer, ey)
        ytile[...] = jnp.where(gz == 1, roll_lanes(tile, 1), tile)
        if grid is Fine:
            e_loads[1].wait()
        layers = HALO // grid.depth
        from_layer = own_first(grid, gz) + (grid.own - layers) * (1 - gz)
        for comp in range(3):
            for layer in range(layers):
                row = layer_row(grid, from_layer + layer)
                zmsg[comp, pl.ds(grid.depth * layer, grid.depth), :] = e_ext[comp, pl.ds(row, grid.depth), :]
        for load in loads:
            load.wait()
        zmsg[6] = m_edge[...].astype(F32)

    by_level(body)


def up_y(grid, ref, comp, row, f):
    lane = lanes_of(f.shape)
    if grid is Fine:
        return jnp.where(lane == 127, 0.0, roll_lanes(f, -1))
    following = ref[comp, pl.ds(row + 1, f.shape[0]), :]
    following = jnp.where(rows_of(f.shape) % 4 == 3, 0.0, following)
    return roll_lanes(jnp.where(lane == 0, following, f), -1)


def down_y(grid, ref, comp, row, f, ghost):
    lane = lanes_of(f.shape)
    if grid is Fine:
        return roll_lanes(jnp.where(lane == 127, ghost, f), 1)
    previous = ref[comp, pl.ds(row - 1, f.shape[0]), :]
    previous = jnp.where(rows_of(f.shape) % 4 == 0, 0.0, previous)
    return roll_lanes(jnp.where(lane == 127, previous, f), 1)


def half_h(grid, e, h_from, from_row, h_to, row):
    for start in range(0, grid.depth, CHUNK):
        r = row + start
        here = pl.ds(r, CHUNK)
        ex, ey, ez = (e[comp, here, :] for comp in range(3))
        above, beside = pl.ds(r + grid.stride, CHUNK), pl.ds(r + grid.step, CHUNK)
        h0 = [h_from(comp, pl.ds(from_row + start, CHUNK)) for comp in range(3)]
        ez_y, ex_y = up_y(grid, e, 2, r, ez), up_y(grid, e, 0, r, ex)
        h_to[0, here, :] = h0[0] - 0.5 * ((ez_y - ez) - (e[1, above, :] - ey))
        h_to[1, here, :] = h0[1] - 0.5 * ((e[0, above, :] - ex) - (e[2, beside, :] - ez))
        h_to[2, here, :] = h0[2] - 0.5 * ((e[1, beside, :] - ey) - (ex_y - ex))


def half_e(grid, h, e_from, e_to, c_ref, row, ghosts):
    for start in range(0, grid.depth, CHUNK):
        r = row + start
        here = pl.ds(r, CHUNK)
        hx, hy, hz = (h[comp, here, :] for comp in range(3))
        below, beside = pl.ds(r - grid.stride, CHUNK), pl.ds(r - grid.step, CHUNK)
        px, pz = ghosts(start)
        hx_y, hz_y = down_y(grid, h, 0, r, hx, px), down_y(grid, h, 2, r, hz, pz)
        c = c_ref[here, :]
        e_to[0, here, :] = e_from[0, here, :] + c * ((hz - hz_y) - (hy - h[1, below, :]))
        e_to[1, here, :] = e_from[1, here, :] + c * ((hx - h[0, below, :]) - (hz - h[2, beside, :]))
        e_to[2, here, :] = e_from[2, here, :] + c * ((hy - h[1, beside, :]) - (hx - hx_y))


def loop(first, count, body):
    def step(index, carry):
        body(index)
        return carry

    lax.fori_loop(first, first + count, step, 0)


def with_halo(tile, halo_tile, gz):
    lane = lanes_of(tile.shape)
    return jnp.where(lane % 8 == 4 * (1 - gz), halo_tile, tile)


def joined(own, other, gz):
    return with_halo(own, jnp.where(gz == 0, roll_lanes(other, 3), roll_lanes(other, -3)), gz)


def column_of(tile, block, sub, slot, shape, per_layer):
    row = jnp.broadcast_to(tile[sub : sub + 1, :], shape)
    wanted = 32 * block + slot + rows_of(shape) // per_layer
    picked = jnp.where((lanes_of(shape) == wanted) & (rows_of(shape) < 5 * per_layer), row, 0.0)
    return jnp.broadcast_to(jnp.sum(picked, axis=1, keepdims=True), shape)


def column(grid, read, x):
    begin = grid.stride + grid.step * x
    planes = [read(pl.ds(begin + part, grid.height, stride=grid.stride)) for part in range(grid.parts)]
    return [jnp.where(rows_of(p.shape) < grid.used, p, 0.0) for p in planes]


def each(fn, *columns):
    return [fn(*parts) for parts in zip(*columns, strict=True)]


def plus_y(f, ghost=0.0):
    following = f[1:] + [ghost]
    return [
        roll_lanes(jnp.where(lanes_of(p.shape) == 0, nxt, p), -1) - p
        for p, nxt in zip(f, following, strict=True)
    ]


def minus_y(f, ghost=0.0):
    previous = [ghost] + f[:-1]
    return [
        p - roll_lanes(jnp.where(lanes_of(p.shape) == 127, prv, p), 1)
        for p, prv in zip(f, previous, strict=True)
    ]


def plus_z(f):
    return [roll_rows(p, -1) - p for p in f]


def minus_z(f):
    return [p - roll_rows(p, 1) for p in f]


def add(a, b):
    return each(lambda p, q: p + q, a, b)


def sub(a, b):
    return each(lambda p, q: p - q, a, b)


def mul(a, b):
    return each(lambda p, q: p * q, a, b)


def scale(by, a):
    return [by * p for p in a]


def halved(a):
    used = 10 if len(a) == 1 else 5
    return [jnp.where(rows_of(p.shape) < used, -0.5 * p, 0.0) for p in a]


def write_planes(grid, ref, columns):
    row = 0
    for col in columns:
        for p in col:
            ref[pl.ds(row, grid.used), :] = p[: grid.used]
            row += grid.used


def read_plane(grid, ref, row):
    start = min(row, ref.shape[0] - grid.height)
    p = ref[pl.ds(start, grid.height), :]
    if start < row:
        p = roll_rows(p, start - row)
    return jnp.where(rows_of(p.shape) < grid.used, p, 0.0)


def read_planes(grid, ref, *wanted):
    used, parts = grid.used, grid.parts
    return [[read_plane(grid, ref, used * (parts * i + part)) for part in range(parts)] for i in wanted]


def extend(e_in, h_own, m_own, zmsg, permittivity, ytile, e_ext, h_ext, c_ext, rtile, up, down):
    def body(grid, gz):
        values = [0.5 / jnp.full((CHUNK, 128), permittivity[i], F32) for i in range(MATS)]

        def coef(is_material):
            found = values[MATS - 1]
            for i in range(MATS - 2, -1, -1):
                found = jnp.where(is_material(i), values[i], found)
            return found

        clear_pads(grid, h_ext, 0)
        halo = halo_first(grid, gz)
        for layer in range(grid.count - grid.own):
            for start in range(0, grid.depth, CHUNK):
                rows = pl.ds(layer_row(grid, halo + layer) + start, CHUNK)
                from_rows = pl.ds(grid.depth * layer + start, CHUNK)
                for comp in range(3):
                    e_ext[comp, rows, :] = zmsg[comp, from_rows, :]
                material = zmsg[6, from_rows, :]
                c_ext[rows, :] = coef(lambda i, m=material: m == float(i))
        for layer in range(grid.count - grid.own):
            row = layer_row(grid, halo + layer)
            half_h(
                grid, e_ext, lambda comp, rows: zmsg[3 + comp, rows, :], grid.depth * layer, h_ext, row
            )

        def own(index):
            row = layer_row(grid, own_first(grid, gz) + index)
            from_row = pl.multiple_of(grid.depth * index, 8)
            half_h(grid, e_ext, lambda comp, rows: h_own[comp, rows, :], from_row, h_ext, row)
            for start in range(0, grid.depth, CHUNK):
                material = m_own[pl.ds(from_row + start, CHUNK), :]
                c_ext[pl.ds(row + start, CHUNK), :] = coef(lambda i, m=material: m == i)

        loop(0, grid.own, own)

        def e(comp, x):
            return column(grid, lambda rows: e_ext[comp, rows, :], x)

        def h(comp, x):
            return column(grid, lambda rows: h_ext[comp, rows, :], x)

        def c(x):
            return column(grid, lambda rows: c_ext[rows, :], x)

        last = grid.last
        if grid is Coarse:
            rtile[...] = jnp.zeros((8, 128), F32)
            write_planes(grid, down, [e(1, 0), e(2, 0)])
            write_planes(grid, up, [h(1, last), h(2, last)])
            return
        tile = jnp.zeros((8, 128), F32)
        for kind, comp in enumerate((0, 2)):
            tile = put_column(tile, 0, 8 * kind + 4, average(zmsg, comp, 0, grid.depth))
        tile = jnp.where(gz == 1, roll_lanes(tile, -4), tile)
        rtile[...] = with_halo(ytile[...], tile, gz)
        ey, ez, hx, hy, hz, c0 = e(1, 0), e(2, 0), h(0, 0), h(1, 0), h(2, 0), c(0)
        ey_next = add(ey, mul(c0, sub(minus_z(hx), hz)))
        ez_next = add(ez, mul(c0, sub(hy, minus_y(hx))))
        write_planes(grid, down, [ey, ez, ey_next, ez_next, c0])
        hx, hy, hz, c63 = h(0, last), h(1, last), h(2, last), c(last)
        hy62, hz62 = h(1, last - 1), h(2, last - 1)
        ex_next = add(e(0, last), mul(c63, sub(minus_y(hz), minus_z(hy))))
        ey_next = add(e(1, last), mul(c63, sub(minus_z(hx), sub(hz, hz62))))
        ez_next = add(e(2, last), mul(c63, sub(sub(hy, hy62), minus_y(hx))))
        write_planes(grid, up, [hy, hz, ex_next, ey_next, ez_next, c63])

    by_level(body)


def join_y(up, down, yin, yzin, rtile, to_up, to_down, ptile):
    def body(grid, gz):
        top = joined(yin[...], yzin[...], gz)
        to_up[...] = up[...]
        to_down[...] = down[...]
        shape = (grid.height, 128)
        if grid is Coarse:
            ptile[...] = top
            at = 5 * 7
            change = jnp.where(lanes_of(shape) == 127, 0.5 * column_of(top, 3, 7, 0, shape, 1), 0.0)
            to_up[pl.ds(at, 5), :] = to_up[pl.ds(at, 5), :] + change[:5]
            return
        r = rtile[...]
        lane, row = lanes_of(top.shape), rows_of(top.shape)
        kind = (lane % 32) // 8
        px = top - 0.5 * roll_lanes(r, -8) + 0.5 * (roll_lanes(top, -17) - roll_lanes(top, -16))
        beside = roll_rows(top, -1)
        beside = jnp.where(row == 7, jnp.where(lane >= 96, 0.0, roll_lanes(beside, -32)), beside)
        pz = top + 0.5 * roll_lanes(r, 8) - 0.5 * (roll_lanes(beside, -8) - roll_lanes(top, -8))
        plane = jnp.where(kind == 0, px, jnp.where(kind == 1, pz, 0.0))
        ptile[...] = plane

        def change(ref, target, index, c, value):
            change = jnp.where(lanes_of(shape) == 0, c * value, 0.0)
            rows = pl.ds(10 * index, 10)
            target[rows, :] = ref[rows, :] + change[:10]

        ((c0,),) = read_planes(grid, down, 4)
        ((c63,),) = read_planes(grid, up, 5)
        change(down, to_down, 3, c0, column_of(plane, 0, 0, 0, shape, 2))
        change(up, to_up, 4, c63, column_of(plane, 3, 7, 0, shape, 2))
        change(up, to_up, 2, c63, -column_of(plane, 3, 7, 8, shape, 2))
        to_down[pl.ds(50, 10), :] = column_of(top, 0, 0, 16, shape, 2)[:10]

    by_level(body)


def advance(
    e_ext, h_ext, c_ext, ptile, e_out, h_out, e_edge, h_edge, e_mid, h_mid, e_last, plane, sems
):
    def body(grid, gz):
        first = own_first(grid, gz)
        tile = ptile[...]

        def write(source, target, sem, layer=None):
            source, target = own_layers(grid, source, gz), block_layers(grid, target)
            if layer is not None:
                source, target = source.at[:, layer], target.at[:, layer]
            return pltpu.make_async_copy(source, target, sem)

        def keep_edges(source, target):
            for comp in range(3):
                for layer in range(grid.own):
                    for edge in range(2):
                        row = layer_row(grid, first + layer) + (grid.depth - 8) * edge
                        target[edge, comp, pl.ds(8 * layer, 8), :] = source[comp, pl.ds(row, 8), :]

        clear_pads(grid, h_mid, 0)
        if grid is Fine:
            clear_pads(grid, e_mid, grid.count + 1)
            for kind in range(2):
                for layer in range(5):
                    for block in range(4):
                        value = roll_lanes(tile, 127 - (32 * block + 8 * kind + layer))
                        for step in range(2):
                            rows = pl.ds(64 * layer + 16 * block + step, 8, stride=2)
                            plane[kind, rows, :] = value

            def ghosts(index):
                begin = 64 * (index // 2)

                def of(start):
                    rows = pl.ds(pl.multiple_of(begin + start, 8), CHUNK)
                    return plane[0, rows, :], plane[1, rows, :]

                return of

            loop(
                0,
                grid.count,
                lambda i: half_e(grid, h_ext, e_ext, e_mid, c_ext, layer_row(grid, i), ghosts(i)),
            )
            loop(
                0,
                grid.count,
                lambda i: half_h(
                    grid,
                    e_mid,
                    lambda comp, rows: h_ext[comp, rows, :],
                    layer_row(grid, i),
                    h_mid,
                    layer_row(grid, i),
                ),
            )
            h_write = write(h_mid, h_out, sems.at[0])
            h_write.start()
            e_begin = e_mid
        else:
            for comp in range(3):
                for layer in range(grid.count):
                    rows = pl.ds(layer_row(grid, layer), grid.depth)
                    h_mid[comp, rows, :] = h_ext[comp, rows, :]
            lane = lanes_of((8, 128))
            for layer in range(grid.count):
                for block in range(4):
                    rows = pl.ds(layer_row(grid, layer) + 32 * block + 3, 8, stride=4)
                    rx = roll_lanes(tile, 127 - (32 * block + layer))
                    rz = roll_lanes(tile, 127 - (32 * block + 8 + layer))
                    h_mid[0, rows, :] = h_mid[0, rows, :] - jnp.where(lane == 127, 0.5 * rz, 0.0)
                    h_mid[2, rows, :] = h_mid[2, rows, :] + jnp.where(lane == 127, 0.5 * rx, 0.0)
            h_write = write(h_mid, h_out, sems.at[0])
            h_write.start()
            e_begin = e_ext

            def ghosts(index):
                return lambda start: (0.0, 0.0)

        def last(index):
            layer = first + index
            half_e(grid, h_mid, e_begin, e_last, c_ext, layer_row(grid, layer), ghosts(layer))
            write(e_last, e_out, sems.at[1], index).start()

        loop(0, grid.own, last)
        keep_edges(h_mid, h_edge)
        keep_edges(e_last, e_edge)
        h_write.wait()
        write(e_last, e_out, sems.at[1]).wait()

    by_level(body)


def correct(
    up_own, down_own, from_below, from_above, c_ext, e_edge, h_edge, e_in, h_in, e_out, h_out, e_tile, h_tile, sems
):
    def body(grid, gz):
        last = grid.last

        def put(ref, edge, comp, x, change):
            for part, p in enumerate(change):
                moved = pltpu.roll(p, grid.height - own_first(grid, gz), 0)[: grid.own]
                rows = pl.ds(grid.step * x % 8 + part, grid.own, stride=8)
                ref[edge, comp, rows, :] = ref[edge, comp, rows, :] + moved

        def c(x):
            return column(grid, lambda rows: c_ext[rows, :], x)

        def finish(edge):
            copies = []
            for slot, (tile, out) in enumerate(((h_tile, h_out), (e_tile, e_out))):
                source = tile.at[edge].reshape(3, 8, 8, 128).at[:, pl.ds(0, grid.own)]
                target = block_layers(grid, out).at[:, :, pl.ds((grid.depth - 8) * edge, 8), :]
                copies.append(pltpu.make_async_copy(source, target, sems.at[2 * edge + slot]))
            for copy in copies:
                copy.start()
            return copies

        for edge in range(2):
            for comp in range(3):
                rows = pl.ds(0, 8 * grid.own)
                e_tile[edge, comp, rows, :] = e_edge[edge, comp, rows, :]
                h_tile[edge, comp, rows, :] = h_edge[edge, comp, rows, :]

        if grid is Fine:
            zero = [jnp.zeros((16, 128), F32)]
            ey64, ez64, ey64_part, ez64_part, c64, ey_top = read_planes(grid, from_above, *range(6))
            hy63, hz63 = read_planes(grid, up_own, 0, 1)
            c62, c63 = c(62), c(63)
            ghost = -0.5 * ey_top[0]
            dhy, dhz = scale(0.5, ez64), scale(-0.5, ey64)
            dex = mul(c63, sub(minus_y(dhz, ghost), minus_z(dhy)))
            dey = scale(-1.0, mul(c63, dhz))
            dez = mul(c63, dhy)
            dex62 = mul(c62, minus_y(zero, ghost))
            ey64_next = add(ey64_part, mul(c64, add(hz63, dhz)))
            ez64_next = sub(ez64_part, mul(c64, add(hy63, dhy)))
            dhx2 = halved(sub(plus_y(dez), plus_z(dey)))
            dhy2 = add(dhy, halved(sub(plus_z(dex), sub(ez64_next, dez))))
            dhz2 = add(dhz, halved(sub(sub(ey64_next, dey), plus_y(dex))))
            dhy62 = halved(sub(plus_z(dex62), dez))
            dhz62 = halved(sub(dey, plus_y(dex62)))
            put(h_tile, 1, 0, 63, dhx2)
            put(h_tile, 1, 1, 63, dhy2)
            put(h_tile, 1, 2, 63, dhz2)
            put(h_tile, 1, 1, 62, dhy62)
            put(h_tile, 1, 2, 62, dhz62)
            put(e_tile, 1, 0, 63, add(dex, mul(c63, sub(minus_y(dhz2, ghost), minus_z(dhy2)))))
            put(e_tile, 1, 1, 63, add(dey, mul(c63, sub(minus_z(dhx2), sub(dhz2, dhz62)))))
            put(e_tile, 1, 2, 63, add(dez, mul(c63, sub(sub(dhy2, dhy62), minus_y(dhx2)))))
            put(e_tile, 1, 0, 62, add(dex62, mul(c62, sub(minus_y(dhz62, ghost), minus_z(dhy62)))))
            put(e_tile, 1, 1, 62, scale(-1.0, mul(c62, dhz62)))
            put(e_tile, 1, 2, 62, mul(c62, dhy62))
            copies = finish(1)

            hy_part, hz_part, ex_part, ey_part, ez_part, cm = read_planes(grid, from_below, *range(6))
            ey0, ez0, ey0_part, ez0_part, c0, ey_top = read_planes(grid, down_own, *range(6))
            c1 = c(1)
            ghost = -0.5 * ey_top[0]
            dhy, dhz = scale(0.5, ez0), scale(-0.5, ey0)
            hym, hzm = add(hy_part, dhy), add(hz_part, dhz)
            exm = add(ex_part, mul(cm, sub(minus_y(dhz, ghost), minus_z(dhy))))
            eym = sub(ey_part, mul(cm, dhz))
            ezm = add(ez_part, mul(cm, dhy))
            dey, dez = mul(c0, hzm), scale(-1.0, mul(c0, hym))
            dhx2 = halved(sub(plus_y(dez), plus_z(dey)))
            dhy2 = scale(-0.5, dez)
            dhz2 = scale(0.5, dey)
            hym2 = add(hym, halved(sub(plus_z(exm), sub(add(ez0_part, dez), ezm))))
            hzm2 = add(hzm, halved(sub(sub(add(ey0_part, dey), eym), plus_y(exm))))
            put(h_tile, 0, 0, 0, dhx2)
            put(h_tile, 0, 1, 0, dhy2)
            put(h_tile, 0, 2, 0, dhz2)
            put(e_tile, 0, 0, 0, mul(c0, sub(minus_y(dhz2), minus_z(dhy2))))
            put(e_tile, 0, 1, 0, add(dey, mul(c0, sub(minus_z(dhx2), sub(dhz2, hzm2)))))
            put(e_tile, 0, 2, 0, add(dez, mul(c0, sub(sub(dhy2, hym2), minus_y(dhx2)))))
            put(e_tile, 0, 1, 1, mul(c1, dhz2))
            put(e_tile, 0, 2, 1, scale(-1.0, mul(c1, dhy2)))
            copies += finish(0)
        else:
            ey32, ez32 = read_planes(grid, from_above, 0, 1)
            c31 = c(last)
            dhy, dhz = scale(0.5, ez32), scale(-0.5, ey32)
            put(h_tile, 1, 1, last, dhy)
            put(h_tile, 1, 2, last, dhz)
            put(e_tile, 1, 0, last, mul(c31, sub(minus_y(dhz), minus_z(dhy))))
            put(e_tile, 1, 1, last, scale(-1.0, mul(c31, dhz)))
            put(e_tile, 1, 2, last, mul(c31, dhy))
            copies = finish(1)
            hy_part, hz_part = read_planes(grid, from_below, 0, 1)
            ey0, ez0 = read_planes(grid, down_own, 0, 1)
            c0 = c(0)
            put(e_tile, 0, 1, 0, mul(c0, add(hz_part, scale(-0.5, ey0))))
            put(e_tile, 0, 2, 0, scale(-1.0, mul(c0, add(hy_part, scale(0.5, ez0)))))
            copies += finish(0)
        for copy in copies:
            copy.wait()

    by_level(body)


def across(x, dx=0, dy=0, dz=0):
    nx, ny, nz = lax.axis_size("gx"), lax.axis_size("gy"), lax.axis_size("gz")
    pairs = [
        ((i * ny + j) * nz + k, ((i + dx) % nx * ny + (j + dy) % ny) * nz + (k + dz) % nz)
        for i in range(nx)
        for j in range(ny)
        for k in range(nz)
    ]
    return lax.ppermute(x, ("gx", "gy", "gz"), pairs)


def fast_shards(electric, magnetic, material, permittivity):
    e = electric.reshape(3, ROWS, 128)
    h = magnetic.reshape(3, ROWS, 128)
    m = material.reshape(ROWS, 128)
    dma = pltpu.SemaphoreType.DMA
    e_ext, zmsg, ytile = kernel_call(
        gather,
        [vmem(3, EXT, 128), vmem(7, HALO, 128), vmem(8, 128)],
        [HBM] * 3,
        [VM] * 3,
        [pltpu.VMEM((3, ROWS, 128), F32), pltpu.VMEM((HALO, 128), jnp.int32), dma((8,))],
    )(far(e), far(h), far(m))
    zin = across(zmsg, dz=1)
    yzin = across(ytile, dy=1, dz=1)
    yin = across(ytile, dy=1)
    e_ext, h_ext, c_ext, rtile, up, down = kernel_call(
        extend,
        [
            vmem(3, EXT, 128),
            vmem(3, EXT, 128),
            vmem(EXT, 128),
            vmem(8, 128),
            vmem(64, 128),
            vmem(64, 128),
        ],
        [VM] * 4 + [pl.BlockSpec(memory_space=pltpu.SMEM), VM],
        [VM] * 6,
        aliases={0: 0},
    )(held(e_ext), held(h), held(m), held(zin), permittivity, held(ytile))
    to_up, to_down, ptile = kernel_call(
        join_y,
        [vmem(64, 128), vmem(64, 128), vmem(8, 128)],
        [VM] * 5,
        [VM] * 3,
    )(*(held(part) for part in (up, down, yin, yzin, rtile)))
    from_below = across(to_up, dx=1)
    from_above = across(to_down, dx=-1)
    whole = jax.ShapeDtypeStruct((3, ROWS, 128), F32)
    e_out, h_out, e_edge, h_edge = kernel_call(
        advance,
        [whole, whole, vmem(2, 3, 64, 128), vmem(2, 3, 64, 128)],
        [VM] * 4,
        [HBM, HBM, VM, VM],
        [pltpu.VMEM((3, EXT, 128), F32)] * 3 + [pltpu.VMEM((2, 320, 128), F32), dma((2,))],
    )(*(held(part) for part in (e_ext, h_ext, c_ext, ptile)))
    e_out, h_out = kernel_call(
        correct,
        [whole, whole],
        [VM] * 7 + [HBM] * 2,
        [HBM] * 2,
        [pltpu.VMEM((2, 3, 64, 128), F32)] * 2 + [dma((4,))],
        aliases={7: 0, 8: 1},
    )(
        *(held(part) for part in (to_up, to_down, from_below, from_above, c_ext, e_edge, h_edge)),
        e_out,
        h_out,
    )
    return e_out.reshape(electric.shape), h_out.reshape(magnetic.shape)


def solution(mesh):
    placed = (
        P(("parts", "gy"), "gx", "gz", None, None),
        P(("parts", "gy"), "gx", "gz", None, None),
        P(("parts", "gy"), "gx", "gz", None),
        P(),
    )
    fast = mesh.shape["gy"] == 2 and mesh.shape["gz"] == 2
    return jax.shard_map(
        fast_shards if fast else general_shards,
        mesh=mesh,
        in_specs=placed,
        out_specs=(
            P(("parts", "gy"), "gx", "gz", None, None),
            P(("parts", "gy"), "gx", "gz", None, None),
        ),
        check_vma=False,
    )
```

profile of v0, /device:TPU:0, one launch (start us, length us, event | category | flops | bytes accessed | tf_op | source)
XLA Modules:
  0.0 14.9 jit_solution(12017058724271282404)
XLA Ops:
  0.6 0.0 copy-start
  0.6 0.0 copy-start.1
  0.6 1.6 %shard_map.59 = (f32[3,1296,128]{2,1,0:T(8,128)S(1)}, f32[7,128,128]{2,1,0:T(8,128)S(1)}, f32[8,128]{1,0:T(8,128)S(1)}) custom-call(f32[3,512,128]{2,1,0:T(8,128)} %bitcast.9, f32[3,512,128]{2,1,0:T(8,128)} %bitcast.5, s32[512,128]{1,0:T(8,128)} %bitcast.7), custom_call_target="tpu_custom_call" | custom-call | tf_op jit(solution)/shard_map/pallas_call | solution.py:858
  2.3 0.5 %collective-permute-start = (f32[7,128,128]{2,1,0:T(8,128)S(1)}, f32[7,128,128]{2,1,0:T(8,128)S(1)}, u32[]{:S(2)}, u32[]{:S(2)}) collective-permute-start(f32[7,128,128]{2,1,0:T(8,128)S(1)} %get-tuple-element.21), channel_id=1, source_target_pairs={{0,1},{1,0},{2,3},{3,2},{4,5},{5,4},{6,7},{7,6},{8,9},{9,8},{10,11... | collective-permute-start | bytes 1376264 | tf_op jit(solution)/shard_map/ppermute | solution.py:850
  2.8 2.3 %collective-permute-start.1 = (f32[8,128]{1,0:T(8,128)S(1)}, f32[8,128]{1,0:T(8,128)S(1)}, u32[]{:S(2)}, u32[]{:S(2)}) collective-permute-start(f32[8,128]{1,0:T(8,128)S(1)} %get-tuple-element.22.ytile), channel_id=1, source_target_pairs={{0,2},{1,3},{2,0},{3,1},{4,6},{5,7},{6,4},{7,5},{8,10},{9,11},{10,... | collective-permute-start | bytes 12296 | tf_op jit(solution)/shard_map/ppermute | solution.py:850
  5.1 0.1 collective-permute-start.2
  5.2 0.0 collective-permute-done.zmsg
  5.2 0.0 copy-done
  5.2 0.0 copy-done.1
  5.2 0.0 copy-start.2
  5.2 0.6 %copy-done.2 = f32[4]{0:T(128)S(1)} copy-done((f32[4]{0:T(128)S(1)}, f32[4]{0:T(128)}, u32[]{:S(2)}) %copy-start.2) | copy-done | bytes 40
  5.9 1.2 %shard_map.60 = (f32[3,1296,128]{2,1,0:T(8,128)S(1)}, f32[3,1296,128]{2,1,0:T(8,128)S(1)}, f32[1296,128]{1,0:T(8,128)S(1)}, f32[8,128]{1,0:T(8,128)S(1)}, f32[64,128]{1,0:T(8,128)S(1)}, /*index=5*/f32[64,128]{1,0:T(8,128)S(1)}) custom-call(f32[3,1296,128]{2,1,0:T(8,128)S(1)} %get-tuple-element.20.e_in, ...), custom_call_target="tpu_custom_call", output_to_operand_aliasing={{0}: (0, {})} | custom-call | tf_op jit(solution)/shard_map/pallas_call | solution.py:868
  7.1 0.0 collective-permute-done.1.yin
  7.1 1.1 %collective-permute-done.2.yzin = f32[8,128]{1,0:T(8,128)S(1)} collective-permute-done((f32[8,128]{1,0:T(8,128)S(1)}, f32[8,128]{1,0:T(8,128)S(1)}, u32[]{:S(2)}, u32[]{:S(2)}) %collective-permute-start.2) | collective-permute-done | bytes 4128 | tf_op jit(solution)/shard_map/ppermute | solution.py:850
  8.2 0.1 %shard_map.61 = (f32[64,128]{1,0:T(8,128)S(1)}, f32[64,128]{1,0:T(8,128)S(1)}, f32[8,128]{1,0:T(8,128)S(1)}) custom-call(f32[64,128]{1,0:T(8,128)S(1)} %get-tuple-element.23.up, f32[64,128]{1,0:T(8,128)S(1)} %get-tuple-element.24.down, f32[8,128]{1,0:T(8,128)S(1)} %collective-permute-done.1.yin, f32[8,128]{1,0:T(8,128)S(1)} %collective-permute-done.2.yzin, ...), custom_call_target="tpu_custom_call" | custom-call | tf_op jit(solution)/shard_map/pallas_call | solution.py:882
  8.3 1.6 %collective-permute-start.3 = (f32[64,128]{1,0:T(8,128)S(1)}, f32[64,128]{1,0:T(8,128)S(1)}, u32[]{:S(2)}, u32[]{:S(2)}) collective-permute-start(f32[64,128]{1,0:T(8,128)S(1)} %get-tuple-element.26.up_own), channel_id=1, source_target_pairs={{0,4},{1,5},{2,6},{3,7},{4,8},{5,9},{6,10},{7,11},{8,12},{9,13},{1... | collective-permute-start | bytes 98312 | tf_op jit(solution)/shard_map/ppermute | solution.py:850
  9.9 2.2 %collective-permute-start.4 = (f32[64,128]{1,0:T(8,128)S(1)}, f32[64,128]{1,0:T(8,128)S(1)}, u32[]{:S(2)}, u32[]{:S(2)}) collective-permute-start(f32[64,128]{1,0:T(8,128)S(1)} %get-tuple-element.27.down_own), channel_id=1, source_target_pairs={{0,12},{1,13},{2,14},{3,15},{4,0},{5,1},{6,2},{7,3},{8,4},{9,5},{1... | collective-permute-start | bytes 98312 | tf_op jit(solution)/shard_map/ppermute | solution.py:850
  12.1 1.3 %shard_map.62 = (f32[3,512,128]{2,1,0:T(8,128)}, f32[3,512,128]{2,1,0:T(8,128)}, f32[2,3,64,128]{3,2,1,0:T(8,128)S(1)}, f32[2,3,64,128]{3,2,1,0:T(8,128)S(1)}) custom-call(f32[3,1296,128]{2,1,0:T(8,128)S(1)} %get-tuple-element.29.e_ext, f32[3,1296,128]{2,1,0:T(8,128)S(1)} %get-tuple-element.30.h_ext, f32[1296,128]{1,0:T(8,128)S(1)} %get-tuple-element.28.c_ext, ...), custom_call_target="tpu_custom_call" | custom-call | tf_op jit(solution)/shard_map/pallas_call | solution.py:891
  13.4 0.7 %collective-permute-done.3.from_below = f32[64,128]{1,0:T(8,128)S(1)} collective-permute-done((f32[64,128]{1,0:T(8,128)S(1)}, f32[64,128]{1,0:T(8,128)S(1)}, u32[]{:S(2)}, u32[]{:S(2)}) %collective-permute-start.3) | collective-permute-done | bytes 32800 | tf_op jit(solution)/shard_map/ppermute | solution.py:850
  14.1 0.0 collective-permute-done.4.from_above
  14.2 0.8 %shard_map.63 = (f32[3,512,128]{2,1,0:T(8,128)}, f32[3,512,128]{2,1,0:T(8,128)}) custom-call(f32[64,128]{1,0:T(8,128)S(1)} %get-tuple-element.26.up_own, f32[64,128]{1,0:T(8,128)S(1)} %get-tuple-element.27.down_own, f32[64,128]{1,0:T(8,128)S(1)} %collective-permute-done.3.from_below, ...), custom_call_target="tpu_custom_call", output_to_operand_aliasing={{0}: (7, {}), {1}: (8, {})} | custom-call | tf_op jit(solution)/shard_map/pallas_call | solution.py:898
Async XLA Ops:
  0.6 4.6 %copy-start = (f32[1,1,1,3,65536]{4,2,3,1,0:T(1,128)S(1)}, f32[1,1,1,3,65536]{4,2,3,1,0:T(1,128)}, u32[]{:S(2)}) copy-start(f32[1,1,1,3,65536]{4,2,3,1,0:T(1,128)} %param.5) | copy-start | bytes 2359300
  0.6 4.6 %copy-start.1 = (s32[1,1,1,65536]{3,2,1,0:T(1,128)S(1)}, s32[1,1,1,65536]{3,2,1,0:T(1,128)}, u32[]{:S(2)}) copy-start(s32[1,1,1,65536]{3,2,1,0:T(1,128)} %param.6) | copy-start | bytes 786436
  2.3 2.9 %collective-permute-start = (f32[7,128,128]{2,1,0:T(8,128)S(1)}, f32[7,128,128]{2,1,0:T(8,128)S(1)}, u32[]{:S(2)}, u32[]{:S(2)}) collective-permute-start(f32[7,128,128]{2,1,0:T(8,128)S(1)} %get-tuple-element.21), channel_id=1, source_target_pairs={{0,1},{1,0},{2,3},{3,2},{4,5},{5,4},{6,7},{7,6},{8,9},{9,8},{10,11... | collective-permute-start | bytes 1376264 | tf_op jit(solution)/shard_map/ppermute | solution.py:850
  2.8 4.2 %collective-permute-start.1 = (f32[8,128]{1,0:T(8,128)S(1)}, f32[8,128]{1,0:T(8,128)S(1)}, u32[]{:S(2)}, u32[]{:S(2)}) collective-permute-start(f32[8,128]{1,0:T(8,128)S(1)} %get-tuple-element.22.ytile), channel_id=1, source_target_pairs={{0,2},{1,3},{2,0},{3,1},{4,6},{5,7},{6,4},{7,5},{8,10},{9,11},{10,... | collective-permute-start | bytes 12296 | tf_op jit(solution)/shard_map/ppermute | solution.py:850
  5.1 3.0 %collective-permute-start.2 = (f32[8,128]{1,0:T(8,128)S(1)}, f32[8,128]{1,0:T(8,128)S(1)}, u32[]{:S(2)}, u32[]{:S(2)}) collective-permute-start(f32[8,128]{1,0:T(8,128)S(1)} %get-tuple-element.22.ytile), channel_id=1, source_target_pairs={{0,3},{1,2},{2,1},{3,0},{4,7},{5,6},{6,5},{7,4},{8,11},{9,10},{10,... | collective-permute-start | bytes 12296 | tf_op jit(solution)/shard_map/ppermute | solution.py:850
  5.2 0.7 %copy-start.2 = (f32[4]{0:T(128)S(1)}, f32[4]{0:T(128)}, u32[]{:S(2)}) copy-start(f32[4]{0:T(128)} %permittivity.1) | copy-start | bytes 52
  8.3 5.8 %collective-permute-start.3 = (f32[64,128]{1,0:T(8,128)S(1)}, f32[64,128]{1,0:T(8,128)S(1)}, u32[]{:S(2)}, u32[]{:S(2)}) collective-permute-start(f32[64,128]{1,0:T(8,128)S(1)} %get-tuple-element.26.up_own), channel_id=1, source_target_pairs={{0,4},{1,5},{2,6},{3,7},{4,8},{5,9},{6,10},{7,11},{8,12},{9,13},{1... | collective-permute-start | bytes 98312 | tf_op jit(solution)/shard_map/ppermute | solution.py:850
  9.9 4.3 %collective-permute-start.4 = (f32[64,128]{1,0:T(8,128)S(1)}, f32[64,128]{1,0:T(8,128)S(1)}, u32[]{:S(2)}, u32[]{:S(2)}) collective-permute-start(f32[64,128]{1,0:T(8,128)S(1)} %get-tuple-element.27.down_own), channel_id=1, source_target_pairs={{0,12},{1,13},{2,14},{3,15},{4,0},{5,1},{6,2},{7,3},{8,4},{9,5},{1... | collective-permute-start | bytes 98312 | tf_op jit(solution)/shard_map/ppermute | solution.py:850
where the time goes:
time: 15.1 us; the launch traced here: 14.9 us
  starting transfers between devices  6.72 us (45%)
  Pallas kernels  5.03 us (33%)
  waiting for transfers between devices  1.84 us (12%)
  between operations  0.69 us (5%)
  local copies, waits for them, and re-layouts  0.66 us (4%)
    ppermute x5, starting transfers between devices, across(): return lax.ppermute(x, ('gx', 'gy', 'gz'), pairs)  6.72 us
    ppermute x5, waiting for transfers between devices, across(): return lax.ppermute(x, ('gx', 'gy', 'gz'), pairs)  1.84 us
    pallas_call x1, Pallas kernels, fast_shards(): kernel_call(gather, [vmem(3, EXT, 128), vmem(7, HALO, 128), vmem(8, 128)]...  1.64 us
    pallas_call x1, Pallas kernels, fast_shards(): kernel_call(advance, [whole, whole, vmem(2, 3, 64, 128), vmem(2, 3, 64, 1...  1.27 us
    pallas_call x1, Pallas kernels, fast_shards(): kernel_call(extend, [vmem(3, EXT, 128), vmem(3, EXT, 128), vmem(EXT, 128)...  1.18 us
    pallas_call x1, Pallas kernels, fast_shards(): kernel_call(correct, [whole, whole], [VM] * 7 + [HBM] * 2, [HBM] * 2, [pl...  0.78 us
    unnamed x6, local copies, waits for them, and re-layouts  0.66 us
  transfers between devices with their start and end apart: 5, of which 2 were waited for; matrix products, arithmetic and copies ran while one was open for 0% of the time, Pallas kernels for 16%

commit v1 on v0

--- a/solution.py
+++ b/solution.py
@@ -430,14 +430,6 @@
         e_to[2, here, :] = e_from[2, here, :] + c * ((hy - h[1, beside, :]) - (hx - hx_y))
 
 
-def loop(first, count, body):
-    def step(index, carry):
-        body(index)
-        return carry
-
-    lax.fori_loop(first, first + count, step, 0)
-
-
 def with_halo(tile, halo_tile, gz):
     lane = lanes_of(tile.shape)
     return jnp.where(lane % 8 == 4 * (1 - gz), halo_tile, tile)
@@ -530,16 +522,12 @@
     return [[read_plane(grid, ref, used * (parts * i + part)) for part in range(parts)] for i in wanted]
 
 
-def extend(e_in, h_own, m_own, zmsg, permittivity, ytile, e_ext, h_ext, c_ext, rtile, up, down):
+def extend(
+    e_in, h_own, m_own, zmsg, permittivity, ytile, e_ext, h_ext, c_ext, rtile, up, down, table, sems
+):
     def body(grid, gz):
-        values = [0.5 / jnp.full((CHUNK, 128), permittivity[i], F32) for i in range(MATS)]
-
-        def coef(is_material):
-            found = values[MATS - 1]
-            for i in range(MATS - 2, -1, -1):
-                found = jnp.where(is_material(i), values[i], found)
-            return found
-
+        load = pltpu.make_async_copy(permittivity, table, sems.at[0])
+        load.start()
         clear_pads(grid, h_ext, 0)
         halo = halo_first(grid, gz)
         for layer in range(grid.count - grid.own):
@@ -548,23 +536,34 @@
                 from_rows = pl.ds(grid.depth * layer + start, CHUNK)
                 for comp in range(3):
                     e_ext[comp, rows, :] = zmsg[comp, from_rows, :]
-                material = zmsg[6, from_rows, :]
-                c_ext[rows, :] = coef(lambda i, m=material: m == float(i))
         for layer in range(grid.count - grid.own):
             row = layer_row(grid, halo + layer)
             half_h(
                 grid, e_ext, lambda comp, rows: zmsg[3 + comp, rows, :], grid.depth * layer, h_ext, row
             )
 
-        def own(index):
-            row = layer_row(grid, own_first(grid, gz) + index)
-            from_row = pl.multiple_of(grid.depth * index, 8)
-            half_h(grid, e_ext, lambda comp, rows: h_own[comp, rows, :], from_row, h_ext, row)
-            for start in range(0, grid.depth, CHUNK):
-                material = m_own[pl.ds(from_row + start, CHUNK), :]
-                c_ext[pl.ds(row + start, CHUNK), :] = coef(lambda i, m=material: m == i)
-
-        loop(0, grid.own, own)
+        for layer in range(grid.own):
+            row = layer_row(grid, own_first(grid, gz) + layer)
+            half_h(grid, e_ext, lambda comp, rows: h_own[comp, rows, :], grid.depth * layer, h_ext, row)
+        load.wait()
+        values = [0.5 / jnp.full((CHUNK, 128), table[i], F32) for i in range(MATS)]
+
+        def coef(is_material):
+            found = values[MATS - 1]
+            for i in range(MATS - 2, -1, -1):
+                found = jnp.where(is_material(i), values[i], found)
+            return found
+
+        for start in range(0, HALO, CHUNK):
+            layer, rest = divmod(start, grid.depth)
+            material = zmsg[6, pl.ds(start, CHUNK), :]
+            row = layer_row(grid, halo + layer) + rest
+            c_ext[pl.ds(row, CHUNK), :] = coef(lambda i, m=material: m == float(i))
+        for start in range(0, ROWS, CHUNK):
+            layer, rest = divmod(start, grid.depth)
+            material = m_own[pl.ds(start, CHUNK), :]
+            row = layer_row(grid, own_first(grid, gz) + layer) + rest
+            c_ext[pl.ds(row, CHUNK), :] = coef(lambda i, m=material: m == i)
 
         def e(comp, x):
             return column(grid, lambda rows: e_ext[comp, rows, :], x)
@@ -677,23 +676,12 @@
 
                 return of
 
-            loop(
-                0,
-                grid.count,
-                lambda i: half_e(grid, h_ext, e_ext, e_mid, c_ext, layer_row(grid, i), ghosts(i)),
-            )
-            loop(
-                0,
-                grid.count,
-                lambda i: half_h(
-                    grid,
-                    e_mid,
-                    lambda comp, rows: h_ext[comp, rows, :],
-                    layer_row(grid, i),
-                    h_mid,
-                    layer_row(grid, i),
-                ),
-            )
+            for layer in range(grid.count):
+                row = grid.stride * (layer + 1)
+                half_e(grid, h_ext, e_ext, e_mid, c_ext, row, ghosts(layer))
+            for layer in range(grid.count):
+                row = grid.stride * (layer + 1)
+                half_h(grid, e_mid, lambda comp, rows: h_ext[comp, rows, :], row, h_mid, row)
             h_write = write(h_mid, h_out, sems.at[0])
             h_write.start()
             e_begin = e_mid
@@ -717,12 +705,10 @@
             def ghosts(index):
                 return lambda start: (0.0, 0.0)
 
-        def last(index):
-            layer = first + index
-            half_e(grid, h_mid, e_begin, e_last, c_ext, layer_row(grid, layer), ghosts(layer))
-            write(e_last, e_out, sems.at[1], index).start()
-
-        loop(0, grid.own, last)
+        for layer in range(grid.own):
+            row = layer_row(grid, first + layer)
+            half_e(grid, h_mid, e_begin, e_last, c_ext, row, ghosts(first + layer))
+            write(e_last, e_out, sems.at[1], layer).start()
         keep_edges(h_mid, h_edge)
         keep_edges(e_last, e_edge)
         h_write.wait()
@@ -755,12 +741,6 @@
             for copy in copies:
                 copy.start()
             return copies
-
-        for edge in range(2):
-            for comp in range(3):
-                rows = pl.ds(0, 8 * grid.own)
-                e_tile[edge, comp, rows, :] = e_edge[edge, comp, rows, :]
-                h_tile[edge, comp, rows, :] = h_edge[edge, comp, rows, :]
 
         if grid is Fine:
             zero = [jnp.zeros((16, 128), F32)]
@@ -862,6 +842,7 @@
         [VM] * 3,
         [pltpu.VMEM((3, ROWS, 128), F32), pltpu.VMEM((HALO, 128), jnp.int32), dma((8,))],
     )(far(e), far(h), far(m))
+    h, m, ytile = lax.optimization_barrier((h, m, ytile))
     zin = across(zmsg, dz=1)
     yzin = across(ytile, dy=1, dz=1)
     yin = across(ytile, dy=1)
@@ -875,10 +856,11 @@
             vmem(64, 128),
             vmem(64, 128),
         ],
-        [VM] * 4 + [pl.BlockSpec(memory_space=pltpu.SMEM), VM],
+        [VM] * 4 + [HBM, VM],
         [VM] * 6,
+        [pltpu.SMEM((MATS,), F32), dma((1,))],
         aliases={0: 0},
-    )(held(e_ext), held(h), held(m), held(zin), permittivity, held(ytile))
+    )(held(e_ext), held(h), held(m), held(zin), far(permittivity), held(ytile))
     to_up, to_down, ptile = kernel_call(
         join_y,
         [vmem(64, 128), vmem(64, 128), vmem(8, 128)],
@@ -895,13 +877,13 @@
         [HBM, HBM, VM, VM],
         [pltpu.VMEM((3, EXT, 128), F32)] * 3 + [pltpu.VMEM((2, 320, 128), F32), dma((2,))],
     )(*(held(part) for part in (e_ext, h_ext, c_ext, ptile)))
-    e_out, h_out = kernel_call(
+    e_out, h_out, _, _ = kernel_call(
         correct,
-        [whole, whole],
+        [whole, whole, vmem(2, 3, 64, 128), vmem(2, 3, 64, 128)],
         [VM] * 7 + [HBM] * 2,
-        [HBM] * 2,
-        [pltpu.VMEM((2, 3, 64, 128), F32)] * 2 + [dma((4,))],
-        aliases={7: 0, 8: 1},
+        [HBM] * 2 + [VM] * 2,
+        [dma((4,))],
+        aliases={7: 0, 8: 1, 5: 2, 6: 3},
     )(
         *(held(part) for part in (to_up, to_down, from_below, from_above, c_ext, e_edge, h_edge)),
         e_out,

time: 15.1 us -> 15.1 us (level)
  waiting for transfers between devices: 1.84 us -> 2.9 us
  local copies, waits for them, and re-layouts: 0.66 us -> 0.01 us
  Pallas kernels: 5.03 us -> 4.63 us
    ppermute x5, waiting for transfers between devices: 1.84 us -> 2.9 us  [across(): return lax.ppermute(x, ('gx', 'gy', 'gz'), pairs)]
    unnamed x6 -> x4, local copies, waits for them, and re-layouts: 0.66 us -> 0.01 us
    pallas_call x1, Pallas kernels: 1.18 us -> 0.79 us  [fast_shards(): kernel_call(extend, [vmem(3, EXT, 128), vmem(3, EXT, 128), vmem(EXT, 128)...]
  transfers between devices with their start and end apart: 5 -> 5, of which waited for: 2 -> 3; matrix products, arithmetic and copies ran while one was open for 0% -> 0% of each run, Pallas kernels for 16% -> 14%
where the time goes in v1:
time: 15.1 us; the launch traced here: 14.9 us
  starting transfers between devices  6.72 us (45%)
  Pallas kernels  4.63 us (31%)
  waiting for transfers between devices  2.9 us (19%)
  between operations  0.68 us (5%)
    ppermute x5, starting transfers between devices, across(): return lax.ppermute(x, ('gx', 'gy', 'gz'), pairs)  6.72 us
    ppermute x5, waiting for transfers between devices, across(): return lax.ppermute(x, ('gx', 'gy', 'gz'), pairs)  2.9 us
    pallas_call x1, Pallas kernels, fast_shards(): kernel_call(gather, [vmem(3, EXT, 128), vmem(7, HALO, 128), vmem(8, 128)]...  1.64 us
    pallas_call x1, Pallas kernels, fast_shards(): kernel_call(advance, [whole, whole, vmem(2, 3, 64, 128), vmem(2, 3, 64, 1...  1.27 us
    pallas_call x1, Pallas kernels, fast_shards(): kernel_call(extend, [vmem(3, EXT, 128), vmem(3, EXT, 128), vmem(EXT, 128)...  0.79 us
    pallas_call x1, Pallas kernels, fast_shards(): kernel_call(correct, [whole, whole, vmem(2, 3, 64, 128), vmem(2, 3, 64, 1...  0.78 us
  transfers between devices with their start and end apart: 5, of which 3 were waited for; matrix products, arithmetic and copies ran while one was open for 0% of the time, Pallas kernels for 14%

profile of v1, /device:TPU:0, one launch (start us, length us, event | category | flops | bytes accessed | tf_op | source)
XLA Modules:
  0.0 14.9 jit_solution(12571993042409482912)
XLA Ops:
  0.6 0.0 copy-start
  0.6 0.0 copy-start.1
  0.6 1.6 %shard_map.59 = (f32[3,1296,128]{2,1,0:T(8,128)S(1)}, f32[7,128,128]{2,1,0:T(8,128)S(1)}, f32[8,128]{1,0:T(8,128)S(1)}) custom-call(f32[3,512,128]{2,1,0:T(8,128)} %bitcast.9, f32[3,512,128]{2,1,0:T(8,128)} %bitcast.5, s32[512,128]{1,0:T(8,128)} %bitcast.7), custom_call_target="tpu_custom_call" | custom-call | tf_op jit(solution)/shard_map/pallas_call | solution.py:838
  2.3 0.5 %collective-permute-start = (f32[7,128,128]{2,1,0:T(8,128)S(1)}, f32[7,128,128]{2,1,0:T(8,128)S(1)}, u32[]{:S(2)}, u32[]{:S(2)}) collective-permute-start(f32[7,128,128]{2,1,0:T(8,128)S(1)} %get-tuple-element.27), channel_id=1, source_target_pairs={{0,1},{1,0},{2,3},{3,2},{4,5},{5,4},{6,7},{7,6},{8,9},{9,8},{10,11... | collective-permute-start | bytes 1376264 | tf_op jit(solution)/shard_map/ppermute | solution.py:830
  2.8 2.3 %collective-permute-start.1 = (f32[8,128]{1,0:T(8,128)S(1)}, f32[8,128]{1,0:T(8,128)S(1)}, u32[]{:S(2)}, u32[]{:S(2)}) collective-permute-start(f32[8,128]{1,0:T(8,128)S(1)} %get-tuple-element.28.ytile), channel_id=1, source_target_pairs={{0,2},{1,3},{2,0},{3,1},{4,6},{5,7},{6,4},{7,5},{8,10},{9,11},{10,... | collective-permute-start | bytes 12296 | tf_op jit(solution)/shard_map/ppermute | solution.py:830
  5.1 0.1 collective-permute-start.2
  5.2 0.0 collective-permute-done.zmsg
  5.2 0.0 copy-done
  5.2 0.0 copy-done.1
  5.2 0.8 %shard_map.60 = (f32[3,1296,128]{2,1,0:T(8,128)S(1)}, f32[3,1296,128]{2,1,0:T(8,128)S(1)}, f32[1296,128]{1,0:T(8,128)S(1)}, f32[8,128]{1,0:T(8,128)S(1)}, f32[64,128]{1,0:T(8,128)S(1)}, /*index=5*/f32[64,128]{1,0:T(8,128)S(1)}) custom-call(f32[3,1296,128]{2,1,0:T(8,128)S(1)} %get-tuple-element.23.e_in, ...), custom_call_target="tpu_custom_call", output_to_operand_aliasing={{0}: (0, {})} | custom-call | tf_op jit(solution)/shard_map/pallas_call | solution.py:849
  6.0 0.7 %collective-permute-done.1.yin = f32[8,128]{1,0:T(8,128)S(1)} collective-permute-done((f32[8,128]{1,0:T(8,128)S(1)}, f32[8,128]{1,0:T(8,128)S(1)}, u32[]{:S(2)}, u32[]{:S(2)}) %collective-permute-start.1) | collective-permute-done | bytes 4128 | tf_op jit(solution)/shard_map/ppermute | solution.py:830
  6.7 1.4 %collective-permute-done.2.yzin = f32[8,128]{1,0:T(8,128)S(1)} collective-permute-done((f32[8,128]{1,0:T(8,128)S(1)}, f32[8,128]{1,0:T(8,128)S(1)}, u32[]{:S(2)}, u32[]{:S(2)}) %collective-permute-start.2) | collective-permute-done | bytes 4128 | tf_op jit(solution)/shard_map/ppermute | solution.py:830
  8.2 0.1 %shard_map.61 = (f32[64,128]{1,0:T(8,128)S(1)}, f32[64,128]{1,0:T(8,128)S(1)}, f32[8,128]{1,0:T(8,128)S(1)}) custom-call(f32[64,128]{1,0:T(8,128)S(1)} %get-tuple-element.29.up, f32[64,128]{1,0:T(8,128)S(1)} %get-tuple-element.30.down, f32[8,128]{1,0:T(8,128)S(1)} %collective-permute-done.1.yin, f32[8,128]{1,0:T(8,128)S(1)} %collective-permute-done.2.yzin, ...), custom_call_target="tpu_custom_call" | custom-call | tf_op jit(solution)/shard_map/pallas_call | solution.py:864
  8.3 1.6 %collective-permute-start.3 = (f32[64,128]{1,0:T(8,128)S(1)}, f32[64,128]{1,0:T(8,128)S(1)}, u32[]{:S(2)}, u32[]{:S(2)}) collective-permute-start(f32[64,128]{1,0:T(8,128)S(1)} %get-tuple-element.32.up_own), channel_id=1, source_target_pairs={{0,4},{1,5},{2,6},{3,7},{4,8},{5,9},{6,10},{7,11},{8,12},{9,13},{1... | collective-permute-start | bytes 98312 | tf_op jit(solution)/shard_map/ppermute | solution.py:830
  9.9 2.2 %collective-permute-start.4 = (f32[64,128]{1,0:T(8,128)S(1)}, f32[64,128]{1,0:T(8,128)S(1)}, u32[]{:S(2)}, u32[]{:S(2)}) collective-permute-start(f32[64,128]{1,0:T(8,128)S(1)} %get-tuple-element.33.down_own), channel_id=1, source_target_pairs={{0,12},{1,13},{2,14},{3,15},{4,0},{5,1},{6,2},{7,3},{8,4},{9,5},{1... | collective-permute-start | bytes 98312 | tf_op jit(solution)/shard_map/ppermute | solution.py:830
  12.1 1.3 %shard_map.62 = (f32[3,512,128]{2,1,0:T(8,128)}, f32[3,512,128]{2,1,0:T(8,128)}, f32[2,3,64,128]{3,2,1,0:T(8,128)S(1)}, f32[2,3,64,128]{3,2,1,0:T(8,128)S(1)}) custom-call(f32[3,1296,128]{2,1,0:T(8,128)S(1)} %get-tuple-element.35.e_ext, f32[3,1296,128]{2,1,0:T(8,128)S(1)} %get-tuple-element.36.h_ext, f32[1296,128]{1,0:T(8,128)S(1)} %get-tuple-element.34.c_ext, ...), custom_call_target="tpu_custom_call" | custom-call | tf_op jit(solution)/shard_map/pallas_call | solution.py:873
  13.4 0.7 %collective-permute-done.3.from_below = f32[64,128]{1,0:T(8,128)S(1)} collective-permute-done((f32[64,128]{1,0:T(8,128)S(1)}, f32[64,128]{1,0:T(8,128)S(1)}, u32[]{:S(2)}, u32[]{:S(2)}) %collective-permute-start.3) | collective-permute-done | bytes 32800 | tf_op jit(solution)/shard_map/ppermute | solution.py:830
  14.1 0.0 collective-permute-done.4.from_above
  14.2 0.8 %shard_map.63 = (f32[3,512,128]{2,1,0:T(8,128)}, f32[3,512,128]{2,1,0:T(8,128)}, f32[2,3,64,128]{3,2,1,0:T(8,128)S(1)}, f32[2,3,64,128]{3,2,1,0:T(8,128)S(1)}) custom-call(f32[64,128]{1,0:T(8,128)S(1)} %get-tuple-element.32.up_own, ...), custom_call_target="tpu_custom_call", output_to_operand_aliasing={{0}: (7, {}), {1}: (8, {}), {2}: (5, {}), {3}: (6, {})} | custom-call | tf_op jit(solution)/shard_map/pallas_call | solution.py:880
Async XLA Ops:
  0.6 4.6 %copy-start = (f32[1,1,1,3,65536]{4,2,3,1,0:T(1,128)S(1)}, f32[1,1,1,3,65536]{4,2,3,1,0:T(1,128)}, u32[]{:S(2)}) copy-start(f32[1,1,1,3,65536]{4,2,3,1,0:T(1,128)} %param.5) | copy-start | bytes 2359300
  0.6 4.6 %copy-start.1 = (s32[1,1,1,65536]{3,2,1,0:T(1,128)S(1)}, s32[1,1,1,65536]{3,2,1,0:T(1,128)}, u32[]{:S(2)}) copy-start(s32[1,1,1,65536]{3,2,1,0:T(1,128)} %param.6) | copy-start | bytes 786436
  2.3 2.9 %collective-permute-start = (f32[7,128,128]{2,1,0:T(8,128)S(1)}, f32[7,128,128]{2,1,0:T(8,128)S(1)}, u32[]{:S(2)}, u32[]{:S(2)}) collective-permute-start(f32[7,128,128]{2,1,0:T(8,128)S(1)} %get-tuple-element.27), channel_id=1, source_target_pairs={{0,1},{1,0},{2,3},{3,2},{4,5},{5,4},{6,7},{7,6},{8,9},{9,8},{10,11... | collective-permute-start | bytes 1376264 | tf_op jit(solution)/shard_map/ppermute | solution.py:830
  2.8 3.9 %collective-permute-start.1 = (f32[8,128]{1,0:T(8,128)S(1)}, f32[8,128]{1,0:T(8,128)S(1)}, u32[]{:S(2)}, u32[]{:S(2)}) collective-permute-start(f32[8,128]{1,0:T(8,128)S(1)} %get-tuple-element.28.ytile), channel_id=1, source_target_pairs={{0,2},{1,3},{2,0},{3,1},{4,6},{5,7},{6,4},{7,5},{8,10},{9,11},{10,... | collective-permute-start | bytes 12296 | tf_op jit(solution)/shard_map/ppermute | solution.py:830
  5.1 3.0 %collective-permute-start.2 = (f32[8,128]{1,0:T(8,128)S(1)}, f32[8,128]{1,0:T(8,128)S(1)}, u32[]{:S(2)}, u32[]{:S(2)}) collective-permute-start(f32[8,128]{1,0:T(8,128)S(1)} %get-tuple-element.28.ytile), channel_id=1, source_target_pairs={{0,3},{1,2},{2,1},{3,0},{4,7},{5,6},{6,5},{7,4},{8,11},{9,10},{10,... | collective-permute-start | bytes 12296 | tf_op jit(solution)/shard_map/ppermute | solution.py:830
  8.3 5.8 %collective-permute-start.3 = (f32[64,128]{1,0:T(8,128)S(1)}, f32[64,128]{1,0:T(8,128)S(1)}, u32[]{:S(2)}, u32[]{:S(2)}) collective-permute-start(f32[64,128]{1,0:T(8,128)S(1)} %get-tuple-element.32.up_own), channel_id=1, source_target_pairs={{0,4},{1,5},{2,6},{3,7},{4,8},{5,9},{6,10},{7,11},{8,12},{9,13},{1... | collective-permute-start | bytes 98312 | tf_op jit(solution)/shard_map/ppermute | solution.py:830
  9.9 4.3 %collective-permute-start.4 = (f32[64,128]{1,0:T(8,128)S(1)}, f32[64,128]{1,0:T(8,128)S(1)}, u32[]{:S(2)}, u32[]{:S(2)}) collective-permute-start(f32[64,128]{1,0:T(8,128)S(1)} %get-tuple-element.33.down_own), channel_id=1, source_target_pairs={{0,12},{1,13},{2,14},{3,15},{4,0},{5,1},{6,2},{7,3},{8,4},{9,5},{1... | collective-permute-start | bytes 98312 | tf_op jit(solution)/shard_map/ppermute | solution.py:830

commit v2 on v1

--- a/solution.py
+++ b/solution.py
@@ -231,11 +231,11 @@
 
 
 class Fine:
-    depth, stride, count, own, step, used, height, parts, last = 64, 72, 10, 8, 1, 10, 16, 1, 63
+    depth, stride, count, own, step, parts, last = 64, 72, 10, 8, 1, 1, 63
 
 
 class Coarse:
-    depth, stride, count, own, step, used, height, parts, last = 128, 144, 5, 4, 4, 5, 8, 4, 31
+    depth, stride, count, own, step, parts, last = 128, 144, 5, 4, 4, 4, 31
 
 
 def vmem(*shape, dtype=F32):
@@ -332,7 +332,28 @@
     return tile
 
 
-def gather(e_hbm, h_hbm, m_hbm, e_ext, zmsg, ytile, h_top, m_edge, sems):
+def edge_tiles(grid, ref):
+    view = ref.reshape(*ref.shape[:-2], grid.own, grid.depth, 128)
+    lead = (slice(None),) * (len(ref.shape) - 1)
+    return [view.at[lead + (pl.ds((grid.depth - 8) * end, 8),)] for end in range(2)]
+
+
+FINE_E = [(0, comp) for comp in range(3)] + [(1, 1), (1, 2)] + [(x, comp) for x in (62, 63) for comp in range(3)]
+FINE_H = [(0, comp) for comp in range(3)] + [(62, 1), (62, 2)] + [(63, comp) for comp in range(3)]
+FINE_M = [0, 1, 62, 63]
+COARSE_E = [(0, 1), (0, 2)] + [(31, comp) for comp in range(3)]
+COARSE_H = [(31, 1), (31, 2)]
+COARSE_M = [0, 31]
+COLUMNS = 192
+R_ROW = COLUMNS - 8
+FACE = 7 * HALO
+
+
+def wanted(grid):
+    return (FINE_E, FINE_H, FINE_M) if grid is Fine else (COARSE_E, COARSE_H, COARSE_M)
+
+
+def gather(e_hbm, h_hbm, m_hbm, e_ext, zmsg, ytile, columns, h_top, m_edge, h_ends, m_ends, sems):
     def body(grid, gz):
         edge = pl.ds((1 - gz) * (ROWS - HALO), HALO)
         source, target = block_layers(grid, e_hbm), own_layers(grid, e_ext, gz)
@@ -345,9 +366,15 @@
             pltpu.make_async_copy(h_hbm.at[comp], h_top.at[comp], sems.at[3 + comp]) for comp in (0, 2)
         ]
         loads = [
-            pltpu.make_async_copy(h_hbm.at[:, edge], zmsg.at[pl.ds(3, 3)], sems.at[6]),
+            pltpu.make_async_copy(h_hbm.at[:, edge], zmsg.at[pl.ds(0, 3 * HALO)].reshape(3, HALO, 128), sems.at[6]),
             pltpu.make_async_copy(m_hbm.at[edge], m_edge, sems.at[7]),
         ]
+        for end in range(2):
+            for slot, (array, ends) in enumerate(((h_hbm, h_ends), (m_hbm, m_ends))):
+                place = ends.at[end].reshape(*ends.shape[1:-2], 8, 8, 128)
+                place = place.at[(slice(None),) * (len(ends.shape) - 3) + (pl.ds(0, grid.own),)]
+                tiles = edge_tiles(grid, array)[end]
+                loads.append(pltpu.make_async_copy(tiles, place, sems.at[8 + 2 * end + slot]))
         for load in list(e_loads.values()) + h_loads + loads:
             load.start()
         clear_pads(grid, e_ext, grid.count + 1)
@@ -369,7 +396,9 @@
                 tile = put_column(tile, 127, layer, h_top[0, h_row, :] + 0.5 * ez)
                 tile = put_column(tile, 127, 8 + layer, h_top[2, h_row, :] - 0.5 * ex)
                 tile = put_column(tile, 127, 16 + layer, ey)
-        ytile[...] = jnp.where(gz == 1, roll_lanes(tile, 1), tile)
+        tile = jnp.where(gz == 1, roll_lanes(tile, 4), tile)
+        ytile[...] = tile
+        columns[pl.ds(R_ROW, 8), :] = tile
         if grid is Fine:
             e_loads[1].wait()
         layers = HALO // grid.depth
@@ -377,10 +406,29 @@
         for comp in range(3):
             for layer in range(layers):
                 row = layer_row(grid, from_layer + layer)
-                zmsg[comp, pl.ds(grid.depth * layer, grid.depth), :] = e_ext[comp, pl.ds(row, grid.depth), :]
+                to = HALO * (3 + comp) + grid.depth * layer
+                zmsg[pl.ds(to, grid.depth), :] = e_ext[comp, pl.ds(row, grid.depth), :]
+        want_e, want_h, want_m = wanted(grid)
+        slot = 0
+        for x, comp in want_e:
+            for part in range(grid.parts):
+                rows = pl.ds(begin + grid.step * x + part, grid.own, stride=grid.stride)
+                columns[pl.ds(slot, grid.own), :] = e_ext[comp, rows, :]
+                slot += grid.own
         for load in loads:
             load.wait()
-        zmsg[6] = m_edge[...].astype(F32)
+        for x, comp in want_h:
+            for part in range(grid.parts):
+                rows = pl.ds(grid.step * x % 8 + part, grid.own, stride=8)
+                columns[pl.ds(slot, grid.own), :] = h_ends[int(x > 1), comp, rows, :]
+                slot += grid.own
+        for x in want_m:
+            for part in range(grid.parts):
+                rows = pl.ds(grid.step * x % 8 + part, grid.own, stride=8)
+                columns[pl.ds(slot, grid.own), :] = m_ends[int(x > 1), rows, :].astype(F32)
+                slot += grid.own
+        zmsg[pl.ds(6 * HALO, HALO), :] = m_edge[...].astype(F32)
+        zmsg[pl.ds(FACE, COLUMNS), :] = columns[...]
 
     by_level(body)
 
@@ -430,26 +478,12 @@
         e_to[2, here, :] = e_from[2, here, :] + c * ((hy - h[1, beside, :]) - (hx - hx_y))
 
 
-def with_halo(tile, halo_tile, gz):
-    lane = lanes_of(tile.shape)
-    return jnp.where(lane % 8 == 4 * (1 - gz), halo_tile, tile)
-
-
-def joined(own, other, gz):
-    return with_halo(own, jnp.where(gz == 0, roll_lanes(other, 3), roll_lanes(other, -3)), gz)
-
-
-def column_of(tile, block, sub, slot, shape, per_layer):
+def column_of(tile, block, sub, slot, grid):
+    shape = (2 * grid.own, 128)
     row = jnp.broadcast_to(tile[sub : sub + 1, :], shape)
-    wanted = 32 * block + slot + rows_of(shape) // per_layer
-    picked = jnp.where((lanes_of(shape) == wanted) & (rows_of(shape) < 5 * per_layer), row, 0.0)
+    lane = 32 * block + slot + rows_of(shape) // (2 * grid.own // 8)
+    picked = jnp.where(lanes_of(shape) == lane, row, 0.0)
     return jnp.broadcast_to(jnp.sum(picked, axis=1, keepdims=True), shape)
-
-
-def column(grid, read, x):
-    begin = grid.stride + grid.step * x
-    planes = [read(pl.ds(begin + part, grid.height, stride=grid.stride)) for part in range(grid.parts)]
-    return [jnp.where(rows_of(p.shape) < grid.used, p, 0.0) for p in planes]
 
 
 def each(fn, *columns):
@@ -473,11 +507,13 @@
 
 
 def plus_z(f):
-    return [roll_rows(p, -1) - p for p in f]
+    return [
+        jnp.where(rows_of(p.shape) == p.shape[0] - 1, 0.0, roll_rows(p, -1)) - p for p in f
+    ]
 
 
 def minus_z(f):
-    return [p - roll_rows(p, 1) for p in f]
+    return [p - jnp.where(rows_of(p.shape) == 0, 0.0, roll_rows(p, 1)) for p in f]
 
 
 def add(a, b):
@@ -496,34 +532,83 @@
     return [by * p for p in a]
 
 
-def halved(a):
-    used = 10 if len(a) == 1 else 5
-    return [jnp.where(rows_of(p.shape) < used, -0.5 * p, 0.0) for p in a]
-
-
-def write_planes(grid, ref, columns):
+def read_columns(grid, own, other, gz):
+    want_e, want_h, want_m = wanted(grid)
+    found, slot = [], 0
+    for _ in range(len(want_e) + len(want_h) + len(want_m)):
+        col = []
+        for _ in range(grid.parts):
+            rows = pl.ds(slot, grid.own)
+            mine, theirs = own[rows, :], other[pl.ds(FACE + slot, grid.own), :]
+            low, high = jnp.where(gz == 0, mine, theirs), jnp.where(gz == 0, theirs, mine)
+            col.append(jnp.concatenate([low, high], axis=0))
+            slot += grid.own
+        found.append(col)
+    e_found, found = found[: len(want_e)], found[len(want_e) :]
+    h_found, m_found = found[: len(want_h)], found[len(want_h) :]
+    return (
+        dict(zip(want_e, e_found, strict=True)),
+        dict(zip(want_h, h_found, strict=True)),
+        dict(zip(want_m, m_found, strict=True)),
+    )
+
+
+def write_planes(ref, columns):
     row = 0
     for col in columns:
         for p in col:
-            ref[pl.ds(row, grid.used), :] = p[: grid.used]
-            row += grid.used
-
-
-def read_plane(grid, ref, row):
-    start = min(row, ref.shape[0] - grid.height)
-    p = ref[pl.ds(start, grid.height), :]
-    if start < row:
-        p = roll_rows(p, start - row)
-    return jnp.where(rows_of(p.shape) < grid.used, p, 0.0)
-
-
-def read_planes(grid, ref, *wanted):
-    used, parts = grid.used, grid.parts
-    return [[read_plane(grid, ref, used * (parts * i + part)) for part in range(parts)] for i in wanted]
+            ref[pl.ds(row, p.shape[0]), :] = p
+            row += p.shape[0]
+
+
+def read_planes(grid, ref, *indices):
+    height, parts = 2 * grid.own, grid.parts
+    return [
+        [ref[pl.ds(height * (parts * i + part), height), :] for part in range(parts)] for i in indices
+    ]
+
+
+def sent_rows(plane, gz):
+    return jnp.where(gz == 0, roll_rows(plane, -6), plane)[:10]
+
+
+def write_message(grid, ref, columns, gz):
+    row = 0
+    for col in columns:
+        for p in col:
+            rows = p if grid is Coarse else sent_rows(p, gz)
+            ref[pl.ds(row, rows.shape[0]), :] = rows
+            row += rows.shape[0]
+
+
+def read_message(grid, ref, count, gz):
+    if grid is Coarse:
+        return read_planes(grid, ref, *range(count))
+    planes = []
+    for i in range(count):
+        start = min(10 * i, ref.shape[0] - 16)
+        p = ref[pl.ds(start, 16), :]
+        planes.append([pltpu.roll(p, 16 + start - 10 * i + 6 * gz, 0)])
+    return planes
 
 
 def extend(
-    e_in, h_own, m_own, zmsg, permittivity, ytile, e_ext, h_ext, c_ext, rtile, up, down, table, sems
+    e_in,
+    h_own,
+    m_own,
+    zmsg,
+    permittivity,
+    columns,
+    e_ext,
+    h_ext,
+    c_ext,
+    up,
+    down,
+    to_up,
+    to_down,
+    c_planes,
+    table,
+    sems,
 ):
     def body(grid, gz):
         load = pltpu.make_async_copy(permittivity, table, sems.at[0])
@@ -533,105 +618,116 @@
         for layer in range(grid.count - grid.own):
             for start in range(0, grid.depth, CHUNK):
                 rows = pl.ds(layer_row(grid, halo + layer) + start, CHUNK)
-                from_rows = pl.ds(grid.depth * layer + start, CHUNK)
                 for comp in range(3):
-                    e_ext[comp, rows, :] = zmsg[comp, from_rows, :]
+                    from_rows = pl.ds(HALO * (3 + comp) + grid.depth * layer + start, CHUNK)
+                    e_ext[comp, rows, :] = zmsg[from_rows, :]
+
+        def h_halo(comp, rows):
+            return zmsg[pl.ds(HALO * comp + rows.start, rows.size), :]
+
         for layer in range(grid.count - grid.own):
             row = layer_row(grid, halo + layer)
-            half_h(
-                grid, e_ext, lambda comp, rows: zmsg[3 + comp, rows, :], grid.depth * layer, h_ext, row
-            )
-
+            half_h(grid, e_ext, h_halo, grid.depth * layer, h_ext, row)
         for layer in range(grid.own):
             row = layer_row(grid, own_first(grid, gz) + layer)
             half_h(grid, e_ext, lambda comp, rows: h_own[comp, rows, :], grid.depth * layer, h_ext, row)
         load.wait()
-        values = [0.5 / jnp.full((CHUNK, 128), table[i], F32) for i in range(MATS)]
-
-        def coef(is_material):
-            found = values[MATS - 1]
+        values = [0.5 / jnp.full((8, 128), table[i], F32) for i in range(MATS)]
+
+        def coef(is_material, rows):
+            parts = [jnp.concatenate([value] * (rows // 8), axis=0) for value in values]
+            found = parts[MATS - 1]
             for i in range(MATS - 2, -1, -1):
-                found = jnp.where(is_material(i), values[i], found)
+                found = jnp.where(is_material(i), parts[i], found)
             return found
 
         for start in range(0, HALO, CHUNK):
             layer, rest = divmod(start, grid.depth)
-            material = zmsg[6, pl.ds(start, CHUNK), :]
+            material = zmsg[pl.ds(6 * HALO + start, CHUNK), :]
             row = layer_row(grid, halo + layer) + rest
-            c_ext[pl.ds(row, CHUNK), :] = coef(lambda i, m=material: m == float(i))
+            c_ext[pl.ds(row, CHUNK), :] = coef(lambda i, m=material: m == float(i), CHUNK)
         for start in range(0, ROWS, CHUNK):
             layer, rest = divmod(start, grid.depth)
             material = m_own[pl.ds(start, CHUNK), :]
             row = layer_row(grid, own_first(grid, gz) + layer) + rest
-            c_ext[pl.ds(row, CHUNK), :] = coef(lambda i, m=material: m == i)
-
-        def e(comp, x):
-            return column(grid, lambda rows: e_ext[comp, rows, :], x)
-
-        def h(comp, x):
-            return column(grid, lambda rows: h_ext[comp, rows, :], x)
-
-        def c(x):
-            return column(grid, lambda rows: c_ext[rows, :], x)
-
-        last = grid.last
+            c_ext[pl.ds(row, CHUNK), :] = coef(lambda i, m=material: m == i, CHUNK)
+
+        e, h, m = read_columns(grid, columns, zmsg, gz)
+        c = {
+            x: [coef(lambda i, q=part: q == float(i), part.shape[0]) for part in col] for x, col in m.items()
+        }
+        write_planes(c_planes, list(c.values()))
         if grid is Coarse:
-            rtile[...] = jnp.zeros((8, 128), F32)
-            write_planes(grid, down, [e(1, 0), e(2, 0)])
-            write_planes(grid, up, [h(1, last), h(2, last)])
-            return
-        tile = jnp.zeros((8, 128), F32)
-        for kind, comp in enumerate((0, 2)):
-            tile = put_column(tile, 0, 8 * kind + 4, average(zmsg, comp, 0, grid.depth))
-        tile = jnp.where(gz == 1, roll_lanes(tile, -4), tile)
-        rtile[...] = with_halo(ytile[...], tile, gz)
-        ey, ez, hx, hy, hz, c0 = e(1, 0), e(2, 0), h(0, 0), h(1, 0), h(2, 0), c(0)
-        ey_next = add(ey, mul(c0, sub(minus_z(hx), hz)))
-        ez_next = add(ez, mul(c0, sub(hy, minus_y(hx))))
-        write_planes(grid, down, [ey, ez, ey_next, ez_next, c0])
-        hx, hy, hz, c63 = h(0, last), h(1, last), h(2, last), c(last)
-        hy62, hz62 = h(1, last - 1), h(2, last - 1)
-        ex_next = add(e(0, last), mul(c63, sub(minus_y(hz), minus_z(hy))))
-        ey_next = add(e(1, last), mul(c63, sub(minus_z(hx), sub(hz, hz62))))
-        ez_next = add(e(2, last), mul(c63, sub(sub(hy, hy62), minus_y(hx))))
-        write_planes(grid, up, [hy, hz, ex_next, ey_next, ez_next, c63])
+            ex, ey, ez = (e[31, comp] for comp in range(3))
+            hy = sub(h[31, 1], scale(0.5, add(plus_z(ex), ez)))
+            hz = add(h[31, 2], scale(0.5, add(ey, plus_y(ex))))
+            sent_up, sent_down = [hy, hz], [e[0, 1], e[0, 2]]
+        else:
+            ex, ey, ez = (e[0, comp] for comp in range(3))
+            hx = sub(h[0, 0], scale(0.5, sub(plus_y(ez), plus_z(ey))))
+            hy = sub(h[0, 1], scale(0.5, sub(plus_z(ex), sub(e[1, 2], ez))))
+            hz = sub(h[0, 2], scale(0.5, sub(sub(e[1, 1], ey), plus_y(ex))))
+            ey_next = add(ey, mul(c[0], sub(minus_z(hx), hz)))
+            ez_next = add(ez, mul(c[0], sub(hy, minus_y(hx))))
+            sent_down = [ey, ez, ey_next, ez_next, c[0]]
+            ex, ey, ez = (e[62, comp] for comp in range(3))
+            hy62 = sub(h[62, 1], scale(0.5, sub(plus_z(ex), sub(e[63, 2], ez))))
+            hz62 = sub(h[62, 2], scale(0.5, sub(sub(e[63, 1], ey), plus_y(ex))))
+            ex, ey, ez = (e[63, comp] for comp in range(3))
+            hx = sub(h[63, 0], scale(0.5, sub(plus_y(ez), plus_z(ey))))
+            hy = sub(h[63, 1], scale(0.5, add(plus_z(ex), ez)))
+            hz = add(h[63, 2], scale(0.5, add(ey, plus_y(ex))))
+            ex_next = add(ex, mul(c[63], sub(minus_y(hz), minus_z(hy))))
+            ey_next = add(ey, mul(c[63], sub(minus_z(hx), sub(hz, hz62))))
+            ez_next = add(ez, mul(c[63], sub(sub(hy, hy62), minus_y(hx))))
+            sent_up = [hy, hz, ex_next, ey_next, ez_next, c[63]]
+        write_planes(up, sent_up)
+        write_planes(down, sent_down)
+        write_message(grid, to_up, sent_up, gz)
+        write_message(grid, to_down, sent_down, gz)
 
     by_level(body)
 
 
-def join_y(up, down, yin, yzin, rtile, to_up, to_down, ptile):
+def join_y(up_in, down_in, c_planes, yin, yzin, r_own, r_other, to_up, to_down, ptile, patched):
     def body(grid, gz):
-        top = joined(yin[...], yzin[...], gz)
-        to_up[...] = up[...]
-        to_down[...] = down[...]
-        shape = (grid.height, 128)
+        top = yin[...] + yzin[...]
+        lane, row = lanes_of(top.shape), rows_of(top.shape)
+        to_up[...] = up_in[...]
+        to_down[...] = down_in[...]
+        shape = (2 * grid.own, 128)
         if grid is Coarse:
             ptile[...] = top
-            at = 5 * 7
-            change = jnp.where(lanes_of(shape) == 127, 0.5 * column_of(top, 3, 7, 0, shape, 1), 0.0)
-            to_up[pl.ds(at, 5), :] = to_up[pl.ds(at, 5), :] + change[:5]
+            rows = pl.ds(8 * 7, 8)
+            change = jnp.where(lanes_of(shape) == 127, 0.5 * column_of(top, 3, 7, 0, grid), 0.0)
+            to_up[rows, :] = to_up[rows, :] + change
             return
-        r = rtile[...]
-        lane, row = lanes_of(top.shape), rows_of(top.shape)
+        r = r_own[pl.ds(R_ROW, 8), :] + r_other[pl.ds(FACE + R_ROW, 8), :]
         kind = (lane % 32) // 8
-        px = top - 0.5 * roll_lanes(r, -8) + 0.5 * (roll_lanes(top, -17) - roll_lanes(top, -16))
+        above = jnp.where(lane % 8 == 7, 0.0, roll_lanes(top, -1))
+        px = top - 0.5 * roll_lanes(r, -8) + 0.5 * roll_lanes(above - top, -16)
         beside = roll_rows(top, -1)
         beside = jnp.where(row == 7, jnp.where(lane >= 96, 0.0, roll_lanes(beside, -32)), beside)
-        pz = top + 0.5 * roll_lanes(r, 8) - 0.5 * (roll_lanes(beside, -8) - roll_lanes(top, -8))
+        pz = top + 0.5 * roll_lanes(r, 8) - 0.5 * roll_lanes(beside - top, -8)
         plane = jnp.where(kind == 0, px, jnp.where(kind == 1, pz, 0.0))
         ptile[...] = plane
-
-        def change(ref, target, index, c, value):
-            change = jnp.where(lanes_of(shape) == 0, c * value, 0.0)
+        bottom = lanes_of(shape) == 0
+        (c0,), (c63,) = read_planes(grid, c_planes, 0, 3)
+        low = jnp.where(bottom, c0 * column_of(plane, 0, 0, 0, grid), 0.0)
+        high_z = jnp.where(bottom, c63 * column_of(plane, 3, 7, 0, grid), 0.0)
+        high_x = jnp.where(bottom, -c63 * column_of(plane, 3, 7, 8, grid), 0.0)
+        ey_top = column_of(top, 0, 0, 16, grid)
+        patched[pl.ds(0, 16), :] = low
+        patched[pl.ds(16, 16), :] = ey_top
+
+        def change(ref, index, value):
             rows = pl.ds(10 * index, 10)
-            target[rows, :] = ref[rows, :] + change[:10]
-
-        ((c0,),) = read_planes(grid, down, 4)
-        ((c63,),) = read_planes(grid, up, 5)
-        change(down, to_down, 3, c0, column_of(plane, 0, 0, 0, shape, 2))
-        change(up, to_up, 4, c63, column_of(plane, 3, 7, 0, shape, 2))
-        change(up, to_up, 2, c63, -column_of(plane, 3, 7, 8, shape, 2))
-        to_down[pl.ds(50, 10), :] = column_of(top, 0, 0, 16, shape, 2)[:10]
+            ref[rows, :] = ref[rows, :] + sent_rows(value, gz)
+
+        change(to_down, 3, low)
+        change(to_up, 4, high_z)
+        change(to_up, 2, high_x)
+        to_down[pl.ds(50, 10), :] = sent_rows(ey_top, gz)
 
     by_level(body)
 
@@ -641,7 +737,7 @@
 ):
     def body(grid, gz):
         first = own_first(grid, gz)
-        tile = ptile[...]
+        tile = jnp.where(gz == 0, ptile[...], roll_lanes(ptile[...], -3))
 
         def write(source, target, sem, layer=None):
             source, target = own_layers(grid, source, gz), block_layers(grid, target)
@@ -718,19 +814,30 @@
 
 
 def correct(
-    up_own, down_own, from_below, from_above, c_ext, e_edge, h_edge, e_in, h_in, e_out, h_out, e_tile, h_tile, sems
+    up,
+    down,
+    c_planes,
+    patched,
+    from_below,
+    from_above,
+    e_edge,
+    h_edge,
+    e_in,
+    h_in,
+    e_out,
+    h_out,
+    e_tile,
+    h_tile,
+    sems,
 ):
     def body(grid, gz):
         last = grid.last
 
         def put(ref, edge, comp, x, change):
             for part, p in enumerate(change):
-                moved = pltpu.roll(p, grid.height - own_first(grid, gz), 0)[: grid.own]
+                own = jnp.where(gz == 0, p[: grid.own], p[grid.own :])
                 rows = pl.ds(grid.step * x % 8 + part, grid.own, stride=8)
-                ref[edge, comp, rows, :] = ref[edge, comp, rows, :] + moved
-
-        def c(x):
-            return column(grid, lambda rows: c_ext[rows, :], x)
+                ref[edge, comp, rows, :] = ref[edge, comp, rows, :] + own
 
         def finish(edge):
             copies = []
@@ -744,9 +851,9 @@
 
         if grid is Fine:
             zero = [jnp.zeros((16, 128), F32)]
-            ey64, ez64, ey64_part, ez64_part, c64, ey_top = read_planes(grid, from_above, *range(6))
-            hy63, hz63 = read_planes(grid, up_own, 0, 1)
-            c62, c63 = c(62), c(63)
+            ey64, ez64, ey64_part, ez64_part, c64, ey_top = read_message(grid, from_above, 6, gz)
+            hy63, hz63 = read_planes(grid, up, 0, 1)
+            c0, c1, c62, c63 = read_planes(grid, c_planes, *range(4))
             ghost = -0.5 * ey_top[0]
             dhy, dhz = scale(0.5, ez64), scale(-0.5, ey64)
             dex = mul(c63, sub(minus_y(dhz, ghost), minus_z(dhy)))
@@ -755,11 +862,11 @@
             dex62 = mul(c62, minus_y(zero, ghost))
             ey64_next = add(ey64_part, mul(c64, add(hz63, dhz)))
             ez64_next = sub(ez64_part, mul(c64, add(hy63, dhy)))
-            dhx2 = halved(sub(plus_y(dez), plus_z(dey)))
-            dhy2 = add(dhy, halved(sub(plus_z(dex), sub(ez64_next, dez))))
-            dhz2 = add(dhz, halved(sub(sub(ey64_next, dey), plus_y(dex))))
-            dhy62 = halved(sub(plus_z(dex62), dez))
-            dhz62 = halved(sub(dey, plus_y(dex62)))
+            dhx2 = scale(-0.5, sub(plus_y(dez), plus_z(dey)))
+            dhy2 = add(dhy, scale(-0.5, sub(plus_z(dex), sub(ez64_next, dez))))
+            dhz2 = add(dhz, scale(-0.5, sub(sub(ey64_next, dey), plus_y(dex))))
+            dhy62 = scale(-0.5, sub(plus_z(dex62), dez))
+            dhz62 = scale(-0.5, sub(dey, plus_y(dex62)))
             put(h_tile, 1, 0, 63, dhx2)
             put(h_tile, 1, 1, 63, dhy2)
             put(h_tile, 1, 2, 63, dhz2)
@@ -773,9 +880,10 @@
             put(e_tile, 1, 2, 62, mul(c62, dhy62))
             copies = finish(1)
 
-            hy_part, hz_part, ex_part, ey_part, ez_part, cm = read_planes(grid, from_below, *range(6))
-            ey0, ez0, ey0_part, ez0_part, c0, ey_top = read_planes(grid, down_own, *range(6))
-            c1 = c(1)
+            hy_part, hz_part, ex_part, ey_part, ez_part, cm = read_message(grid, from_below, 6, gz)
+            ey0, ez0, ey0_part, ez0_part = read_planes(grid, down, *range(4))
+            ez0_change, ey_top = read_planes(grid, patched, 0, 1)
+            ez0_part = add(ez0_part, ez0_change)
             ghost = -0.5 * ey_top[0]
             dhy, dhz = scale(0.5, ez0), scale(-0.5, ey0)
             hym, hzm = add(hy_part, dhy), add(hz_part, dhz)
@@ -783,11 +891,11 @@
             eym = sub(ey_part, mul(cm, dhz))
             ezm = add(ez_part, mul(cm, dhy))
             dey, dez = mul(c0, hzm), scale(-1.0, mul(c0, hym))
-            dhx2 = halved(sub(plus_y(dez), plus_z(dey)))
+            dhx2 = scale(-0.5, sub(plus_y(dez), plus_z(dey)))
             dhy2 = scale(-0.5, dez)
             dhz2 = scale(0.5, dey)
-            hym2 = add(hym, halved(sub(plus_z(exm), sub(add(ez0_part, dez), ezm))))
-            hzm2 = add(hzm, halved(sub(sub(add(ey0_part, dey), eym), plus_y(exm))))
+            hym2 = add(hym, scale(-0.5, sub(plus_z(exm), sub(add(ez0_part, dez), ezm))))
+            hzm2 = add(hzm, scale(-0.5, sub(sub(add(ey0_part, dey), eym), plus_y(exm))))
             put(h_tile, 0, 0, 0, dhx2)
             put(h_tile, 0, 1, 0, dhy2)
             put(h_tile, 0, 2, 0, dhz2)
@@ -798,8 +906,8 @@
             put(e_tile, 0, 2, 1, scale(-1.0, mul(c1, dhy2)))
             copies += finish(0)
         else:
-            ey32, ez32 = read_planes(grid, from_above, 0, 1)
-            c31 = c(last)
+            ey32, ez32 = read_message(grid, from_above, 2, gz)
+            c0, c31 = read_planes(grid, c_planes, 0, 1)
             dhy, dhz = scale(0.5, ez32), scale(-0.5, ey32)
             put(h_tile, 1, 1, last, dhy)
             put(h_tile, 1, 2, last, dhz)
@@ -807,9 +915,8 @@
             put(e_tile, 1, 1, last, scale(-1.0, mul(c31, dhz)))
             put(e_tile, 1, 2, last, mul(c31, dhy))
             copies = finish(1)
-            hy_part, hz_part = read_planes(grid, from_below, 0, 1)
-            ey0, ez0 = read_planes(grid, down_own, 0, 1)
-            c0 = c(0)
+            hy_part, hz_part = read_message(grid, from_below, 2, gz)
+            ey0, ez0 = read_planes(grid, down, 0, 1)
             put(e_tile, 0, 1, 0, mul(c0, add(hz_part, scale(-0.5, ey0))))
             put(e_tile, 0, 2, 0, scale(-1.0, mul(c0, add(hy_part, scale(0.5, ez0)))))
             copies += finish(0)
@@ -835,40 +942,47 @@
     h = magnetic.reshape(3, ROWS, 128)
     m = material.reshape(ROWS, 128)
     dma = pltpu.SemaphoreType.DMA
-    e_ext, zmsg, ytile = kernel_call(
+    e_ext, zmsg, ytile, columns = kernel_call(
         gather,
-        [vmem(3, EXT, 128), vmem(7, HALO, 128), vmem(8, 128)],
+        [vmem(3, EXT, 128), vmem(FACE + COLUMNS, 128), vmem(8, 128), vmem(COLUMNS, 128)],
         [HBM] * 3,
-        [VM] * 3,
-        [pltpu.VMEM((3, ROWS, 128), F32), pltpu.VMEM((HALO, 128), jnp.int32), dma((8,))],
+        [VM] * 4,
+        [
+            pltpu.VMEM((3, ROWS, 128), F32),
+            pltpu.VMEM((HALO, 128), jnp.int32),
+            pltpu.VMEM((2, 3, 64, 128), F32),
+            pltpu.VMEM((2, 64, 128), jnp.int32),
+            dma((12,)),
+        ],
     )(far(e), far(h), far(m))
-    h, m, ytile = lax.optimization_barrier((h, m, ytile))
     zin = across(zmsg, dz=1)
     yzin = across(ytile, dy=1, dz=1)
     yin = across(ytile, dy=1)
-    e_ext, h_ext, c_ext, rtile, up, down = kernel_call(
+    e_ext, h_ext, c_ext, up, down, up_part, down_part, c_planes = kernel_call(
         extend,
         [
             vmem(3, EXT, 128),
             vmem(3, EXT, 128),
             vmem(EXT, 128),
-            vmem(8, 128),
+            vmem(96, 128),
+            vmem(96, 128),
+            vmem(64, 128),
             vmem(64, 128),
             vmem(64, 128),
         ],
         [VM] * 4 + [HBM, VM],
-        [VM] * 6,
+        [VM] * 8,
         [pltpu.SMEM((MATS,), F32), dma((1,))],
         aliases={0: 0},
-    )(held(e_ext), held(h), held(m), held(zin), far(permittivity), held(ytile))
-    to_up, to_down, ptile = kernel_call(
+    )(held(e_ext), held(h), held(m), held(zin), far(permittivity), held(columns))
+    to_up, to_down, ptile, patched = kernel_call(
         join_y,
-        [vmem(64, 128), vmem(64, 128), vmem(8, 128)],
-        [VM] * 5,
-        [VM] * 3,
-    )(*(held(part) for part in (up, down, yin, yzin, rtile)))
-    from_below = across(to_up, dx=1)
-    from_above = across(to_down, dx=-1)
+        [vmem(64, 128), vmem(64, 128), vmem(8, 128), vmem(32, 128)],
+        [VM] * 7,
+        [VM] * 4,
+    )(*(held(part) for part in (up_part, down_part, c_planes, yin, yzin, columns, zin)))
+    from_below = across(to_up, dx=1, dz=1)
+    from_above = across(to_down, dx=-1, dz=1)
     whole = jax.ShapeDtypeStruct((3, ROWS, 128), F32)
     e_out, h_out, e_edge, h_edge = kernel_call(
         advance,
@@ -880,12 +994,12 @@
     e_out, h_out, _, _ = kernel_call(
         correct,
         [whole, whole, vmem(2, 3, 64, 128), vmem(2, 3, 64, 128)],
-        [VM] * 7 + [HBM] * 2,
+        [VM] * 8 + [HBM] * 2,
         [HBM] * 2 + [VM] * 2,
         [dma((4,))],
-        aliases={7: 0, 8: 1, 5: 2, 6: 3},
+        aliases={8: 0, 9: 1, 6: 2, 7: 3},
     )(
-        *(held(part) for part in (to_up, to_down, from_below, from_above, c_ext, e_edge, h_edge)),
+        *(held(part) for part in (up, down, c_planes, patched, from_below, from_above, e_edge, h_edge)),
         e_out,
         h_out,
     )

time: 15.1 us -> 14.5 us (0.960)
  waiting for transfers between devices: 2.9 us -> 2.44 us
  starting transfers between devices: 6.72 us -> 6.45 us
    ppermute x5, waiting for transfers between devices: 2.9 us -> 2.44 us  [across(): return lax.ppermute(x, ('gx', 'gy', 'gz'), pairs)]
    ppermute x5, starting transfers between devices: 6.72 us -> 6.45 us  [across(): return lax.ppermute(x, ('gx', 'gy', 'gz'), pairs)]
  transfers between devices with their start and end apart: 5 -> 5, of which waited for: 3 -> 3; matrix products, arithmetic and copies ran while one was open for 0% -> 0% of each run, Pallas kernels for 14% -> 15%
where the time goes in v2:
time: 14.5 us; the launch traced here: 14.3 us
  starting transfers between devices  6.45 us (44%)
  Pallas kernels  4.71 us (32%)
  waiting for transfers between devices  2.44 us (17%)
  between operations  0.68 us (5%)
    ppermute x5, starting transfers between devices, across(): return lax.ppermute(x, ('gx', 'gy', 'gz'), pairs)  6.45 us
    ppermute x5, waiting for transfers between devices, across(): return lax.ppermute(x, ('gx', 'gy', 'gz'), pairs)  2.44 us
    pallas_call x1, Pallas kernels, fast_shards(): kernel_call(gather, [vmem(3, EXT, 128), vmem(FACE + COLUMNS, 128), vmem(8...  1.72 us
    pallas_call x1, Pallas kernels, fast_shards(): kernel_call(advance, [whole, whole, vmem(2, 3, 64, 128), vmem(2, 3, 64, 1...  1.32 us
    pallas_call x1, Pallas kernels, fast_shards(): kernel_call(extend, [vmem(3, EXT, 128), vmem(3, EXT, 128), vmem(EXT, 128)...  0.8 us
    pallas_call x1, Pallas kernels, fast_shards(): kernel_call(correct, [whole, whole, vmem(2, 3, 64, 128), vmem(2, 3, 64, 1...  0.78 us
  transfers between devices with their start and end apart: 5, of which 3 were waited for; matrix products, arithmetic and copies ran while one was open for 0% of the time, Pallas kernels for 15%

profile of v2, /device:TPU:0, one launch (start us, length us, event | category | flops | bytes accessed | tf_op | source)
XLA Modules:
  0.0 14.3 jit_solution(8263843524376529)
XLA Ops:
  0.6 0.0 copy-start
  0.6 0.0 copy-start.1
  0.6 1.7 %shard_map.59 = (f32[3,1296,128]{2,1,0:T(8,128)S(1)}, f32[1088,128]{1,0:T(8,128)S(1)}, f32[8,128]{1,0:T(8,128)S(1)}, f32[192,128]{1,0:T(8,128)S(1)}) custom-call(f32[3,512,128]{2,1,0:T(8,128)} %bitcast.9, f32[3,512,128]{2,1,0:T(8,128)} %bitcast.5, s32[512,128]{1,0:T(8,128)} %bitcast.7), custom_call_target="tpu_custom_call" | custom-call | tf_op jit(solution)/shard_map/pallas_call | solution.py:945
  2.4 0.5 %collective-permute-start = (f32[1088,128]{1,0:T(8,128)S(1)}, f32[1088,128]{1,0:T(8,128)S(1)}, u32[]{:S(2)}, u32[]{:S(2)}) collective-permute-start(f32[1088,128]{1,0:T(8,128)S(1)} %get-tuple-element.25), channel_id=1, source_target_pairs={{0,1},{1,0},{2,3},{3,2},{4,5},{5,4},{6,7},{7,6},{8,9},{9,8},{10,11... | collective-permute-start | bytes 1671176 | tf_op jit(solution)/shard_map/ppermute | solution.py:937
  2.9 2.3 %collective-permute-start.1 = (f32[8,128]{1,0:T(8,128)S(1)}, f32[8,128]{1,0:T(8,128)S(1)}, u32[]{:S(2)}, u32[]{:S(2)}) collective-permute-start(f32[8,128]{1,0:T(8,128)S(1)} %get-tuple-element.32), channel_id=1, source_target_pairs={{0,2},{1,3},{2,0},{3,1},{4,6},{5,7},{6,4},{7,5},{8,10},{9,11},{10,... | collective-permute-start | bytes 12296 | tf_op jit(solution)/shard_map/ppermute | solution.py:937
  5.2 0.1 collective-permute-start.2
  5.3 0.0 collective-permute-done.zmsg.r_other
  5.3 0.0 copy-done
  5.3 0.0 copy-done.1
  5.3 0.8 %shard_map.60 = (f32[3,1296,128]{2,1,0:T(8,128)S(1)}, f32[3,1296,128]{2,1,0:T(8,128)S(1)}, f32[1296,128]{1,0:T(8,128)S(1)}, f32[96,128]{1,0:T(8,128)S(1)}, f32[9...) custom-call(f32[3,1296,128]{2,1,0:T(8,128)S(1)} %get-tuple-element.2, ...), custom_call_target="tpu_custom_call", output_to_operand_aliasing={{0}: (0, {})} | custom-call | tf_op jit(solution)/shard_map/pallas_call | solution.py:961
  6.1 0.7 %collective-permute-done.1.yin = f32[8,128]{1,0:T(8,128)S(1)} collective-permute-done((f32[8,128]{1,0:T(8,128)S(1)}, f32[8,128]{1,0:T(8,128)S(1)}, u32[]{:S(2)}, u32[]{:S(2)}) %collective-permute-start.1) | collective-permute-done | bytes 4128 | tf_op jit(solution)/shard_map/ppermute | solution.py:937
  6.8 1.4 %collective-permute-done.2.yzin = f32[8,128]{1,0:T(8,128)S(1)} collective-permute-done((f32[8,128]{1,0:T(8,128)S(1)}, f32[8,128]{1,0:T(8,128)S(1)}, u32[]{:S(2)}, u32[]{:S(2)}) %collective-permute-start.2) | collective-permute-done | bytes 4128 | tf_op jit(solution)/shard_map/ppermute | solution.py:937
  8.2 0.1 shard_map.61
  8.3 1.3 %collective-permute-start.3 = (f32[64,128]{1,0:T(8,128)S(1)}, f32[64,128]{1,0:T(8,128)S(1)}, u32[]{:S(2)}, u32[]{:S(2)}) collective-permute-start(f32[64,128]{1,0:T(8,128)S(1)} %get-tuple-element.34), channel_id=1, source_target_pairs={{0,5},{1,4},{2,7},{3,6},{4,9},{5,8},{6,11},{7,10},{8,13},{9,12},{1... | collective-permute-start | bytes 98312 | tf_op jit(solution)/shard_map/ppermute | solution.py:937
  9.7 2.2 %collective-permute-start.4 = (f32[64,128]{1,0:T(8,128)S(1)}, f32[64,128]{1,0:T(8,128)S(1)}, u32[]{:S(2)}, u32[]{:S(2)}) collective-permute-start(f32[64,128]{1,0:T(8,128)S(1)} %get-tuple-element.35), channel_id=1, source_target_pairs={{0,13},{1,12},{2,15},{3,14},{4,1},{5,0},{6,3},{7,2},{8,5},{9,4},{1... | collective-permute-start | bytes 98312 | tf_op jit(solution)/shard_map/ppermute | solution.py:937
  11.9 1.3 %shard_map.62 = (f32[3,512,128]{2,1,0:T(8,128)}, f32[3,512,128]{2,1,0:T(8,128)}, f32[2,3,64,128]{3,2,1,0:T(8,128)S(1)}, f32[2,3,64,128]{3,2,1,0:T(8,128)S(1)}) custom-call(f32[3,1296,128]{2,1,0:T(8,128)S(1)} %get-tuple-element.36.e_ext, f32[3,1296,128]{2,1,0:T(8,128)S(1)} %get-tuple-element.37.h_ext, f32[1296,128]{1,0:T(8,128)S(1)} %get-tuple-element.38.c_ext, ...), custom_call_target="tpu_custom_call" | custom-call | tf_op jit(solution)/shard_map/pallas_call | solution.py:987
  13.2 0.3 %collective-permute-done.3.from_below = f32[64,128]{1,0:T(8,128)S(1)} collective-permute-done((f32[64,128]{1,0:T(8,128)S(1)}, f32[64,128]{1,0:T(8,128)S(1)}, u32[]{:S(2)}, u32[]{:S(2)}) %collective-permute-start.3) | collective-permute-done | bytes 32800 | tf_op jit(solution)/shard_map/ppermute | solution.py:937
  13.5 0.0 collective-permute-done.4.from_above
  13.5 0.8 %shard_map.63 = (f32[3,512,128]{2,1,0:T(8,128)}, f32[3,512,128]{2,1,0:T(8,128)}, f32[2,3,64,128]{3,2,1,0:T(8,128)S(1)}, f32[2,3,64,128]{3,2,1,0:T(8,128)S(1)}) custom-call(f32[96,128]{1,0:T(8,128)S(1)} %get-tuple-element.27.up, f32[96,128]{1,0:T(8,128)S(1)} %get-tuple-element.28.down, ...), custom_call_target="tpu_custom_call", output_to_operand_aliasing={{0}: (8, {}), {1}: (9, {}), {2}: (6, {}), {3}: (7, {})} | custom-call | tf_op jit(solution)/shard_map/pallas_call | solution.py:994
Async XLA Ops:
  0.6 4.7 %copy-start = (f32[1,1,1,3,65536]{4,2,3,1,0:T(1,128)S(1)}, f32[1,1,1,3,65536]{4,2,3,1,0:T(1,128)}, u32[]{:S(2)}) copy-start(f32[1,1,1,3,65536]{4,2,3,1,0:T(1,128)} %param.5) | copy-start | bytes 2359300
  0.6 4.7 %copy-start.1 = (s32[1,1,1,65536]{3,2,1,0:T(1,128)S(1)}, s32[1,1,1,65536]{3,2,1,0:T(1,128)}, u32[]{:S(2)}) copy-start(s32[1,1,1,65536]{3,2,1,0:T(1,128)} %param.6) | copy-start | bytes 786436
  2.4 2.9 %collective-permute-start = (f32[1088,128]{1,0:T(8,128)S(1)}, f32[1088,128]{1,0:T(8,128)S(1)}, u32[]{:S(2)}, u32[]{:S(2)}) collective-permute-start(f32[1088,128]{1,0:T(8,128)S(1)} %get-tuple-element.25), channel_id=1, source_target_pairs={{0,1},{1,0},{2,3},{3,2},{4,5},{5,4},{6,7},{7,6},{8,9},{9,8},{10,11... | collective-permute-start | bytes 1671176 | tf_op jit(solution)/shard_map/ppermute | solution.py:937
  2.9 3.9 %collective-permute-start.1 = (f32[8,128]{1,0:T(8,128)S(1)}, f32[8,128]{1,0:T(8,128)S(1)}, u32[]{:S(2)}, u32[]{:S(2)}) collective-permute-start(f32[8,128]{1,0:T(8,128)S(1)} %get-tuple-element.32), channel_id=1, source_target_pairs={{0,2},{1,3},{2,0},{3,1},{4,6},{5,7},{6,4},{7,5},{8,10},{9,11},{10,... | collective-permute-start | bytes 12296 | tf_op jit(solution)/shard_map/ppermute | solution.py:937
  5.2 3.0 %collective-permute-start.2 = (f32[8,128]{1,0:T(8,128)S(1)}, f32[8,128]{1,0:T(8,128)S(1)}, u32[]{:S(2)}, u32[]{:S(2)}) collective-permute-start(f32[8,128]{1,0:T(8,128)S(1)} %get-tuple-element.32), channel_id=1, source_target_pairs={{0,3},{1,2},{2,1},{3,0},{4,7},{5,6},{6,5},{7,4},{8,11},{9,10},{10,... | collective-permute-start | bytes 12296 | tf_op jit(solution)/shard_map/ppermute | solution.py:937
  8.3 5.2 %collective-permute-start.3 = (f32[64,128]{1,0:T(8,128)S(1)}, f32[64,128]{1,0:T(8,128)S(1)}, u32[]{:S(2)}, u32[]{:S(2)}) collective-permute-start(f32[64,128]{1,0:T(8,128)S(1)} %get-tuple-element.34), channel_id=1, source_target_pairs={{0,5},{1,4},{2,7},{3,6},{4,9},{5,8},{6,11},{7,10},{8,13},{9,12},{1... | collective-permute-start | bytes 98312 | tf_op jit(solution)/shard_map/ppermute | solution.py:937
  9.7 3.8 %collective-permute-start.4 = (f32[64,128]{1,0:T(8,128)S(1)}, f32[64,128]{1,0:T(8,128)S(1)}, u32[]{:S(2)}, u32[]{:S(2)}) collective-permute-start(f32[64,128]{1,0:T(8,128)S(1)} %get-tuple-element.35), channel_id=1, source_target_pairs={{0,13},{1,12},{2,15},{3,14},{4,1},{5,0},{6,3},{7,2},{8,5},{9,4},{1... | collective-permute-start | bytes 98312 | tf_op jit(solution)/shard_map/ppermute | solution.py:937

commit v3 on v2

--- a/solution.py
+++ b/solution.py
@@ -250,9 +250,10 @@
     return pltpu.with_memory_space_constraint(x, pltpu.HBM)
 
 
-def kernel_call(body, out_shape, in_specs, out_specs, scratch=(), aliases=None):
+def kernel_call(body, out_shape, in_specs, out_specs, scratch=(), aliases=None, cost=None):
     return pl.pallas_call(
         body,
+        cost_estimate=cost,
         out_shape=out_shape,
         in_specs=in_specs,
         out_specs=out_specs,
@@ -330,12 +331,6 @@
     for block in range(4):
         tile = at_lane(tile, lane_from, 32 * block + slot, column[8 * block : 8 * block + 8])
     return tile
-
-
-def edge_tiles(grid, ref):
-    view = ref.reshape(*ref.shape[:-2], grid.own, grid.depth, 128)
-    lead = (slice(None),) * (len(ref.shape) - 1)
-    return [view.at[lead + (pl.ds((grid.depth - 8) * end, 8),)] for end in range(2)]
 
 
 FINE_E = [(0, comp) for comp in range(3)] + [(1, 1), (1, 2)] + [(x, comp) for x in (62, 63) for comp in range(3)]
@@ -353,84 +348,106 @@
     return (FINE_E, FINE_H, FINE_M) if grid is Fine else (COARSE_E, COARSE_H, COARSE_M)
 
 
-def gather(e_hbm, h_hbm, m_hbm, e_ext, zmsg, ytile, columns, h_top, m_edge, h_ends, m_ends, sems):
+def top_tile(tile, layer, ex, ey, ez, hx, hz):
+    tile = put_column(tile, 127, layer, hx + 0.5 * ez)
+    tile = put_column(tile, 127, 8 + layer, hz - 0.5 * ex)
+    return put_column(tile, 127, 16 + layer, ey)
+
+
+def edge_tiles(grid, ref):
+    view = ref.reshape(grid.own, grid.depth, 128)
+    return [view.at[:, pl.ds((grid.depth - 8) * end, 8), :] for end in range(2)]
+
+
+def peek(e_hbm, h_hbm, edge_tile, e_ends, h_ends, sems):
     def body(grid, gz):
-        edge = pl.ds((1 - gz) * (ROWS - HALO), HALO)
-        source, target = block_layers(grid, e_hbm), own_layers(grid, e_ext, gz)
-        first = [0, 2] if grid is Fine else [0, 1, 2]
-        e_loads = {
-            comp: pltpu.make_async_copy(source.at[comp], target.at[comp], sems.at[comp])
-            for comp in (0, 2, 1)
-        }
-        h_loads = [] if grid is Fine else [
-            pltpu.make_async_copy(h_hbm.at[comp], h_top.at[comp], sems.at[3 + comp]) for comp in (0, 2)
-        ]
-        loads = [
-            pltpu.make_async_copy(h_hbm.at[:, edge], zmsg.at[pl.ds(0, 3 * HALO)].reshape(3, HALO, 128), sems.at[6]),
-            pltpu.make_async_copy(m_hbm.at[edge], m_edge, sems.at[7]),
-        ]
+        if grid is Fine:
+            edge_tile[...] = jnp.zeros((8, 128), F32)
+            return
+        loads = []
         for end in range(2):
-            for slot, (array, ends) in enumerate(((h_hbm, h_ends), (m_hbm, m_ends))):
-                place = ends.at[end].reshape(*ends.shape[1:-2], 8, 8, 128)
-                place = place.at[(slice(None),) * (len(ends.shape) - 3) + (pl.ds(0, grid.own),)]
-                tiles = edge_tiles(grid, array)[end]
-                loads.append(pltpu.make_async_copy(tiles, place, sems.at[8 + 2 * end + slot]))
-        for load in list(e_loads.values()) + h_loads + loads:
+            rows = pl.ds((1 - gz) * (ROWS - HALO) + (HALO - 8) * end, 8)
+            loads.append(pltpu.make_async_copy(e_hbm.at[:, rows], e_ends.at[end], sems.at[2 * end]))
+            loads.append(pltpu.make_async_copy(h_hbm.at[:, rows], h_ends.at[end], sems.at[2 * end + 1]))
+        for load in loads:
             load.start()
-        clear_pads(grid, e_ext, grid.count + 1)
-        for comp in first:
-            e_loads[comp].wait()
-        for load in h_loads:
+        for load in loads:
             load.wait()
-        begin = layer_row(grid, own_first(grid, gz))
+        tile = jnp.zeros((8, 128), F32)
+        for end in range(2):
+            ex, ey, ez = (e_ends[end, comp] for comp in range(3))
+            hx, hz = h_ends[end, 0], h_ends[end, 2]
+            for kind, value in enumerate((hx + 0.5 * ez, hz - 0.5 * ex, ey)):
+                value = value if end else roll_rows(value, -3)
+                tile = at_lane(tile, 127, 96 * end + 8 * kind + 3, value)
+        edge_tile[...] = jnp.where(gz == 1, roll_lanes(tile, 1), tile)
+
+    by_level(body)
+
+
+def take_material(m_hbm, after, m_face, m_ends, sems):
+    def body(grid, gz):
+        layer = pl.ds((1 - gz) * (ROWS - HALO), HALO)
+        loads = [pltpu.make_async_copy(m_hbm.at[layer], m_face, sems.at[0])]
+        for end, tiles in enumerate(edge_tiles(grid, m_hbm)):
+            place = m_ends.at[end].reshape(8, 8, 128).at[pl.ds(0, grid.own)]
+            loads.append(pltpu.make_async_copy(tiles, place, sems.at[1 + end]))
+        for load in loads:
+            load.start()
+        for load in loads:
+            load.wait()
+
+    by_level(body)
+
+
+def gather(e_own, h_own, m_face, m_ends, zmsg, ytile, columns):
+    def body(grid, gz):
         tile = jnp.zeros((8, 128), F32)
         for layer in range(4):
             if grid is Fine:
-                row = begin + 2 * grid.stride * layer
-                tile = put_column(tile, 0, layer, average(e_ext, 0, row, grid.stride))
-                tile = put_column(tile, 0, 8 + layer, average(e_ext, 2, row, grid.stride))
+                row = 2 * grid.depth * layer
+                tile = put_column(tile, 0, layer, average(e_own, 0, row, grid.depth))
+                tile = put_column(tile, 0, 8 + layer, average(e_own, 2, row, grid.depth))
             else:
-                top = pl.ds(begin + grid.stride * layer + 3, 32, stride=4)
-                h_row = pl.ds(grid.depth * layer + 3, 32, stride=4)
-                ex, ey, ez = (e_ext[comp, top, :] for comp in range(3))
-                tile = put_column(tile, 127, layer, h_top[0, h_row, :] + 0.5 * ez)
-                tile = put_column(tile, 127, 8 + layer, h_top[2, h_row, :] - 0.5 * ex)
-                tile = put_column(tile, 127, 16 + layer, ey)
+                top = pl.ds(grid.depth * layer + 3, 32, stride=4)
+                ex, ey, ez = (e_own[comp, top, :] for comp in range(3))
+                tile = top_tile(tile, layer, ex, ey, ez, h_own[0, top, :], h_own[2, top, :])
         tile = jnp.where(gz == 1, roll_lanes(tile, 4), tile)
         ytile[...] = tile
         columns[pl.ds(R_ROW, 8), :] = tile
-        if grid is Fine:
-            e_loads[1].wait()
-        layers = HALO // grid.depth
-        from_layer = own_first(grid, gz) + (grid.own - layers) * (1 - gz)
-        for comp in range(3):
-            for layer in range(layers):
-                row = layer_row(grid, from_layer + layer)
-                to = HALO * (3 + comp) + grid.depth * layer
-                zmsg[pl.ds(to, grid.depth), :] = e_ext[comp, pl.ds(row, grid.depth), :]
         want_e, want_h, want_m = wanted(grid)
         slot = 0
+
+        def column_rows(x, part):
+            return pl.ds(grid.step * x + part, grid.own, stride=grid.depth)
+
+        def put(value):
+            nonlocal slot
+            columns[pl.ds(slot, grid.own), :] = value
+            slot += grid.own
+
         for x, comp in want_e:
             for part in range(grid.parts):
-                rows = pl.ds(begin + grid.step * x + part, grid.own, stride=grid.stride)
-                columns[pl.ds(slot, grid.own), :] = e_ext[comp, rows, :]
-                slot += grid.own
-        for load in loads:
-            load.wait()
+                put(e_own[comp, column_rows(x, part), :])
         for x, comp in want_h:
             for part in range(grid.parts):
-                rows = pl.ds(grid.step * x % 8 + part, grid.own, stride=8)
-                columns[pl.ds(slot, grid.own), :] = h_ends[int(x > 1), comp, rows, :]
-                slot += grid.own
+                put(h_own[comp, column_rows(x, part), :])
         for x in want_m:
             for part in range(grid.parts):
                 rows = pl.ds(grid.step * x % 8 + part, grid.own, stride=8)
-                columns[pl.ds(slot, grid.own), :] = m_ends[int(x > 1), rows, :].astype(F32)
-                slot += grid.own
-        zmsg[pl.ds(6 * HALO, HALO), :] = m_edge[...].astype(F32)
+                put(m_ends[int(x > 1), rows, :].astype(F32))
+        edge = pl.ds(pl.multiple_of((1 - gz) * (ROWS - HALO), HALO), HALO)
+        for comp in range(3):
+            zmsg[pl.ds(HALO * comp, HALO), :] = h_own[comp, edge, :]
+            zmsg[pl.ds(HALO * (3 + comp), HALO), :] = e_own[comp, edge, :]
+        zmsg[pl.ds(6 * HALO, HALO), :] = m_face[...].astype(F32)
         zmsg[pl.ds(FACE, COLUMNS), :] = columns[...]
 
     by_level(body)
+
+
+def join_z(ytile, edge_tile, z_in, joined, z_out):
+    joined[...] = ytile[...] + edge_tile[...]
 
 
 def up_y(grid, ref, comp, row, f):
@@ -593,7 +610,7 @@
 
 
 def extend(
-    e_in,
+    e_own,
     h_own,
     m_own,
     zmsg,
@@ -614,6 +631,13 @@
         load = pltpu.make_async_copy(permittivity, table, sems.at[0])
         load.start()
         clear_pads(grid, h_ext, 0)
+        clear_pads(grid, e_ext, grid.count + 1)
+        for layer in range(grid.own):
+            for start in range(0, grid.depth, CHUNK):
+                rows = pl.ds(layer_row(grid, own_first(grid, gz) + layer) + start, CHUNK)
+                from_rows = pl.ds(grid.depth * layer + start, CHUNK)
+                for comp in range(3):
+                    e_ext[comp, rows, :] = e_own[comp, from_rows, :]
         halo = halo_first(grid, gz)
         for layer in range(grid.count - grid.own):
             for start in range(0, grid.depth, CHUNK):
@@ -689,55 +713,76 @@
     by_level(body)
 
 
-def join_y(up_in, down_in, c_planes, yin, yzin, r_own, r_other, to_up, to_down, ptile, patched):
+def between(top, r):
+    lane, row = lanes_of(top.shape), rows_of(top.shape)
+    kind = (lane % 32) // 8
+    above = jnp.where(lane % 8 == 7, 0.0, roll_lanes(top, -1))
+    px = top - 0.5 * roll_lanes(r, -8) + 0.5 * roll_lanes(above - top, -16)
+    beside = roll_rows(top, -1)
+    beside = jnp.where(row == 7, jnp.where(lane >= 96, 0.0, roll_lanes(beside, -32)), beside)
+    pz = top + 0.5 * roll_lanes(r, 8) - 0.5 * roll_lanes(beside - top, -8)
+    return jnp.where(kind == 0, px, jnp.where(kind == 1, pz, 0.0))
+
+
+def join_y(up_in, down_in, c_planes, yzin, r_own, r_other, to_up, to_down):
     def body(grid, gz):
-        top = yin[...] + yzin[...]
-        lane, row = lanes_of(top.shape), rows_of(top.shape)
+        top = yzin[...]
         to_up[...] = up_in[...]
         to_down[...] = down_in[...]
         shape = (2 * grid.own, 128)
         if grid is Coarse:
-            ptile[...] = top
             rows = pl.ds(8 * 7, 8)
             change = jnp.where(lanes_of(shape) == 127, 0.5 * column_of(top, 3, 7, 0, grid), 0.0)
             to_up[rows, :] = to_up[rows, :] + change
             return
-        r = r_own[pl.ds(R_ROW, 8), :] + r_other[pl.ds(FACE + R_ROW, 8), :]
-        kind = (lane % 32) // 8
-        above = jnp.where(lane % 8 == 7, 0.0, roll_lanes(top, -1))
-        px = top - 0.5 * roll_lanes(r, -8) + 0.5 * roll_lanes(above - top, -16)
-        beside = roll_rows(top, -1)
-        beside = jnp.where(row == 7, jnp.where(lane >= 96, 0.0, roll_lanes(beside, -32)), beside)
-        pz = top + 0.5 * roll_lanes(r, 8) - 0.5 * roll_lanes(beside - top, -8)
-        plane = jnp.where(kind == 0, px, jnp.where(kind == 1, pz, 0.0))
-        ptile[...] = plane
+        plane = between(top, r_own[pl.ds(R_ROW, 8), :] + r_other[pl.ds(FACE + R_ROW, 8), :])
         bottom = lanes_of(shape) == 0
         (c0,), (c63,) = read_planes(grid, c_planes, 0, 3)
-        low = jnp.where(bottom, c0 * column_of(plane, 0, 0, 0, grid), 0.0)
-        high_z = jnp.where(bottom, c63 * column_of(plane, 3, 7, 0, grid), 0.0)
-        high_x = jnp.where(bottom, -c63 * column_of(plane, 3, 7, 8, grid), 0.0)
-        ey_top = column_of(top, 0, 0, 16, grid)
-        patched[pl.ds(0, 16), :] = low
-        patched[pl.ds(16, 16), :] = ey_top
 
         def change(ref, index, value):
             rows = pl.ds(10 * index, 10)
             ref[rows, :] = ref[rows, :] + sent_rows(value, gz)
 
-        change(to_down, 3, low)
-        change(to_up, 4, high_z)
-        change(to_up, 2, high_x)
-        to_down[pl.ds(50, 10), :] = sent_rows(ey_top, gz)
+        change(to_down, 3, jnp.where(bottom, c0 * column_of(plane, 0, 0, 0, grid), 0.0))
+        change(to_up, 4, jnp.where(bottom, c63 * column_of(plane, 3, 7, 0, grid), 0.0))
+        change(to_up, 2, jnp.where(bottom, -c63 * column_of(plane, 3, 7, 8, grid), 0.0))
+        to_down[pl.ds(50, 10), :] = sent_rows(column_of(top, 0, 0, 16, grid), gz)
 
     by_level(body)
 
 
 def advance(
-    e_ext, h_ext, c_ext, ptile, e_out, h_out, e_edge, h_edge, e_mid, h_mid, e_last, plane, sems
+    e_ext,
+    h_ext,
+    c_ext,
+    c_planes,
+    yin,
+    yzin,
+    r_own,
+    r_other,
+    e_out,
+    h_out,
+    e_edge,
+    h_edge,
+    patched,
+    e_mid,
+    h_mid,
+    e_last,
+    plane,
+    sems,
 ):
     def body(grid, gz):
         first = own_first(grid, gz)
-        tile = jnp.where(gz == 0, ptile[...], roll_lanes(ptile[...], -3))
+        upper = lanes_of((8, 128)) % 8 >= 4
+        tile = jnp.where(upper == (gz == 0), yzin[...], yin[...])
+        if grid is Fine:
+            top = tile
+            tile = between(top, r_own[pl.ds(R_ROW, 8), :] + r_other[pl.ds(FACE + R_ROW, 8), :])
+            ((c0,),) = read_planes(grid, c_planes, 0)
+            change = jnp.where(lanes_of((16, 128)) == 0, c0 * column_of(tile, 0, 0, 0, grid), 0.0)
+            patched[pl.ds(0, 16), :] = change
+            patched[pl.ds(16, 16), :] = column_of(top, 0, 0, 16, grid)
+        tile = jnp.where(gz == 0, tile, roll_lanes(tile, -3))
 
         def write(source, target, sem, layer=None):
             source, target = own_layers(grid, source, gz), block_layers(grid, target)
@@ -942,22 +987,37 @@
     h = magnetic.reshape(3, ROWS, 128)
     m = material.reshape(ROWS, 128)
     dma = pltpu.SemaphoreType.DMA
-    e_ext, zmsg, ytile, columns = kernel_call(
+    edge_tile = kernel_call(
+        peek,
+        vmem(8, 128),
+        [HBM] * 2,
+        VM,
+        [pltpu.VMEM((2, 3, 8, 128), F32)] * 2 + [dma((4,))],
+    )(far(e), far(h))
+    m_face, m_ends = kernel_call(
+        take_material,
+        [vmem(HALO, 128, dtype=jnp.int32), vmem(2, 64, 128, dtype=jnp.int32)],
+        [HBM, VM],
+        [VM] * 2,
+        [dma((3,))],
+    )(far(m), held(edge_tile))
+    edge_tile = across(edge_tile, dz=1)
+    zmsg, ytile, columns = kernel_call(
         gather,
-        [vmem(3, EXT, 128), vmem(FACE + COLUMNS, 128), vmem(8, 128), vmem(COLUMNS, 128)],
-        [HBM] * 3,
+        [vmem(FACE + COLUMNS, 128), vmem(8, 128), vmem(COLUMNS, 128)],
         [VM] * 4,
-        [
-            pltpu.VMEM((3, ROWS, 128), F32),
-            pltpu.VMEM((HALO, 128), jnp.int32),
-            pltpu.VMEM((2, 3, 64, 128), F32),
-            pltpu.VMEM((2, 64, 128), jnp.int32),
-            dma((12,)),
-        ],
-    )(far(e), far(h), far(m))
+        [VM] * 3,
+    )(held(e), held(h), held(m_face), held(m_ends))
+    ytile, zmsg = kernel_call(
+        join_z,
+        [vmem(8, 128), vmem(FACE + COLUMNS, 128)],
+        [VM] * 3,
+        [VM] * 2,
+        aliases={2: 1},
+    )(held(ytile), held(edge_tile), held(zmsg))
     zin = across(zmsg, dz=1)
+    yin = across(ytile, dy=1)
     yzin = across(ytile, dy=1, dz=1)
-    yin = across(ytile, dy=1)
     e_ext, h_ext, c_ext, up, down, up_part, down_part, c_planes = kernel_call(
         extend,
         [
@@ -973,24 +1033,24 @@
         [VM] * 4 + [HBM, VM],
         [VM] * 8,
         [pltpu.SMEM((MATS,), F32), dma((1,))],
-        aliases={0: 0},
-    )(held(e_ext), held(h), held(m), held(zin), far(permittivity), held(columns))
-    to_up, to_down, ptile, patched = kernel_call(
+    )(held(e), held(h), held(m), held(zin), far(permittivity), held(columns))
+    to_up, to_down = kernel_call(
         join_y,
-        [vmem(64, 128), vmem(64, 128), vmem(8, 128), vmem(32, 128)],
-        [VM] * 7,
-        [VM] * 4,
-    )(*(held(part) for part in (up_part, down_part, c_planes, yin, yzin, columns, zin)))
+        [vmem(64, 128), vmem(64, 128)],
+        [VM] * 6,
+        [VM] * 2,
+    )(*(held(part) for part in (up_part, down_part, c_planes, yzin, columns, zin)))
     from_below = across(to_up, dx=1, dz=1)
     from_above = across(to_down, dx=-1, dz=1)
     whole = jax.ShapeDtypeStruct((3, ROWS, 128), F32)
-    e_out, h_out, e_edge, h_edge = kernel_call(
+    e_out, h_out, e_edge, h_edge, patched = kernel_call(
         advance,
-        [whole, whole, vmem(2, 3, 64, 128), vmem(2, 3, 64, 128)],
-        [VM] * 4,
-        [HBM, HBM, VM, VM],
+        [whole, whole, vmem(2, 3, 64, 128), vmem(2, 3, 64, 128), vmem(32, 128)],
+        [VM] * 8,
+        [HBM, HBM, VM, VM, VM],
         [pltpu.VMEM((3, EXT, 128), F32)] * 3 + [pltpu.VMEM((2, 320, 128), F32), dma((2,))],
-    )(*(held(part) for part in (e_ext, h_ext, c_ext, ptile)))
+        cost=pl.CostEstimate(flops=10**10, bytes_accessed=10**8, transcendentals=0),
+    )(*(held(part) for part in (e_ext, h_ext, c_ext, c_planes, yin, yzin, columns, zin)))
     e_out, h_out, _, _ = kernel_call(
         correct,
         [whole, whole, vmem(2, 3, 64, 128), vmem(2, 3, 64, 128)],

time: 14.5 us -> 14.1 us (0.972)
  waiting for transfers between devices: 2.44 us -> 0.6 us
  starting transfers between devices: 6.45 us -> 7.38 us
  Pallas kernels: 4.71 us -> 5.13 us
    ppermute x5 -> x6, waiting for transfers between devices: 2.44 us -> 0.6 us  [across(): return lax.ppermute(x, ('gx', 'gy', 'gz'), pairs)]
    ppermute x5 -> x6, starting transfers between devices: 6.45 us -> 7.38 us  [across(): return lax.ppermute(x, ('gx', 'gy', 'gz'), pairs)]
    pallas_call x2 -> x5, Pallas kernels: 1.8 us -> 2.24 us  [the longest x1 1.08 us: fast_shards(): kernel_call(peek, vmem(8, 128), [HBM] * 2, VM, [pltpu.VMEM((2, 3, 8, 128)...]
  transfers between devices with their start and end apart: 5 -> 6, of which waited for: 3 -> 2; matrix products, arithmetic and copies ran while one was open for 0% -> 0% of each run, Pallas kernels for 15% -> 24%
where the time goes in v3:
time: 14.1 us; the launch traced here: 13.8 us
  starting transfers between devices  7.38 us (52%)
  Pallas kernels  5.13 us (36%)
  between operations  0.72 us (5%)
  waiting for transfers between devices  0.6 us (4%)
    ppermute x6, starting transfers between devices, across(): return lax.ppermute(x, ('gx', 'gy', 'gz'), pairs)  7.38 us
    pallas_call x1, Pallas kernels, fast_shards(): kernel_call(advance, [whole, whole, vmem(2, 3, 64, 128), vmem(2, 3, 64, 1...  1.33 us
    pallas_call x1, Pallas kernels, fast_shards(): kernel_call(peek, vmem(8, 128), [HBM] * 2, VM, [pltpu.VMEM((2, 3, 8, 128)...  1.08 us
    pallas_call x1, Pallas kernels, fast_shards(): kernel_call(take_material, [vmem(HALO, 128, dtype=jnp.int32), vmem(2, 64,...  0.87 us
    pallas_call x1, Pallas kernels, fast_shards(): kernel_call(extend, [vmem(3, EXT, 128), vmem(3, EXT, 128), vmem(EXT, 128)...  0.78 us
    pallas_call x1, Pallas kernels, fast_shards(): kernel_call(correct, [whole, whole, vmem(2, 3, 64, 128), vmem(2, 3, 64, 1...  0.78 us
    ppermute x6, waiting for transfers between devices, across(): return lax.ppermute(x, ('gx', 'gy', 'gz'), pairs)  0.6 us
  transfers between devices with their start and end apart: 6, of which 2 were waited for; matrix products, arithmetic and copies ran while one was open for 0% of the time, Pallas kernels for 24%

profile of v3, /device:TPU:0, one launch (start us, length us, event | category | flops | bytes accessed | tf_op | source)
XLA Modules:
  0.0 13.8 jit_solution(11209150426779100772)
XLA Ops:
  0.6 0.0 copy-start.1
  0.6 0.0 copy-start
  0.6 0.0 copy-start.2
  0.7 1.1 %shard_map.59.after = f32[8,128]{1,0:T(8,128)S(1)} custom-call(f32[3,512,128]{2,1,0:T(8,128)} %bitcast.5, f32[3,512,128]{2,1,0:T(8,128)} %bitcast.8), custom_call_target="tpu_custom_call" | custom-call | tf_op jit(solution)/shard_map/pallas_call | solution.py:990
  1.7 0.5 %collective-permute-start = (f32[8,128]{1,0:T(8,128)S(1)}, f32[8,128]{1,0:T(8,128)S(1)}, u32[]{:S(2)}, u32[]{:S(2)}) collective-permute-start(f32[8,128]{1,0:T(8,128)S(1)} %shard_map.59.after), channel_id=1, source_target_pairs={{0,1},{1,0},{2,3},{3,2},{4,5},{5,4},{6,7},{7,6},{8,9},{9,8},{10,11... | collective-permute-start | bytes 12296 | tf_op jit(solution)/shard_map/ppermute | solution.py:982
  2.3 0.9 %shard_map.60 = (s32[128,128]{1,0:T(8,128)S(1)}, s32[2,64,128]{2,1,0:T(8,128)S(1)}) custom-call(s32[512,128]{1,0:T(8,128)} %bitcast.11, f32[8,128]{1,0:T(8,128)S(1)} %shard_map.59.after), custom_call_target="tpu_custom_call" | custom-call | tf_op jit(solution)/shard_map/pallas_call | solution.py:997
  3.1 0.0 copy-done.1
  3.2 0.0 copy-done
  3.2 0.2 %shard_map.61 = (f32[1088,128]{1,0:T(8,128)S(1)}, f32[8,128]{1,0:T(8,128)S(1)}, f32[192,128]{1,0:T(8,128)S(1)}) custom-call(f32[3,512,128]{2,1,0:T(8,128)S(1)} %bitcast.6, f32[3,512,128]{2,1,0:T(8,128)S(1)} %bitcast.9, s32[128,128]{1,0:T(8,128)S(1)} %get-tuple-element.26.m_face, s32[2,64,128]{2,1,0:T(8,128)S(1)} %get-tuple-element.27.m_ends), custom_call_target="tpu_custom_call" | custom-call | tf_op jit(solution)/shard_map/pallas_call | solution.py:1005
  3.4 0.0 collective-permute-done.edge_tile
  3.4 0.1 collective-permute-start.1
  3.5 1.9 %collective-permute-start.3 = (f32[8,128]{1,0:T(8,128)S(1)}, f32[8,128]{1,0:T(8,128)S(1)}, u32[]{:S(2)}, u32[]{:S(2)}) collective-permute-start(f32[8,128]{1,0:T(8,128)S(1)} %get-tuple-element.38), channel_id=1, source_target_pairs={{0,3},{1,2},{2,1},{3,0},{4,7},{5,6},{6,5},{7,4},{8,11},{9,10},{10,... | collective-permute-start | bytes 12296 | tf_op jit(solution)/shard_map/ppermute | solution.py:982
  5.4 0.2 %collective-permute-start.2 = (f32[8,128]{1,0:T(8,128)S(1)}, f32[8,128]{1,0:T(8,128)S(1)}, u32[]{:S(2)}, u32[]{:S(2)}) collective-permute-start(f32[8,128]{1,0:T(8,128)S(1)} %get-tuple-element.38), channel_id=1, source_target_pairs={{0,2},{1,3},{2,0},{3,1},{4,6},{5,7},{6,4},{7,5},{8,10},{9,11},{10,... | collective-permute-start | bytes 12296 | tf_op jit(solution)/shard_map/ppermute | solution.py:982
  5.6 0.0 collective-permute-done.1.zmsg.r_other
  5.6 0.0 copy-done.2
  5.6 0.8 %shard_map.63 = (f32[3,1296,128]{2,1,0:T(8,128)S(1)}, f32[3,1296,128]{2,1,0:T(8,128)S(1)}, f32[1296,128]{1,0:T(8,128)S(1)}, f32[96,128]{1,0:T(8,128)S(1)}, f32[9...) custom-call(f32[3,512,128]{2,1,0:T(8,128)S(1)} %bitcast.7, ...), custom_call_target="tpu_custom_call" | custom-call | tf_op jit(solution)/shard_map/pallas_call | solution.py:1021
  6.4 0.3 %collective-permute-done.3.yzin = f32[8,128]{1,0:T(8,128)S(1)} collective-permute-done((f32[8,128]{1,0:T(8,128)S(1)}, f32[8,128]{1,0:T(8,128)S(1)}, u32[]{:S(2)}, u32[]{:S(2)}) %collective-permute-start.3) | collective-permute-done | bytes 4128 | tf_op jit(solution)/shard_map/ppermute | solution.py:982
  6.7 0.1 shard_map.65
  6.8 2.6 %collective-permute-start.4 = (f32[64,128]{1,0:T(8,128)S(1)}, f32[64,128]{1,0:T(8,128)S(1)}, u32[]{:S(2)}, u32[]{:S(2)}) collective-permute-start(f32[64,128]{1,0:T(8,128)S(1)} %get-tuple-element.42), channel_id=1, source_target_pairs={{0,5},{1,4},{2,7},{3,6},{4,9},{5,8},{6,11},{7,10},{8,13},{9,12},{1... | collective-permute-start | bytes 98312 | tf_op jit(solution)/shard_map/ppermute | solution.py:982
  9.4 2.1 %collective-permute-start.5 = (f32[64,128]{1,0:T(8,128)S(1)}, f32[64,128]{1,0:T(8,128)S(1)}, u32[]{:S(2)}, u32[]{:S(2)}) collective-permute-start(f32[64,128]{1,0:T(8,128)S(1)} %get-tuple-element.43), channel_id=1, source_target_pairs={{0,13},{1,12},{2,15},{3,14},{4,1},{5,0},{6,3},{7,2},{8,5},{9,4},{1... | collective-permute-start | bytes 98312 | tf_op jit(solution)/shard_map/ppermute | solution.py:982
  11.4 0.0 collective-permute-done.2.yin
  11.4 1.3 %shard_map.64 = (f32[3,512,128]{2,1,0:T(8,128)}, f32[3,512,128]{2,1,0:T(8,128)}, f32[2,3,64,128]{3,2,1,0:T(8,128)S(1)}, f32[2,3,64,128]{3,2,1,0:T(8,128)S(1)}, f32[32,128]{1,0:T(8,128)S(1)}) custom-call(f32[3,1296,128]{2,1,0:T(8,128)S(1)} %get-tuple-element.35.e_ext, f32[3,1296,128]{2,1,0:T(8,128)S(1)} %get-tuple-element.36.h_ext, ...), custom_call_target="tpu_custom_call" | custom-call | flops 10000000000 | bytes 100000000 | tf_op jit(solution)/shard_map/pallas_call | solution.py:1046
  12.8 0.3 %collective-permute-done.4.from_below = f32[64,128]{1,0:T(8,128)S(1)} collective-permute-done((f32[64,128]{1,0:T(8,128)S(1)}, f32[64,128]{1,0:T(8,128)S(1)}, u32[]{:S(2)}, u32[]{:S(2)}) %collective-permute-start.4) | collective-permute-done | bytes 32800 | tf_op jit(solution)/shard_map/ppermute | solution.py:982
  13.1 0.0 collective-permute-done.5.from_above
  13.1 0.8 %shard_map.66 = (f32[3,512,128]{2,1,0:T(8,128)}, f32[3,512,128]{2,1,0:T(8,128)}, f32[2,3,64,128]{3,2,1,0:T(8,128)S(1)}, f32[2,3,64,128]{3,2,1,0:T(8,128)S(1)}) custom-call(f32[96,128]{1,0:T(8,128)S(1)} %get-tuple-element.32.up, f32[96,128]{1,0:T(8,128)S(1)} %get-tuple-element.33.down, ...), custom_call_target="tpu_custom_call", output_to_operand_aliasing={{0}: (8, {}), {1}: (9, {}), {2}: (6, {}), {3}: (7, {})} | custom-call | tf_op jit(solution)/shard_map/pallas_call | solution.py:1054
  (1 shorter events, 0.0 us)
Async XLA Ops:
  0.6 2.5 %copy-start.1 = (f32[1,1,1,3,65536]{4,2,3,1,0:T(1,128)S(1)}, f32[1,1,1,3,65536]{4,2,3,1,0:T(1,128)}, u32[]{:S(2)}) copy-start(f32[1,1,1,3,65536]{4,2,3,1,0:T(1,128)} %param.5) | copy-start | bytes 2359300
  0.6 2.5 %copy-start = (f32[1,1,1,3,65536]{4,2,3,1,0:T(1,128)S(1)}, f32[1,1,1,3,65536]{4,2,3,1,0:T(1,128)}, u32[]{:S(2)}) copy-start(f32[1,1,1,3,65536]{4,2,3,1,0:T(1,128)} %param.4) | copy-start | bytes 2359300
  0.6 5.0 %copy-start.2 = (s32[1,1,1,65536]{3,2,1,0:T(1,128)S(1)}, s32[1,1,1,65536]{3,2,1,0:T(1,128)}, u32[]{:S(2)}) copy-start(s32[1,1,1,65536]{3,2,1,0:T(1,128)} %param.6) | copy-start | bytes 786436
  1.7 1.6 %collective-permute-start = (f32[8,128]{1,0:T(8,128)S(1)}, f32[8,128]{1,0:T(8,128)S(1)}, u32[]{:S(2)}, u32[]{:S(2)}) collective-permute-start(f32[8,128]{1,0:T(8,128)S(1)} %shard_map.59.after), channel_id=1, source_target_pairs={{0,1},{1,0},{2,3},{3,2},{4,5},{5,4},{6,7},{7,6},{8,9},{9,8},{10,11... | collective-permute-start | bytes 12296 | tf_op jit(solution)/shard_map/ppermute | solution.py:982
  3.4 2.2 %collective-permute-start.1 = (f32[1088,128]{1,0:T(8,128)S(1)}, f32[1088,128]{1,0:T(8,128)S(1)}, u32[]{:S(2)}, u32[]{:S(2)}) collective-permute-start(f32[1088,128]{1,0:T(8,128)S(1)} %get-tuple-element.30), channel_id=1, source_target_pairs={{0,1},{1,0},{2,3},{3,2},{4,5},{5,4},{6,7},{7,6},{8,9},{9,8},{10,11... | collective-permute-start | bytes 1671176 | tf_op jit(solution)/shard_map/ppermute | solution.py:982
  3.5 3.2 %collective-permute-start.3 = (f32[8,128]{1,0:T(8,128)S(1)}, f32[8,128]{1,0:T(8,128)S(1)}, u32[]{:S(2)}, u32[]{:S(2)}) collective-permute-start(f32[8,128]{1,0:T(8,128)S(1)} %get-tuple-element.38), channel_id=1, source_target_pairs={{0,3},{1,2},{2,1},{3,0},{4,7},{5,6},{6,5},{7,4},{8,11},{9,10},{10,... | collective-permute-start | bytes 12296 | tf_op jit(solution)/shard_map/ppermute | solution.py:982
  5.4 6.1 %collective-permute-start.2 = (f32[8,128]{1,0:T(8,128)S(1)}, f32[8,128]{1,0:T(8,128)S(1)}, u32[]{:S(2)}, u32[]{:S(2)}) collective-permute-start(f32[8,128]{1,0:T(8,128)S(1)} %get-tuple-element.38), channel_id=1, source_target_pairs={{0,2},{1,3},{2,0},{3,1},{4,6},{5,7},{6,4},{7,5},{8,10},{9,11},{10,... | collective-permute-start | bytes 12296 | tf_op jit(solution)/shard_map/ppermute | solution.py:982
  6.8 6.3 %collective-permute-start.4 = (f32[64,128]{1,0:T(8,128)S(1)}, f32[64,128]{1,0:T(8,128)S(1)}, u32[]{:S(2)}, u32[]{:S(2)}) collective-permute-start(f32[64,128]{1,0:T(8,128)S(1)} %get-tuple-element.42), channel_id=1, source_target_pairs={{0,5},{1,4},{2,7},{3,6},{4,9},{5,8},{6,11},{7,10},{8,13},{9,12},{1... | collective-permute-start | bytes 98312 | tf_op jit(solution)/shard_map/ppermute | solution.py:982
  9.4 3.7 %collective-permute-start.5 = (f32[64,128]{1,0:T(8,128)S(1)}, f32[64,128]{1,0:T(8,128)S(1)}, u32[]{:S(2)}, u32[]{:S(2)}) collective-permute-start(f32[64,128]{1,0:T(8,128)S(1)} %get-tuple-element.43), channel_id=1, source_target_pairs={{0,13},{1,12},{2,15},{3,14},{4,1},{5,0},{6,3},{7,2},{8,5},{9,4},{1... | collective-permute-start | bytes 98312 | tf_op jit(solution)/shard_map/ppermute | solution.py:982

commit v4 on v3

--- a/solution.py
+++ b/solution.py
@@ -359,39 +359,52 @@
     return [view.at[:, pl.ds((grid.depth - 8) * end, 8), :] for end in range(2)]
 
 
-def peek(e_hbm, h_hbm, edge_tile, e_ends, h_ends, sems):
+def material_loads(grid, gz, m_hbm, m_face, m_ends, sems):
+    face = pl.ds((1 - gz) * (ROWS - HALO), HALO)
+    loads = [pltpu.make_async_copy(m_hbm.at[face], m_face, sems.at[0])]
+    for end, tiles in enumerate(edge_tiles(grid, m_hbm)):
+        place = m_ends.at[end].reshape(8, 8, 128).at[pl.ds(0, grid.own)]
+        loads.append(pltpu.make_async_copy(tiles, place, sems.at[1 + end]))
+    return loads
+
+
+def peek(e_hbm, h_hbm, m_hbm, edge_tile, m_face, m_ends, e_ends, h_ends, sems, m_sems):
     def body(grid, gz):
         if grid is Fine:
             edge_tile[...] = jnp.zeros((8, 128), F32)
             return
+        m_loads = material_loads(grid, gz, m_hbm, m_face, m_ends, m_sems)
         loads = []
         for end in range(2):
             rows = pl.ds((1 - gz) * (ROWS - HALO) + (HALO - 8) * end, 8)
-            loads.append(pltpu.make_async_copy(e_hbm.at[:, rows], e_ends.at[end], sems.at[2 * end]))
-            loads.append(pltpu.make_async_copy(h_hbm.at[:, rows], h_ends.at[end], sems.at[2 * end + 1]))
-        for load in loads:
+            place = pl.ds(0, 8)
+            loads.append(pltpu.make_async_copy(e_hbm.at[:, rows], e_ends.at[end, :, place], sems.at[2 * end]))
+            loads.append(pltpu.make_async_copy(h_hbm.at[:, rows], h_ends.at[end, :, place], sems.at[2 * end + 1]))
+        for load in loads + m_loads:
             load.start()
         for load in loads:
             load.wait()
         tile = jnp.zeros((8, 128), F32)
+        lane = lanes_of((8, 128))
         for end in range(2):
-            ex, ey, ez = (e_ends[end, comp] for comp in range(3))
-            hx, hz = h_ends[end, 0], h_ends[end, 2]
+            rows = pl.ds(0 if end else 3, 8)
+            ex, ey, ez = (e_ends[end, comp, rows, :] for comp in range(3))
+            hx, hz = h_ends[end, 0, rows, :], h_ends[end, 2, rows, :]
             for kind, value in enumerate((hx + 0.5 * ez, hz - 0.5 * ex, ey)):
-                value = value if end else roll_rows(value, -3)
-                tile = at_lane(tile, 127, 96 * end + 8 * kind + 3, value)
-        edge_tile[...] = jnp.where(gz == 1, roll_lanes(tile, 1), tile)
+                to = 96 * end + 8 * kind + 3 + gz
+                tile = jnp.where(lane == to, pltpu.roll(value, to + 1, 1), tile)
+        edge_tile[...] = tile
+        for load in m_loads:
+            load.wait()
 
     by_level(body)
 
 
-def take_material(m_hbm, after, m_face, m_ends, sems):
+def fine_material(m_hbm, face_in, ends_in, m_face, m_ends, sems):
     def body(grid, gz):
-        layer = pl.ds((1 - gz) * (ROWS - HALO), HALO)
-        loads = [pltpu.make_async_copy(m_hbm.at[layer], m_face, sems.at[0])]
-        for end, tiles in enumerate(edge_tiles(grid, m_hbm)):
-            place = m_ends.at[end].reshape(8, 8, 128).at[pl.ds(0, grid.own)]
-            loads.append(pltpu.make_async_copy(tiles, place, sems.at[1 + end]))
+        if grid is Coarse:
+            return
+        loads = material_loads(grid, gz, m_hbm, m_face, m_ends, sems)
         for load in loads:
             load.start()
         for load in loads:
@@ -446,7 +459,7 @@
     by_level(body)
 
 
-def join_z(ytile, edge_tile, z_in, joined, z_out):
+def join_z(ytile, edge_tile, joined):
     joined[...] = ytile[...] + edge_tile[...]
 
 
@@ -987,20 +1000,21 @@
     h = magnetic.reshape(3, ROWS, 128)
     m = material.reshape(ROWS, 128)
     dma = pltpu.SemaphoreType.DMA
-    edge_tile = kernel_call(
+    edge_tile, m_face, m_ends = kernel_call(
         peek,
-        vmem(8, 128),
-        [HBM] * 2,
-        VM,
-        [pltpu.VMEM((2, 3, 8, 128), F32)] * 2 + [dma((4,))],
-    )(far(e), far(h))
+        [vmem(8, 128), vmem(HALO, 128, dtype=jnp.int32), vmem(2, 64, 128, dtype=jnp.int32)],
+        [HBM] * 3,
+        [VM] * 3,
+        [pltpu.VMEM((2, 3, 16, 128), F32)] * 2 + [dma((4,)), dma((3,))],
+    )(far(e), far(h), far(m))
     m_face, m_ends = kernel_call(
-        take_material,
+        fine_material,
         [vmem(HALO, 128, dtype=jnp.int32), vmem(2, 64, 128, dtype=jnp.int32)],
-        [HBM, VM],
+        [HBM, VM, VM],
         [VM] * 2,
         [dma((3,))],
-    )(far(m), held(edge_tile))
+        aliases={1: 0, 2: 1},
+    )(far(m), held(m_face), held(m_ends))
     edge_tile = across(edge_tile, dz=1)
     zmsg, ytile, columns = kernel_call(
         gather,
@@ -1008,13 +1022,13 @@
         [VM] * 4,
         [VM] * 3,
     )(held(e), held(h), held(m_face), held(m_ends))
-    ytile, zmsg = kernel_call(
+    ytile = kernel_call(
         join_z,
-        [vmem(8, 128), vmem(FACE + COLUMNS, 128)],
-        [VM] * 3,
+        vmem(8, 128),
         [VM] * 2,
-        aliases={2: 1},
-    )(held(ytile), held(edge_tile), held(zmsg))
+        VM,
+        cost=pl.CostEstimate(flops=10**10, bytes_accessed=10**8, transcendentals=0),
+    )(held(ytile), held(edge_tile))
     zin = across(zmsg, dz=1)
     yin = across(ytile, dy=1)
     yzin = across(ytile, dy=1, dz=1)

time: 14.1 us -> 13.6 us (0.965)
  Pallas kernels: 5.13 us -> 4.28 us
  waiting for transfers between devices: 0.6 us -> 0.97 us
    pallas_call x3, Pallas kernels: 1.95 us -> 1.1 us  [the longest x1 1.07 us: fast_shards(): kernel_call(peek, [vmem(8, 128), vmem(HALO, 128, dtype=jnp.int32), vmem(2...]
    ppermute x6, waiting for transfers between devices: 0.6 us -> 0.97 us  [across(): return lax.ppermute(x, ('gx', 'gy', 'gz'), pairs)]
  transfers between devices with their start and end apart: 6 -> 6, of which waited for: 2 -> 3; matrix products, arithmetic and copies ran while one was open for 0% -> 0% of each run, Pallas kernels for 24% -> 18%
where the time goes in v4:
time: 13.6 us; the launch traced here: 13.4 us
  starting transfers between devices  7.41 us (54%)
  Pallas kernels  4.28 us (31%)
  waiting for transfers between devices  0.97 us (7%)
  between operations  0.7 us (5%)
    ppermute x6, starting transfers between devices, across(): return lax.ppermute(x, ('gx', 'gy', 'gz'), pairs)  7.41 us
    pallas_call x1, Pallas kernels, fast_shards(): kernel_call(advance, [whole, whole, vmem(2, 3, 64, 128), vmem(2, 3, 64, 1...  1.33 us
    pallas_call x1, Pallas kernels, fast_shards(): kernel_call(peek, [vmem(8, 128), vmem(HALO, 128, dtype=jnp.int32), vmem(2...  1.07 us
    ppermute x6, waiting for transfers between devices, across(): return lax.ppermute(x, ('gx', 'gy', 'gz'), pairs)  0.97 us
    pallas_call x1, Pallas kernels, fast_shards(): kernel_call(extend, [vmem(3, EXT, 128), vmem(3, EXT, 128), vmem(EXT, 128)...  0.78 us
    pallas_call x1, Pallas kernels, fast_shards(): kernel_call(correct, [whole, whole, vmem(2, 3, 64, 128), vmem(2, 3, 64, 1...  0.78 us
  transfers between devices with their start and end apart: 6, of which 3 were waited for; matrix products, arithmetic and copies ran while one was open for 0% of the time, Pallas kernels for 18%

profile of v4, /device:TPU:0, one launch (start us, length us, event | category | flops | bytes accessed | tf_op | source)
XLA Modules:
  0.0 13.4 jit_solution(1312855218887093897)
XLA Ops:
  0.6 0.0 copy-start.1
  0.6 0.0 copy-start
  0.6 1.1 %shard_map.59 = (f32[8,128]{1,0:T(8,128)S(1)}, s32[128,128]{1,0:T(8,128)S(1)}, s32[2,64,128]{2,1,0:T(8,128)S(1)}) custom-call(f32[3,512,128]{2,1,0:T(8,128)} %bitcast.5, f32[3,512,128]{2,1,0:T(8,128)} %bitcast.8, s32[512,128]{1,0:T(8,128)} %bitcast.11), custom_call_target="tpu_custom_call" | custom-call | tf_op jit(solution)/shard_map/pallas_call | solution.py:1003
  1.7 0.5 %collective-permute-start.1 = (f32[8,128]{1,0:T(8,128)S(1)}, f32[8,128]{1,0:T(8,128)S(1)}, u32[]{:S(2)}, u32[]{:S(2)}) collective-permute-start(f32[8,128]{1,0:T(8,128)S(1)} %get-tuple-element.40), channel_id=1, source_target_pairs={{0,1},{1,0},{2,3},{3,2},{4,5},{5,4},{6,7},{7,6},{8,9},{9,8},{10,11... | collective-permute-start | bytes 12296 | tf_op jit(solution)/shard_map/ppermute | solution.py:995
  2.3 0.0 copy-done.1
  2.3 0.0 copy-done
  2.3 0.2 %shard_map.61 = (f32[1088,128]{1,0:T(8,128)S(1)}, f32[8,128]{1,0:T(8,128)S(1)}, f32[192,128]{1,0:T(8,128)S(1)}) custom-call(f32[3,512,128]{2,1,0:T(8,128)S(1)} %bitcast.6, f32[3,512,128]{2,1,0:T(8,128)S(1)} %bitcast.9, s32[128,128]{1,0:T(8,128)S(1)} %get-tuple-element.29.m_face, s32[2,64,128]{2,1,0:T(8,128)S(1)} %get-tuple-element.30.m_ends), custom_call_target="tpu_custom_call" | custom-call | tf_op jit(solution)/shard_map/pallas_call | solution.py:1019
  2.5 0.3 %collective-permute-start = (f32[1088,128]{1,0:T(8,128)S(1)}, f32[1088,128]{1,0:T(8,128)S(1)}, u32[]{:S(2)}, u32[]{:S(2)}) collective-permute-start(f32[1088,128]{1,0:T(8,128)S(1)} %get-tuple-element.31), channel_id=1, source_target_pairs={{0,1},{1,0},{2,3},{3,2},{4,5},{5,4},{6,7},{7,6},{8,9},{9,8},{10,11... | collective-permute-start | bytes 1671176 | tf_op jit(solution)/shard_map/ppermute | solution.py:995
  2.8 0.3 %collective-permute-done.1.edge_tile = f32[8,128]{1,0:T(8,128)S(1)} collective-permute-done((f32[8,128]{1,0:T(8,128)S(1)}, f32[8,128]{1,0:T(8,128)S(1)}, u32[]{:S(2)}, u32[]{:S(2)}) %collective-permute-start.1) | collective-permute-done | bytes 4128 | tf_op jit(solution)/shard_map/ppermute | solution.py:995
  3.1 0.0 copy-start.2
  3.1 2.4 %collective-permute-start.3 = (f32[8,128]{1,0:T(8,128)S(1)}, f32[8,128]{1,0:T(8,128)S(1)}, u32[]{:S(2)}, u32[]{:S(2)}) collective-permute-start(f32[8,128]{1,0:T(8,128)S(1)} %shard_map.63), channel_id=1, source_target_pairs={{0,3},{1,2},{2,1},{3,0},{4,7},{5,6},{6,5},{7,4},{8,11},{9,10},{10,... | collective-permute-start | bytes 12296 | tf_op jit(solution)/shard_map/ppermute | solution.py:995
  5.4 0.1 collective-permute-start.2
  5.6 0.0 collective-permute-done.zmsg.r_other
  5.6 0.0 copy-done.2
  5.6 0.8 %shard_map.62 = (f32[3,1296,128]{2,1,0:T(8,128)S(1)}, f32[3,1296,128]{2,1,0:T(8,128)S(1)}, f32[1296,128]{1,0:T(8,128)S(1)}, f32[96,128]{1,0:T(8,128)S(1)}, f32[9...) custom-call(f32[3,512,128]{2,1,0:T(8,128)S(1)} %bitcast.7, ...), custom_call_target="tpu_custom_call" | custom-call | tf_op jit(solution)/shard_map/pallas_call | solution.py:1035
  6.4 0.4 %collective-permute-done.3.yzin = f32[8,128]{1,0:T(8,128)S(1)} collective-permute-done((f32[8,128]{1,0:T(8,128)S(1)}, f32[8,128]{1,0:T(8,128)S(1)}, u32[]{:S(2)}, u32[]{:S(2)}) %collective-permute-start.3) | collective-permute-done | bytes 4128 | tf_op jit(solution)/shard_map/ppermute | solution.py:995
  6.8 0.1 shard_map.65
  6.8 2.0 %collective-permute-start.4 = (f32[64,128]{1,0:T(8,128)S(1)}, f32[64,128]{1,0:T(8,128)S(1)}, u32[]{:S(2)}, u32[]{:S(2)}) collective-permute-start(f32[64,128]{1,0:T(8,128)S(1)} %get-tuple-element.44), channel_id=1, source_target_pairs={{0,5},{1,4},{2,7},{3,6},{4,9},{5,8},{6,11},{7,10},{8,13},{9,12},{1... | collective-permute-start | bytes 98312 | tf_op jit(solution)/shard_map/ppermute | solution.py:995
  8.9 2.1 %collective-permute-start.5 = (f32[64,128]{1,0:T(8,128)S(1)}, f32[64,128]{1,0:T(8,128)S(1)}, u32[]{:S(2)}, u32[]{:S(2)}) collective-permute-start(f32[64,128]{1,0:T(8,128)S(1)} %get-tuple-element.45), channel_id=1, source_target_pairs={{0,13},{1,12},{2,15},{3,14},{4,1},{5,0},{6,3},{7,2},{8,5},{9,4},{1... | collective-permute-start | bytes 98312 | tf_op jit(solution)/shard_map/ppermute | solution.py:995
  11.0 0.0 collective-permute-done.2.yin
  11.0 1.3 %shard_map.64 = (f32[3,512,128]{2,1,0:T(8,128)}, f32[3,512,128]{2,1,0:T(8,128)}, f32[2,3,64,128]{3,2,1,0:T(8,128)S(1)}, f32[2,3,64,128]{3,2,1,0:T(8,128)S(1)}, f32[32,128]{1,0:T(8,128)S(1)}) custom-call(f32[3,1296,128]{2,1,0:T(8,128)S(1)} %get-tuple-element.36.e_ext, f32[3,1296,128]{2,1,0:T(8,128)S(1)} %get-tuple-element.37.h_ext, ...), custom_call_target="tpu_custom_call" | custom-call | flops 10000000000 | bytes 100000000 | tf_op jit(solution)/shard_map/pallas_call | solution.py:1060
  12.3 0.3 %collective-permute-done.4.from_below = f32[64,128]{1,0:T(8,128)S(1)} collective-permute-done((f32[64,128]{1,0:T(8,128)S(1)}, f32[64,128]{1,0:T(8,128)S(1)}, u32[]{:S(2)}, u32[]{:S(2)}) %collective-permute-start.4) | collective-permute-done | bytes 32800 | tf_op jit(solution)/shard_map/ppermute | solution.py:995
  12.6 0.0 collective-permute-done.5.from_above
  12.6 0.8 %shard_map.66 = (f32[3,512,128]{2,1,0:T(8,128)}, f32[3,512,128]{2,1,0:T(8,128)}, f32[2,3,64,128]{3,2,1,0:T(8,128)S(1)}, f32[2,3,64,128]{3,2,1,0:T(8,128)S(1)}) custom-call(f32[96,128]{1,0:T(8,128)S(1)} %get-tuple-element.33.up, f32[96,128]{1,0:T(8,128)S(1)} %get-tuple-element.34.down, ...), custom_call_target="tpu_custom_call", output_to_operand_aliasing={{0}: (8, {}), {1}: (9, {}), {2}: (6, {}), {3}: (7, {})} | custom-call | tf_op jit(solution)/shard_map/pallas_call | solution.py:1068
  (2 shorter events, 0.0 us)
Async XLA Ops:
  0.6 1.7 %copy-start.1 = (f32[1,1,1,3,65536]{4,2,3,1,0:T(1,128)S(1)}, f32[1,1,1,3,65536]{4,2,3,1,0:T(1,128)}, u32[]{:S(2)}) copy-start(f32[1,1,1,3,65536]{4,2,3,1,0:T(1,128)} %param.5) | copy-start | bytes 2359300
  0.6 1.7 %copy-start = (f32[1,1,1,3,65536]{4,2,3,1,0:T(1,128)S(1)}, f32[1,1,1,3,65536]{4,2,3,1,0:T(1,128)}, u32[]{:S(2)}) copy-start(f32[1,1,1,3,65536]{4,2,3,1,0:T(1,128)} %param.4) | copy-start | bytes 2359300
  1.7 1.3 %collective-permute-start.1 = (f32[8,128]{1,0:T(8,128)S(1)}, f32[8,128]{1,0:T(8,128)S(1)}, u32[]{:S(2)}, u32[]{:S(2)}) collective-permute-start(f32[8,128]{1,0:T(8,128)S(1)} %get-tuple-element.40), channel_id=1, source_target_pairs={{0,1},{1,0},{2,3},{3,2},{4,5},{5,4},{6,7},{7,6},{8,9},{9,8},{10,11... | collective-permute-start | bytes 12296 | tf_op jit(solution)/shard_map/ppermute | solution.py:995
  2.5 3.0 %collective-permute-start = (f32[1088,128]{1,0:T(8,128)S(1)}, f32[1088,128]{1,0:T(8,128)S(1)}, u32[]{:S(2)}, u32[]{:S(2)}) collective-permute-start(f32[1088,128]{1,0:T(8,128)S(1)} %get-tuple-element.31), channel_id=1, source_target_pairs={{0,1},{1,0},{2,3},{3,2},{4,5},{5,4},{6,7},{7,6},{8,9},{9,8},{10,11... | collective-permute-start | bytes 1671176 | tf_op jit(solution)/shard_map/ppermute | solution.py:995
  3.1 2.5 %copy-start.2 = (s32[1,1,1,65536]{3,2,1,0:T(1,128)S(1)}, s32[1,1,1,65536]{3,2,1,0:T(1,128)}, u32[]{:S(2)}) copy-start(s32[1,1,1,65536]{3,2,1,0:T(1,128)} %param.6) | copy-start | bytes 786436
  3.1 3.7 %collective-permute-start.3 = (f32[8,128]{1,0:T(8,128)S(1)}, f32[8,128]{1,0:T(8,128)S(1)}, u32[]{:S(2)}, u32[]{:S(2)}) collective-permute-start(f32[8,128]{1,0:T(8,128)S(1)} %shard_map.63), channel_id=1, source_target_pairs={{0,3},{1,2},{2,1},{3,0},{4,7},{5,6},{6,5},{7,4},{8,11},{9,10},{10,... | collective-permute-start | bytes 12296 | tf_op jit(solution)/shard_map/ppermute | solution.py:995
  5.4 5.5 %collective-permute-start.2 = (f32[8,128]{1,0:T(8,128)S(1)}, f32[8,128]{1,0:T(8,128)S(1)}, u32[]{:S(2)}, u32[]{:S(2)}) collective-permute-start(f32[8,128]{1,0:T(8,128)S(1)} %shard_map.63), channel_id=1, source_target_pairs={{0,2},{1,3},{2,0},{3,1},{4,6},{5,7},{6,4},{7,5},{8,10},{9,11},{10,... | collective-permute-start | bytes 12296 | tf_op jit(solution)/shard_map/ppermute | solution.py:995
  6.8 5.7 %collective-permute-start.4 = (f32[64,128]{1,0:T(8,128)S(1)}, f32[64,128]{1,0:T(8,128)S(1)}, u32[]{:S(2)}, u32[]{:S(2)}) collective-permute-start(f32[64,128]{1,0:T(8,128)S(1)} %get-tuple-element.44), channel_id=1, source_target_pairs={{0,5},{1,4},{2,7},{3,6},{4,9},{5,8},{6,11},{7,10},{8,13},{9,12},{1... | collective-permute-start | bytes 98312 | tf_op jit(solution)/shard_map/ppermute | solution.py:995
  8.9 3.7 %collective-permute-start.5 = (f32[64,128]{1,0:T(8,128)S(1)}, f32[64,128]{1,0:T(8,128)S(1)}, u32[]{:S(2)}, u32[]{:S(2)}) collective-permute-start(f32[64,128]{1,0:T(8,128)S(1)} %get-tuple-element.45), channel_id=1, source_target_pairs={{0,13},{1,12},{2,15},{3,14},{4,1},{5,0},{6,3},{7,2},{8,5},{9,4},{1... | collective-permute-start | bytes 98312 | tf_op jit(solution)/shard_map/ppermute | solution.py:995

commit v5 on v4

--- a/solution.py
+++ b/solution.py
@@ -228,6 +228,7 @@
 VM = pl.BlockSpec(memory_space=pltpu.VMEM)
 HBM = pl.BlockSpec(memory_space=pltpu.HBM)
 CHUNK = 32
+SKEW = 2
 
 
 class Fine:
@@ -598,28 +599,37 @@
     ]
 
 
-def sent_rows(plane, gz):
-    return jnp.where(gz == 0, roll_rows(plane, -6), plane)[:10]
-
-
-def write_message(grid, ref, columns, gz):
+MESSAGE = 48
+UP = {Fine: [(9, 7)] * 5, Coarse: [(4, 4)] * 2}
+DOWN = {Fine: [(10, 6)] + [(9, 7)] * 4, Coarse: [(5, 3)] * 2}
+
+
+def sent_rows(plane, entry, gz):
+    count, begin = entry
+    return jnp.where(gz == 0, roll_rows(plane, -begin), plane)[:count]
+
+
+def places(grid, entries):
     row = 0
-    for col in columns:
-        for p in col:
-            rows = p if grid is Coarse else sent_rows(p, gz)
-            ref[pl.ds(row, rows.shape[0]), :] = rows
-            row += rows.shape[0]
-
-
-def read_message(grid, ref, count, gz):
-    if grid is Coarse:
-        return read_planes(grid, ref, *range(count))
-    planes = []
-    for i in range(count):
-        start = min(10 * i, ref.shape[0] - 16)
-        p = ref[pl.ds(start, 16), :]
-        planes.append([pltpu.roll(p, 16 + start - 10 * i + 6 * gz, 0)])
-    return planes
+    for entry in entries:
+        for _ in range(grid.parts):
+            yield row, entry
+            row += entry[0]
+
+
+def write_message(grid, ref, entries, columns, gz):
+    planes = [p for col in columns for p in col]
+    for (row, entry), p in zip(places(grid, entries), planes, strict=True):
+        ref[pl.ds(row, entry[0]), :] = sent_rows(p, entry, gz)
+
+
+def read_message(grid, ref, entries, gz):
+    height, planes = 2 * grid.own, []
+    for row, (_, begin) in places(grid, entries):
+        start = min(row, MESSAGE - height)
+        p = ref[pl.ds(start, height), :]
+        planes.append(pltpu.roll(p, height + start - row + begin * gz, 0))
+    return [planes[i : i + grid.parts] for i in range(0, len(planes), grid.parts)]
 
 
 def extend(
@@ -698,7 +708,7 @@
             ex, ey, ez = (e[31, comp] for comp in range(3))
             hy = sub(h[31, 1], scale(0.5, add(plus_z(ex), ez)))
             hz = add(h[31, 2], scale(0.5, add(ey, plus_y(ex))))
-            sent_up, sent_down = [hy, hz], [e[0, 1], e[0, 2]]
+            sent_up, sent_down = [hy, hz], [e[0, 2], e[0, 1]]
         else:
             ex, ey, ez = (e[0, comp] for comp in range(3))
             hx = sub(h[0, 0], scale(0.5, sub(plus_y(ez), plus_z(ey))))
@@ -706,7 +716,7 @@
             hz = sub(h[0, 2], scale(0.5, sub(sub(e[1, 1], ey), plus_y(ex))))
             ey_next = add(ey, mul(c[0], sub(minus_z(hx), hz)))
             ez_next = add(ez, mul(c[0], sub(hy, minus_y(hx))))
-            sent_down = [ey, ez, ey_next, ez_next, c[0]]
+            sent_down = [ez, ey, ey_next, ez_next, c[0]]
             ex, ey, ez = (e[62, comp] for comp in range(3))
             hy62 = sub(h[62, 1], scale(0.5, sub(plus_z(ex), sub(e[63, 2], ez))))
             hz62 = sub(h[62, 2], scale(0.5, sub(sub(e[63, 1], ey), plus_y(ex))))
@@ -717,11 +727,13 @@
             ex_next = add(ex, mul(c[63], sub(minus_y(hz), minus_z(hy))))
             ey_next = add(ey, mul(c[63], sub(minus_z(hx), sub(hz, hz62))))
             ez_next = add(ez, mul(c[63], sub(sub(hy, hy62), minus_y(hx))))
-            sent_up = [hy, hz, ex_next, ey_next, ez_next, c[63]]
+            next_y = sub(hy, scale(0.5, add(plus_z(ex_next), ez_next)))
+            next_z = add(hz, scale(0.5, add(ey_next, plus_y(ex_next))))
+            sent_up = [hy, hz, next_y, next_z, c[63]]
         write_planes(up, sent_up)
         write_planes(down, sent_down)
-        write_message(grid, to_up, sent_up, gz)
-        write_message(grid, to_down, sent_down, gz)
+        write_message(grid, to_up, UP[grid], sent_up, gz)
+        write_message(grid, to_down, DOWN[grid], sent_down, gz)
 
     by_level(body)
 
@@ -739,27 +751,29 @@
 
 def join_y(up_in, down_in, c_planes, yzin, r_own, r_other, to_up, to_down):
     def body(grid, gz):
+        def patch(ref, entries, index, value):
+            row, entry = list(places(grid, entries))[index]
+            rows = pl.ds(row, entry[0])
+            ref[rows, :] = ref[rows, :] + sent_rows(value, entry, gz)
+
         top = yzin[...]
         to_up[...] = up_in[...]
         to_down[...] = down_in[...]
         shape = (2 * grid.own, 128)
         if grid is Coarse:
-            rows = pl.ds(8 * 7, 8)
             change = jnp.where(lanes_of(shape) == 127, 0.5 * column_of(top, 3, 7, 0, grid), 0.0)
-            to_up[rows, :] = to_up[rows, :] + change
+            patch(to_up, UP[grid], 7, change)
             return
         plane = between(top, r_own[pl.ds(R_ROW, 8), :] + r_other[pl.ds(FACE + R_ROW, 8), :])
         bottom = lanes_of(shape) == 0
         (c0,), (c63,) = read_planes(grid, c_planes, 0, 3)
 
-        def change(ref, index, value):
-            rows = pl.ds(10 * index, 10)
-            ref[rows, :] = ref[rows, :] + sent_rows(value, gz)
-
-        change(to_down, 3, jnp.where(bottom, c0 * column_of(plane, 0, 0, 0, grid), 0.0))
-        change(to_up, 4, jnp.where(bottom, c63 * column_of(plane, 3, 7, 0, grid), 0.0))
-        change(to_up, 2, jnp.where(bottom, -c63 * column_of(plane, 3, 7, 8, grid), 0.0))
-        to_down[pl.ds(50, 10), :] = sent_rows(column_of(top, 0, 0, 16, grid), gz)
+        patch(to_down, DOWN[grid], 3, jnp.where(bottom, c0 * column_of(plane, 0, 0, 0, grid), 0.0))
+        ez_change = jnp.where(bottom, c63 * column_of(plane, 3, 7, 0, grid), 0.0)
+        ex_change = jnp.where(bottom, -c63 * column_of(plane, 3, 7, 8, grid), 0.0)
+        patch(to_up, UP[grid], 2, -0.5 * (plus_z([ex_change])[0] + ez_change))
+        patch(to_up, UP[grid], 3, -0.5 * ex_change)
+        to_down[pl.ds(MESSAGE - 1, 1), :] = top[:1]
 
     by_level(body)
 
@@ -830,15 +844,33 @@
 
                 return of
 
-            for layer in range(grid.count):
-                row = grid.stride * (layer + 1)
-                half_e(grid, h_ext, e_ext, e_mid, c_ext, row, ghosts(layer))
-            for layer in range(grid.count):
-                row = grid.stride * (layer + 1)
-                half_h(grid, e_mid, lambda comp, rows: h_ext[comp, rows, :], row, h_mid, row)
-            h_write = write(h_mid, h_out, sems.at[0])
-            h_write.start()
-            e_begin = e_mid
+            def own_write(source, target, sem, layer):
+                def start():
+                    rows = pl.ds(layer_row(grid, layer), grid.depth)
+                    to = block_layers(grid, target).at[:, layer - first]
+                    pltpu.make_async_copy(source.at[:, rows], to, sem).start()
+
+                if 2 <= layer < 8:
+                    start()
+                else:
+                    pl.when((layer < 8) == (gz == 0))(start)
+
+            def h1(comp, rows):
+                return h_ext[comp, rows, :]
+
+            for step in range(grid.count + 2 * SKEW):
+                if step < grid.count:
+                    half_e(grid, h_ext, e_ext, e_mid, c_ext, grid.stride * (step + 1), ghosts(step))
+                layer = step - SKEW
+                if 0 <= layer < grid.count:
+                    row = grid.stride * (layer + 1)
+                    half_h(grid, e_mid, h1, row, h_mid, row)
+                    own_write(h_mid, h_out, sems.at[0], layer)
+                layer = step - 2 * SKEW
+                if 0 <= layer < grid.count:
+                    row = grid.stride * (layer + 1)
+                    half_e(grid, h_mid, e_mid, e_last, c_ext, row, ghosts(layer))
+                    own_write(e_last, e_out, sems.at[1], layer)
         else:
             for comp in range(3):
                 for layer in range(grid.count):
@@ -852,20 +884,14 @@
                     rz = roll_lanes(tile, 127 - (32 * block + 8 + layer))
                     h_mid[0, rows, :] = h_mid[0, rows, :] - jnp.where(lane == 127, 0.5 * rz, 0.0)
                     h_mid[2, rows, :] = h_mid[2, rows, :] + jnp.where(lane == 127, 0.5 * rx, 0.0)
-            h_write = write(h_mid, h_out, sems.at[0])
-            h_write.start()
-            e_begin = e_ext
-
-            def ghosts(index):
-                return lambda start: (0.0, 0.0)
-
-        for layer in range(grid.own):
-            row = layer_row(grid, first + layer)
-            half_e(grid, h_mid, e_begin, e_last, c_ext, row, ghosts(first + layer))
-            write(e_last, e_out, sems.at[1], layer).start()
+            write(h_mid, h_out, sems.at[0]).start()
+            for layer in range(grid.own):
+                row = layer_row(grid, first + layer)
+                half_e(grid, h_mid, e_ext, e_last, c_ext, row, lambda start: (0.0, 0.0))
+                write(e_last, e_out, sems.at[1], layer).start()
         keep_edges(h_mid, h_edge)
         keep_edges(e_last, e_edge)
-        h_write.wait()
+        write(h_mid, h_out, sems.at[0]).wait()
         write(e_last, e_out, sems.at[1]).wait()
 
     by_level(body)
@@ -909,10 +935,11 @@
 
         if grid is Fine:
             zero = [jnp.zeros((16, 128), F32)]
-            ey64, ez64, ey64_part, ez64_part, c64, ey_top = read_message(grid, from_above, 6, gz)
+            ez64, ey64, ey64_part, ez64_part, c64 = read_message(grid, from_above, DOWN[grid], gz)
+            ey_top = column_of(from_above[pl.ds(MESSAGE - 8, 8), :], 0, 7, 16, grid)
             hy63, hz63 = read_planes(grid, up, 0, 1)
             c0, c1, c62, c63 = read_planes(grid, c_planes, *range(4))
-            ghost = -0.5 * ey_top[0]
+            ghost = -0.5 * ey_top
             dhy, dhz = scale(0.5, ez64), scale(-0.5, ey64)
             dex = mul(c63, sub(minus_y(dhz, ghost), minus_z(dhy)))
             dey = scale(-1.0, mul(c63, dhz))
@@ -938,22 +965,22 @@
             put(e_tile, 1, 2, 62, mul(c62, dhy62))
             copies = finish(1)
 
-            hy_part, hz_part, ex_part, ey_part, ez_part, cm = read_message(grid, from_below, 6, gz)
-            ey0, ez0, ey0_part, ez0_part = read_planes(grid, down, *range(4))
+            hy_part, hz_part, next_y, next_z, cm = read_message(grid, from_below, UP[grid], gz)
+            ez0, ey0, ey0_part, ez0_part = read_planes(grid, down, *range(4))
             ez0_change, ey_top = read_planes(grid, patched, 0, 1)
             ez0_part = add(ez0_part, ez0_change)
             ghost = -0.5 * ey_top[0]
             dhy, dhz = scale(0.5, ez0), scale(-0.5, ey0)
             hym, hzm = add(hy_part, dhy), add(hz_part, dhz)
-            exm = add(ex_part, mul(cm, sub(minus_y(dhz, ghost), minus_z(dhy))))
-            eym = sub(ey_part, mul(cm, dhz))
-            ezm = add(ez_part, mul(cm, dhy))
+            dexm = mul(cm, sub(minus_y(dhz, ghost), minus_z(dhy)))
             dey, dez = mul(c0, hzm), scale(-1.0, mul(c0, hym))
             dhx2 = scale(-0.5, sub(plus_y(dez), plus_z(dey)))
             dhy2 = scale(-0.5, dez)
             dhz2 = scale(0.5, dey)
-            hym2 = add(hym, scale(-0.5, sub(plus_z(exm), sub(add(ez0_part, dez), ezm))))
-            hzm2 = add(hzm, scale(-0.5, sub(sub(add(ey0_part, dey), eym), plus_y(exm))))
+            change = sub(sub(add(ez0_part, dez), plus_z(dexm)), mul(cm, dhy))
+            hym2 = add(add(next_y, dhy), scale(0.5, change))
+            change = sub(sub(plus_y(dexm), add(ey0_part, dey)), mul(cm, dhz))
+            hzm2 = add(add(next_z, dhz), scale(0.5, change))
             put(h_tile, 0, 0, 0, dhx2)
             put(h_tile, 0, 1, 0, dhy2)
             put(h_tile, 0, 2, 0, dhz2)
@@ -964,7 +991,7 @@
             put(e_tile, 0, 2, 1, scale(-1.0, mul(c1, dhy2)))
             copies += finish(0)
         else:
-            ey32, ez32 = read_message(grid, from_above, 2, gz)
+            ez32, ey32 = read_message(grid, from_above, DOWN[grid], gz)
             c0, c31 = read_planes(grid, c_planes, 0, 1)
             dhy, dhz = scale(0.5, ez32), scale(-0.5, ey32)
             put(h_tile, 1, 1, last, dhy)
@@ -973,8 +1000,8 @@
             put(e_tile, 1, 1, last, scale(-1.0, mul(c31, dhz)))
             put(e_tile, 1, 2, last, mul(c31, dhy))
             copies = finish(1)
-            hy_part, hz_part = read_message(grid, from_below, 2, gz)
-            ey0, ez0 = read_planes(grid, down, 0, 1)
+            hy_part, hz_part = read_message(grid, from_below, UP[grid], gz)
+            ez0, ey0 = read_planes(grid, down, 0, 1)
             put(e_tile, 0, 1, 0, mul(c0, add(hz_part, scale(-0.5, ey0))))
             put(e_tile, 0, 2, 0, scale(-1.0, mul(c0, add(hy_part, scale(0.5, ez0)))))
             copies += finish(0)
@@ -1040,8 +1067,8 @@
             vmem(EXT, 128),
             vmem(96, 128),
             vmem(96, 128),
-            vmem(64, 128),
-            vmem(64, 128),
+            vmem(MESSAGE, 128),
+            vmem(MESSAGE, 128),
             vmem(64, 128),
         ],
         [VM] * 4 + [HBM, VM],
@@ -1050,7 +1077,7 @@
     )(held(e), held(h), held(m), held(zin), far(permittivity), held(columns))
     to_up, to_down = kernel_call(
         join_y,
-        [vmem(64, 128), vmem(64, 128)],
+        [vmem(MESSAGE, 128), vmem(MESSAGE, 128)],
         [VM] * 6,
         [VM] * 2,
     )(*(held(part) for part in (up_part, down_part, c_planes, yzin, columns, zin)))

time: 13.6 us -> 13.4 us (0.985)
  transfers between devices with their start and end apart: 6 -> 6, of which waited for: 3 -> 4; matrix products, arithmetic and copies ran while one was open for 0% -> 0% of each run, Pallas kernels for 18% -> 18%
where the time goes in v5:
time: 13.4 us; the launch traced here: 13.3 us
  starting transfers between devices  7.41 us (55%)
  Pallas kernels  4.29 us (32%)
  waiting for transfers between devices  0.85 us (6%)
  between operations  0.7 us (5%)
    ppermute x6, starting transfers between devices, across(): return lax.ppermute(x, ('gx', 'gy', 'gz'), pairs)  7.41 us
    pallas_call x1, Pallas kernels, fast_shards(): kernel_call(advance, [whole, whole, vmem(2, 3, 64, 128), vmem(2, 3, 64, 1...  1.33 us
    pallas_call x1, Pallas kernels, fast_shards(): kernel_call(peek, [vmem(8, 128), vmem(HALO, 128, dtype=jnp.int32), vmem(2...  1.07 us
    ppermute x6, waiting for transfers between devices, across(): return lax.ppermute(x, ('gx', 'gy', 'gz'), pairs)  0.85 us
    pallas_call x1, Pallas kernels, fast_shards(): kernel_call(extend, [vmem(3, EXT, 128), vmem(3, EXT, 128), vmem(EXT, 128)...  0.79 us
    pallas_call x1, Pallas kernels, fast_shards(): kernel_call(correct, [whole, whole, vmem(2, 3, 64, 128), vmem(2, 3, 64, 1...  0.78 us
  transfers between devices with their start and end apart: 6, of which 4 were waited for; matrix products, arithmetic and copies ran while one was open for 0% of the time, Pallas kernels for 18%

profile of v5, /device:TPU:0, one launch (start us, length us, event | category | flops | bytes accessed | tf_op | source)
XLA Modules:
  0.0 13.3 jit_solution(10290276022200399760)
XLA Ops:
  0.6 0.0 copy-start.1
  0.6 0.0 copy-start
  0.6 1.1 %shard_map.59 = (f32[8,128]{1,0:T(8,128)S(1)}, s32[128,128]{1,0:T(8,128)S(1)}, s32[2,64,128]{2,1,0:T(8,128)S(1)}) custom-call(f32[3,512,128]{2,1,0:T(8,128)} %bitcast.5, f32[3,512,128]{2,1,0:T(8,128)} %bitcast.8, s32[512,128]{1,0:T(8,128)} %bitcast.11), custom_call_target="tpu_custom_call" | custom-call | tf_op jit(solution)/shard_map/pallas_call | solution.py:1030
  1.7 0.5 %collective-permute-start.1 = (f32[8,128]{1,0:T(8,128)S(1)}, f32[8,128]{1,0:T(8,128)S(1)}, u32[]{:S(2)}, u32[]{:S(2)}) collective-permute-start(f32[8,128]{1,0:T(8,128)S(1)} %get-tuple-element.40), channel_id=1, source_target_pairs={{0,1},{1,0},{2,3},{3,2},{4,5},{5,4},{6,7},{7,6},{8,9},{9,8},{10,11... | collective-permute-start | bytes 12296 | tf_op jit(solution)/shard_map/ppermute | solution.py:1022
  2.3 0.0 copy-done.1
  2.3 0.0 copy-done
  2.3 0.2 %shard_map.61 = (f32[1088,128]{1,0:T(8,128)S(1)}, f32[8,128]{1,0:T(8,128)S(1)}, f32[192,128]{1,0:T(8,128)S(1)}) custom-call(f32[3,512,128]{2,1,0:T(8,128)S(1)} %bitcast.6, f32[3,512,128]{2,1,0:T(8,128)S(1)} %bitcast.9, s32[128,128]{1,0:T(8,128)S(1)} %get-tuple-element.29.m_face, s32[2,64,128]{2,1,0:T(8,128)S(1)} %get-tuple-element.30.m_ends), custom_call_target="tpu_custom_call" | custom-call | tf_op jit(solution)/shard_map/pallas_call | solution.py:1046
  2.5 0.3 %collective-permute-start = (f32[1088,128]{1,0:T(8,128)S(1)}, f32[1088,128]{1,0:T(8,128)S(1)}, u32[]{:S(2)}, u32[]{:S(2)}) collective-permute-start(f32[1088,128]{1,0:T(8,128)S(1)} %get-tuple-element.31), channel_id=1, source_target_pairs={{0,1},{1,0},{2,3},{3,2},{4,5},{5,4},{6,7},{7,6},{8,9},{9,8},{10,11... | collective-permute-start | bytes 1671176 | tf_op jit(solution)/shard_map/ppermute | solution.py:1022
  2.8 0.3 %collective-permute-done.1.edge_tile = f32[8,128]{1,0:T(8,128)S(1)} collective-permute-done((f32[8,128]{1,0:T(8,128)S(1)}, f32[8,128]{1,0:T(8,128)S(1)}, u32[]{:S(2)}, u32[]{:S(2)}) %collective-permute-start.1) | collective-permute-done | bytes 4128 | tf_op jit(solution)/shard_map/ppermute | solution.py:1022
  3.1 0.0 copy-start.2
  3.1 2.4 %collective-permute-start.3 = (f32[8,128]{1,0:T(8,128)S(1)}, f32[8,128]{1,0:T(8,128)S(1)}, u32[]{:S(2)}, u32[]{:S(2)}) collective-permute-start(f32[8,128]{1,0:T(8,128)S(1)} %shard_map.63), channel_id=1, source_target_pairs={{0,3},{1,2},{2,1},{3,0},{4,7},{5,6},{6,5},{7,4},{8,11},{9,10},{10,... | collective-permute-start | bytes 12296 | tf_op jit(solution)/shard_map/ppermute | solution.py:1022
  5.4 0.1 collective-permute-start.2
  5.6 0.0 collective-permute-done.zmsg.r_other
  5.6 0.0 copy-done.2
  5.6 0.8 %shard_map.62 = (f32[3,1296,128]{2,1,0:T(8,128)S(1)}, f32[3,1296,128]{2,1,0:T(8,128)S(1)}, f32[1296,128]{1,0:T(8,128)S(1)}, f32[96,128]{1,0:T(8,128)S(1)}, f32[9...) custom-call(f32[3,512,128]{2,1,0:T(8,128)S(1)} %bitcast.7, ...), custom_call_target="tpu_custom_call" | custom-call | tf_op jit(solution)/shard_map/pallas_call | solution.py:1062
  6.4 0.4 %collective-permute-done.3.yzin = f32[8,128]{1,0:T(8,128)S(1)} collective-permute-done((f32[8,128]{1,0:T(8,128)S(1)}, f32[8,128]{1,0:T(8,128)S(1)}, u32[]{:S(2)}, u32[]{:S(2)}) %collective-permute-start.3) | collective-permute-done | bytes 4128 | tf_op jit(solution)/shard_map/ppermute | solution.py:1022
  6.8 0.1 shard_map.65
  6.8 2.0 %collective-permute-start.4 = (f32[48,128]{1,0:T(8,128)S(1)}, f32[48,128]{1,0:T(8,128)S(1)}, u32[]{:S(2)}, u32[]{:S(2)}) collective-permute-start(f32[48,128]{1,0:T(8,128)S(1)} %get-tuple-element.44), channel_id=1, source_target_pairs={{0,5},{1,4},{2,7},{3,6},{4,9},{5,8},{6,11},{7,10},{8,13},{9,12},{1... | collective-permute-start | bytes 73736 | tf_op jit(solution)/shard_map/ppermute | solution.py:1022
  8.9 2.1 %collective-permute-start.5 = (f32[48,128]{1,0:T(8,128)S(1)}, f32[48,128]{1,0:T(8,128)S(1)}, u32[]{:S(2)}, u32[]{:S(2)}) collective-permute-start(f32[48,128]{1,0:T(8,128)S(1)} %get-tuple-element.45), channel_id=1, source_target_pairs={{0,13},{1,12},{2,15},{3,14},{4,1},{5,0},{6,3},{7,2},{8,5},{9,4},{1... | collective-permute-start | bytes 73736 | tf_op jit(solution)/shard_map/ppermute | solution.py:1022
  11.0 0.0 collective-permute-done.2.yin
  11.0 1.3 %shard_map.64 = (f32[3,512,128]{2,1,0:T(8,128)}, f32[3,512,128]{2,1,0:T(8,128)}, f32[2,3,64,128]{3,2,1,0:T(8,128)S(1)}, f32[2,3,64,128]{3,2,1,0:T(8,128)S(1)}, f32[32,128]{1,0:T(8,128)S(1)}) custom-call(f32[3,1296,128]{2,1,0:T(8,128)S(1)} %get-tuple-element.36.e_ext, f32[3,1296,128]{2,1,0:T(8,128)S(1)} %get-tuple-element.37.h_ext, ...), custom_call_target="tpu_custom_call" | custom-call | flops 10000000000 | bytes 100000000 | tf_op jit(solution)/shard_map/pallas_call | solution.py:1087
  12.3 0.1 collective-permute-done.4.from_below
  12.4 0.1 collective-permute-done.5.from_above
  12.5 0.8 %shard_map.66 = (f32[3,512,128]{2,1,0:T(8,128)}, f32[3,512,128]{2,1,0:T(8,128)}, f32[2,3,64,128]{3,2,1,0:T(8,128)S(1)}, f32[2,3,64,128]{3,2,1,0:T(8,128)S(1)}) custom-call(f32[96,128]{1,0:T(8,128)S(1)} %get-tuple-element.33.up, f32[96,128]{1,0:T(8,128)S(1)} %get-tuple-element.34.down, ...), custom_call_target="tpu_custom_call", output_to_operand_aliasing={{0}: (8, {}), {1}: (9, {}), {2}: (6, {}), {3}: (7, {})} | custom-call | tf_op jit(solution)/shard_map/pallas_call | solution.py:1095
  (2 shorter events, 0.0 us)
Async XLA Ops:
  0.6 1.7 %copy-start.1 = (f32[1,1,1,3,65536]{4,2,3,1,0:T(1,128)S(1)}, f32[1,1,1,3,65536]{4,2,3,1,0:T(1,128)}, u32[]{:S(2)}) copy-start(f32[1,1,1,3,65536]{4,2,3,1,0:T(1,128)} %param.5) | copy-start | bytes 2359300
  0.6 1.7 %copy-start = (f32[1,1,1,3,65536]{4,2,3,1,0:T(1,128)S(1)}, f32[1,1,1,3,65536]{4,2,3,1,0:T(1,128)}, u32[]{:S(2)}) copy-start(f32[1,1,1,3,65536]{4,2,3,1,0:T(1,128)} %param.4) | copy-start | bytes 2359300
  1.7 1.3 %collective-permute-start.1 = (f32[8,128]{1,0:T(8,128)S(1)}, f32[8,128]{1,0:T(8,128)S(1)}, u32[]{:S(2)}, u32[]{:S(2)}) collective-permute-start(f32[8,128]{1,0:T(8,128)S(1)} %get-tuple-element.40), channel_id=1, source_target_pairs={{0,1},{1,0},{2,3},{3,2},{4,5},{5,4},{6,7},{7,6},{8,9},{9,8},{10,11... | collective-permute-start | bytes 12296 | tf_op jit(solution)/shard_map/ppermute | solution.py:1022
  2.5 3.0 %collective-permute-start = (f32[1088,128]{1,0:T(8,128)S(1)}, f32[1088,128]{1,0:T(8,128)S(1)}, u32[]{:S(2)}, u32[]{:S(2)}) collective-permute-start(f32[1088,128]{1,0:T(8,128)S(1)} %get-tuple-element.31), channel_id=1, source_target_pairs={{0,1},{1,0},{2,3},{3,2},{4,5},{5,4},{6,7},{7,6},{8,9},{9,8},{10,11... | collective-permute-start | bytes 1671176 | tf_op jit(solution)/shard_map/ppermute | solution.py:1022
  3.1 2.5 %copy-start.2 = (s32[1,1,1,65536]{3,2,1,0:T(1,128)S(1)}, s32[1,1,1,65536]{3,2,1,0:T(1,128)}, u32[]{:S(2)}) copy-start(s32[1,1,1,65536]{3,2,1,0:T(1,128)} %param.6) | copy-start | bytes 786436
  3.1 3.7 %collective-permute-start.3 = (f32[8,128]{1,0:T(8,128)S(1)}, f32[8,128]{1,0:T(8,128)S(1)}, u32[]{:S(2)}, u32[]{:S(2)}) collective-permute-start(f32[8,128]{1,0:T(8,128)S(1)} %shard_map.63), channel_id=1, source_target_pairs={{0,3},{1,2},{2,1},{3,0},{4,7},{5,6},{6,5},{7,4},{8,11},{9,10},{10,... | collective-permute-start | bytes 12296 | tf_op jit(solution)/shard_map/ppermute | solution.py:1022
  5.4 5.5 %collective-permute-start.2 = (f32[8,128]{1,0:T(8,128)S(1)}, f32[8,128]{1,0:T(8,128)S(1)}, u32[]{:S(2)}, u32[]{:S(2)}) collective-permute-start(f32[8,128]{1,0:T(8,128)S(1)} %shard_map.63), channel_id=1, source_target_pairs={{0,2},{1,3},{2,0},{3,1},{4,6},{5,7},{6,4},{7,5},{8,10},{9,11},{10,... | collective-permute-start | bytes 12296 | tf_op jit(solution)/shard_map/ppermute | solution.py:1022
  6.8 5.6 %collective-permute-start.4 = (f32[48,128]{1,0:T(8,128)S(1)}, f32[48,128]{1,0:T(8,128)S(1)}, u32[]{:S(2)}, u32[]{:S(2)}) collective-permute-start(f32[48,128]{1,0:T(8,128)S(1)} %get-tuple-element.44), channel_id=1, source_target_pairs={{0,5},{1,4},{2,7},{3,6},{4,9},{5,8},{6,11},{7,10},{8,13},{9,12},{1... | collective-permute-start | bytes 73736 | tf_op jit(solution)/shard_map/ppermute | solution.py:1022
  8.9 3.6 %collective-permute-start.5 = (f32[48,128]{1,0:T(8,128)S(1)}, f32[48,128]{1,0:T(8,128)S(1)}, u32[]{:S(2)}, u32[]{:S(2)}) collective-permute-start(f32[48,128]{1,0:T(8,128)S(1)} %get-tuple-element.45), channel_id=1, source_target_pairs={{0,13},{1,12},{2,15},{3,14},{4,1},{5,0},{6,3},{7,2},{8,5},{9,4},{1... | collective-permute-start | bytes 73736 | tf_op jit(solution)/shard_map/ppermute | solution.py:1022

commit v6 on v5

--- a/solution.py
+++ b/solution.py
@@ -369,19 +369,20 @@
     return loads
 
 
-def peek(e_hbm, h_hbm, m_hbm, edge_tile, m_face, m_ends, e_ends, h_ends, sems, m_sems):
+def peek(e_hbm, h_hbm, edge_tile, e_ends, h_ends, sems):
     def body(grid, gz):
         if grid is Fine:
             edge_tile[...] = jnp.zeros((8, 128), F32)
             return
-        m_loads = material_loads(grid, gz, m_hbm, m_face, m_ends, m_sems)
         loads = []
         for end in range(2):
             rows = pl.ds((1 - gz) * (ROWS - HALO) + (HALO - 8) * end, 8)
             place = pl.ds(0, 8)
             loads.append(pltpu.make_async_copy(e_hbm.at[:, rows], e_ends.at[end, :, place], sems.at[2 * end]))
-            loads.append(pltpu.make_async_copy(h_hbm.at[:, rows], h_ends.at[end, :, place], sems.at[2 * end + 1]))
-        for load in loads + m_loads:
+            for slot, comp in enumerate((0, 2)):
+                into = h_ends.at[end, comp, place]
+                loads.append(pltpu.make_async_copy(h_hbm.at[comp, rows], into, sems.at[4 + 2 * end + slot]))
+        for load in loads:
             load.start()
         for load in loads:
             load.wait()
@@ -395,13 +396,11 @@
                 to = 96 * end + 8 * kind + 3 + gz
                 tile = jnp.where(lane == to, pltpu.roll(value, to + 1, 1), tile)
         edge_tile[...] = tile
-        for load in m_loads:
-            load.wait()
 
     by_level(body)
 
 
-def fine_material(m_hbm, face_in, ends_in, m_face, m_ends, sems):
+def fine_material(m_hbm, after, m_face, m_ends, sems):
     def body(grid, gz):
         if grid is Coarse:
             return
@@ -446,7 +445,7 @@
         for x, comp in want_h:
             for part in range(grid.parts):
                 put(h_own[comp, column_rows(x, part), :])
-        for x in want_m:
+        for x in want_m if grid is Fine else []:
             for part in range(grid.parts):
                 rows = pl.ds(grid.step * x % 8 + part, grid.own, stride=8)
                 put(m_ends[int(x > 1), rows, :].astype(F32))
@@ -454,7 +453,8 @@
         for comp in range(3):
             zmsg[pl.ds(HALO * comp, HALO), :] = h_own[comp, edge, :]
             zmsg[pl.ds(HALO * (3 + comp), HALO), :] = e_own[comp, edge, :]
-        zmsg[pl.ds(6 * HALO, HALO), :] = m_face[...].astype(F32)
+        if grid is Fine:
+            zmsg[pl.ds(6 * HALO, HALO), :] = m_face[...].astype(F32)
         zmsg[pl.ds(FACE, COLUMNS), :] = columns[...]
 
     by_level(body)
@@ -688,7 +688,7 @@
                 found = jnp.where(is_material(i), parts[i], found)
             return found
 
-        for start in range(0, HALO, CHUNK):
+        for start in range(0, HALO if grid is Fine else 0, CHUNK):
             layer, rest = divmod(start, grid.depth)
             material = zmsg[pl.ds(6 * HALO + start, CHUNK), :]
             row = layer_row(grid, halo + layer) + rest
@@ -700,6 +700,11 @@
             c_ext[pl.ds(row, CHUNK), :] = coef(lambda i, m=material: m == i, CHUNK)
 
         e, h, m = read_columns(grid, columns, zmsg, gz)
+        if grid is Coarse:
+            for x in m:
+                rows = [pl.ds(4 * x + part, 4, stride=grid.depth) for part in range(4)]
+                own = [m_own[part, :].astype(F32) for part in rows]
+                m[x] = [jnp.concatenate([part, part], axis=0) for part in own]
         c = {
             x: [coef(lambda i, q=part: q == float(i), part.shape[0]) for part in col] for x, col in m.items()
         }
@@ -926,6 +931,8 @@
         def finish(edge):
             copies = []
             for slot, (tile, out) in enumerate(((h_tile, h_out), (e_tile, e_out))):
+                if grid is Coarse and edge == 0 and slot == 0:
+                    continue
                 source = tile.at[edge].reshape(3, 8, 8, 128).at[:, pl.ds(0, grid.own)]
                 target = block_layers(grid, out).at[:, :, pl.ds((grid.depth - 8) * edge, 8), :]
                 copies.append(pltpu.make_async_copy(source, target, sems.at[2 * edge + slot]))
@@ -1027,21 +1034,20 @@
     h = magnetic.reshape(3, ROWS, 128)
     m = material.reshape(ROWS, 128)
     dma = pltpu.SemaphoreType.DMA
-    edge_tile, m_face, m_ends = kernel_call(
+    edge_tile = kernel_call(
         peek,
-        [vmem(8, 128), vmem(HALO, 128, dtype=jnp.int32), vmem(2, 64, 128, dtype=jnp.int32)],
-        [HBM] * 3,
-        [VM] * 3,
-        [pltpu.VMEM((2, 3, 16, 128), F32)] * 2 + [dma((4,)), dma((3,))],
-    )(far(e), far(h), far(m))
+        vmem(8, 128),
+        [HBM] * 2,
+        VM,
+        [pltpu.VMEM((2, 3, 16, 128), F32)] * 2 + [dma((8,))],
+    )(far(e), far(h))
     m_face, m_ends = kernel_call(
         fine_material,
         [vmem(HALO, 128, dtype=jnp.int32), vmem(2, 64, 128, dtype=jnp.int32)],
-        [HBM, VM, VM],
+        [HBM, VM],
         [VM] * 2,
         [dma((3,))],
-        aliases={1: 0, 2: 1},
-    )(far(m), held(m_face), held(m_ends))
+    )(far(m), held(edge_tile))
     edge_tile = across(edge_tile, dz=1)
     zmsg, ytile, columns = kernel_call(
         gather,

time: 13.4 us -> 13.4 us (level)
  no operation moved by 1% of the time
where the time goes in v6:
time: 13.4 us; the launch traced here: 13.2 us
  starting transfers between devices  7.42 us (55%)
  Pallas kernels  4.24 us (32%)
  waiting for transfers between devices  0.84 us (6%)
  between operations  0.7 us (5%)
    ppermute x6, starting transfers between devices, across(): return lax.ppermute(x, ('gx', 'gy', 'gz'), pairs)  7.42 us
    pallas_call x1, Pallas kernels, fast_shards(): kernel_call(advance, [whole, whole, vmem(2, 3, 64, 128), vmem(2, 3, 64, 1...  1.33 us
    pallas_call x1, Pallas kernels, fast_shards(): kernel_call(peek, vmem(8, 128), [HBM] * 2, VM, [pltpu.VMEM((2, 3, 16, 128...  1.04 us
    ppermute x6, waiting for transfers between devices, across(): return lax.ppermute(x, ('gx', 'gy', 'gz'), pairs)  0.84 us
    pallas_call x1, Pallas kernels, fast_shards(): kernel_call(extend, [vmem(3, EXT, 128), vmem(3, EXT, 128), vmem(EXT, 128)...  0.78 us
    pallas_call x1, Pallas kernels, fast_shards(): kernel_call(correct, [whole, whole, vmem(2, 3, 64, 128), vmem(2, 3, 64, 1...  0.77 us
  transfers between devices with their start and end apart: 6, of which 4 were waited for; matrix products, arithmetic and copies ran while one was open for 0% of the time, Pallas kernels for 18%

profile of v6, /device:TPU:0, one launch (start us, length us, event | category | flops | bytes accessed | tf_op | source)
XLA Modules:
  0.0 13.2 jit_solution(9369076185216106999)
XLA Ops:
  0.6 0.0 copy-start.1
  0.6 0.0 copy-start
  0.6 1.0 %shard_map.59.after = f32[8,128]{1,0:T(8,128)S(1)} custom-call(f32[3,512,128]{2,1,0:T(8,128)} %bitcast.5, f32[3,512,128]{2,1,0:T(8,128)} %bitcast.8), custom_call_target="tpu_custom_call" | custom-call | tf_op jit(solution)/shard_map/pallas_call | solution.py:1037
  1.7 0.5 %collective-permute-start.1 = (f32[8,128]{1,0:T(8,128)S(1)}, f32[8,128]{1,0:T(8,128)S(1)}, u32[]{:S(2)}, u32[]{:S(2)}) collective-permute-start(f32[8,128]{1,0:T(8,128)S(1)} %shard_map.59.after), channel_id=1, source_target_pairs={{0,1},{1,0},{2,3},{3,2},{4,5},{5,4},{6,7},{7,6},{8,9},{9,8},{10,11... | collective-permute-start | bytes 12296 | tf_op jit(solution)/shard_map/ppermute | solution.py:1029
  2.3 0.0 copy-done.1
  2.3 0.0 copy-done
  2.3 0.2 %shard_map.61 = (f32[1088,128]{1,0:T(8,128)S(1)}, f32[8,128]{1,0:T(8,128)S(1)}, f32[192,128]{1,0:T(8,128)S(1)}) custom-call(f32[3,512,128]{2,1,0:T(8,128)S(1)} %bitcast.6, f32[3,512,128]{2,1,0:T(8,128)S(1)} %bitcast.9, s32[128,128]{1,0:T(8,128)S(1)} %get-tuple-element.24.m_face, s32[2,64,128]{2,1,0:T(8,128)S(1)} %get-tuple-element.25.m_ends), custom_call_target="tpu_custom_call" | custom-call | tf_op jit(solution)/shard_map/pallas_call | solution.py:1052
  2.5 0.3 %collective-permute-start = (f32[1088,128]{1,0:T(8,128)S(1)}, f32[1088,128]{1,0:T(8,128)S(1)}, u32[]{:S(2)}, u32[]{:S(2)}) collective-permute-start(f32[1088,128]{1,0:T(8,128)S(1)} %get-tuple-element.26), channel_id=1, source_target_pairs={{0,1},{1,0},{2,3},{3,2},{4,5},{5,4},{6,7},{7,6},{8,9},{9,8},{10,11... | collective-permute-start | bytes 1671176 | tf_op jit(solution)/shard_map/ppermute | solution.py:1029
  2.8 0.3 %collective-permute-done.1.edge_tile = f32[8,128]{1,0:T(8,128)S(1)} collective-permute-done((f32[8,128]{1,0:T(8,128)S(1)}, f32[8,128]{1,0:T(8,128)S(1)}, u32[]{:S(2)}, u32[]{:S(2)}) %collective-permute-start.1) | collective-permute-done | bytes 4128 | tf_op jit(solution)/shard_map/ppermute | solution.py:1029
  3.0 0.0 copy-start.2
  3.0 2.4 %collective-permute-start.3 = (f32[8,128]{1,0:T(8,128)S(1)}, f32[8,128]{1,0:T(8,128)S(1)}, u32[]{:S(2)}, u32[]{:S(2)}) collective-permute-start(f32[8,128]{1,0:T(8,128)S(1)} %shard_map.63), channel_id=1, source_target_pairs={{0,3},{1,2},{2,1},{3,0},{4,7},{5,6},{6,5},{7,4},{8,11},{9,10},{10,... | collective-permute-start | bytes 12296 | tf_op jit(solution)/shard_map/ppermute | solution.py:1029
  5.4 0.1 collective-permute-start.2
  5.6 0.0 collective-permute-done.zmsg.r_other
  5.6 0.0 copy-done.2
  5.6 0.8 %shard_map.62 = (f32[3,1296,128]{2,1,0:T(8,128)S(1)}, f32[3,1296,128]{2,1,0:T(8,128)S(1)}, f32[1296,128]{1,0:T(8,128)S(1)}, f32[96,128]{1,0:T(8,128)S(1)}, f32[9...) custom-call(f32[3,512,128]{2,1,0:T(8,128)S(1)} %bitcast.7, ...), custom_call_target="tpu_custom_call" | custom-call | tf_op jit(solution)/shard_map/pallas_call | solution.py:1068
  6.4 0.4 %collective-permute-done.3.yzin = f32[8,128]{1,0:T(8,128)S(1)} collective-permute-done((f32[8,128]{1,0:T(8,128)S(1)}, f32[8,128]{1,0:T(8,128)S(1)}, u32[]{:S(2)}, u32[]{:S(2)}) %collective-permute-start.3) | collective-permute-done | bytes 4128 | tf_op jit(solution)/shard_map/ppermute | solution.py:1029
  6.8 0.1 shard_map.65
  6.8 2.0 %collective-permute-start.4 = (f32[48,128]{1,0:T(8,128)S(1)}, f32[48,128]{1,0:T(8,128)S(1)}, u32[]{:S(2)}, u32[]{:S(2)}) collective-permute-start(f32[48,128]{1,0:T(8,128)S(1)} %get-tuple-element.38), channel_id=1, source_target_pairs={{0,5},{1,4},{2,7},{3,6},{4,9},{5,8},{6,11},{7,10},{8,13},{9,12},{1... | collective-permute-start | bytes 73736 | tf_op jit(solution)/shard_map/ppermute | solution.py:1029
  8.9 2.1 %collective-permute-start.5 = (f32[48,128]{1,0:T(8,128)S(1)}, f32[48,128]{1,0:T(8,128)S(1)}, u32[]{:S(2)}, u32[]{:S(2)}) collective-permute-start(f32[48,128]{1,0:T(8,128)S(1)} %get-tuple-element.39), channel_id=1, source_target_pairs={{0,13},{1,12},{2,15},{3,14},{4,1},{5,0},{6,3},{7,2},{8,5},{9,4},{1... | collective-permute-start | bytes 73736 | tf_op jit(solution)/shard_map/ppermute | solution.py:1029
  10.9 0.0 collective-permute-done.2.yin
  10.9 1.3 %shard_map.64 = (f32[3,512,128]{2,1,0:T(8,128)}, f32[3,512,128]{2,1,0:T(8,128)}, f32[2,3,64,128]{3,2,1,0:T(8,128)S(1)}, f32[2,3,64,128]{3,2,1,0:T(8,128)S(1)}, f32[32,128]{1,0:T(8,128)S(1)}) custom-call(f32[3,1296,128]{2,1,0:T(8,128)S(1)} %get-tuple-element.31.e_ext, f32[3,1296,128]{2,1,0:T(8,128)S(1)} %get-tuple-element.32.h_ext, ...), custom_call_target="tpu_custom_call" | custom-call | flops 10000000000 | bytes 100000000 | tf_op jit(solution)/shard_map/pallas_call | solution.py:1093
  12.3 0.1 collective-permute-done.4.from_below
  12.4 0.1 collective-permute-done.5.from_above
  12.4 0.8 %shard_map.66 = (f32[3,512,128]{2,1,0:T(8,128)}, f32[3,512,128]{2,1,0:T(8,128)}, f32[2,3,64,128]{3,2,1,0:T(8,128)S(1)}, f32[2,3,64,128]{3,2,1,0:T(8,128)S(1)}) custom-call(f32[96,128]{1,0:T(8,128)S(1)} %get-tuple-element.28.up, f32[96,128]{1,0:T(8,128)S(1)} %get-tuple-element.29.down, ...), custom_call_target="tpu_custom_call", output_to_operand_aliasing={{0}: (8, {}), {1}: (9, {}), {2}: (6, {}), {3}: (7, {})} | custom-call | tf_op jit(solution)/shard_map/pallas_call | solution.py:1101
  (2 shorter events, 0.0 us)
Async XLA Ops:
  0.6 1.6 %copy-start.1 = (f32[1,1,1,3,65536]{4,2,3,1,0:T(1,128)S(1)}, f32[1,1,1,3,65536]{4,2,3,1,0:T(1,128)}, u32[]{:S(2)}) copy-start(f32[1,1,1,3,65536]{4,2,3,1,0:T(1,128)} %param.5) | copy-start | bytes 2359300
  0.6 1.6 %copy-start = (f32[1,1,1,3,65536]{4,2,3,1,0:T(1,128)S(1)}, f32[1,1,1,3,65536]{4,2,3,1,0:T(1,128)}, u32[]{:S(2)}) copy-start(f32[1,1,1,3,65536]{4,2,3,1,0:T(1,128)} %param.4) | copy-start | bytes 2359300
  1.7 1.3 %collective-permute-start.1 = (f32[8,128]{1,0:T(8,128)S(1)}, f32[8,128]{1,0:T(8,128)S(1)}, u32[]{:S(2)}, u32[]{:S(2)}) collective-permute-start(f32[8,128]{1,0:T(8,128)S(1)} %shard_map.59.after), channel_id=1, source_target_pairs={{0,1},{1,0},{2,3},{3,2},{4,5},{5,4},{6,7},{7,6},{8,9},{9,8},{10,11... | collective-permute-start | bytes 12296 | tf_op jit(solution)/shard_map/ppermute | solution.py:1029
  2.5 3.1 %collective-permute-start = (f32[1088,128]{1,0:T(8,128)S(1)}, f32[1088,128]{1,0:T(8,128)S(1)}, u32[]{:S(2)}, u32[]{:S(2)}) collective-permute-start(f32[1088,128]{1,0:T(8,128)S(1)} %get-tuple-element.26), channel_id=1, source_target_pairs={{0,1},{1,0},{2,3},{3,2},{4,5},{5,4},{6,7},{7,6},{8,9},{9,8},{10,11... | collective-permute-start | bytes 1671176 | tf_op jit(solution)/shard_map/ppermute | solution.py:1029
  3.0 2.5 %copy-start.2 = (s32[1,1,1,65536]{3,2,1,0:T(1,128)S(1)}, s32[1,1,1,65536]{3,2,1,0:T(1,128)}, u32[]{:S(2)}) copy-start(s32[1,1,1,65536]{3,2,1,0:T(1,128)} %param.6) | copy-start | bytes 786436
  3.0 3.7 %collective-permute-start.3 = (f32[8,128]{1,0:T(8,128)S(1)}, f32[8,128]{1,0:T(8,128)S(1)}, u32[]{:S(2)}, u32[]{:S(2)}) collective-permute-start(f32[8,128]{1,0:T(8,128)S(1)} %shard_map.63), channel_id=1, source_target_pairs={{0,3},{1,2},{2,1},{3,0},{4,7},{5,6},{6,5},{7,4},{8,11},{9,10},{10,... | collective-permute-start | bytes 12296 | tf_op jit(solution)/shard_map/ppermute | solution.py:1029
  5.4 5.5 %collective-permute-start.2 = (f32[8,128]{1,0:T(8,128)S(1)}, f32[8,128]{1,0:T(8,128)S(1)}, u32[]{:S(2)}, u32[]{:S(2)}) collective-permute-start(f32[8,128]{1,0:T(8,128)S(1)} %shard_map.63), channel_id=1, source_target_pairs={{0,2},{1,3},{2,0},{3,1},{4,6},{5,7},{6,4},{7,5},{8,10},{9,11},{10,... | collective-permute-start | bytes 12296 | tf_op jit(solution)/shard_map/ppermute | solution.py:1029
  6.8 5.5 %collective-permute-start.4 = (f32[48,128]{1,0:T(8,128)S(1)}, f32[48,128]{1,0:T(8,128)S(1)}, u32[]{:S(2)}, u32[]{:S(2)}) collective-permute-start(f32[48,128]{1,0:T(8,128)S(1)} %get-tuple-element.38), channel_id=1, source_target_pairs={{0,5},{1,4},{2,7},{3,6},{4,9},{5,8},{6,11},{7,10},{8,13},{9,12},{1... | collective-permute-start | bytes 73736 | tf_op jit(solution)/shard_map/ppermute | solution.py:1029
  8.9 3.6 %collective-permute-start.5 = (f32[48,128]{1,0:T(8,128)S(1)}, f32[48,128]{1,0:T(8,128)S(1)}, u32[]{:S(2)}, u32[]{:S(2)}) collective-permute-start(f32[48,128]{1,0:T(8,128)S(1)} %get-tuple-element.39), channel_id=1, source_target_pairs={{0,13},{1,12},{2,15},{3,14},{4,1},{5,0},{6,3},{7,2},{8,5},{9,4},{1... | collective-permute-start | bytes 73736 | tf_op jit(solution)/shard_map/ppermute | solution.py:1029

commit v7 on v6

--- a/solution.py
+++ b/solution.py
@@ -943,35 +943,9 @@
         if grid is Fine:
             zero = [jnp.zeros((16, 128), F32)]
             ez64, ey64, ey64_part, ez64_part, c64 = read_message(grid, from_above, DOWN[grid], gz)
-            ey_top = column_of(from_above[pl.ds(MESSAGE - 8, 8), :], 0, 7, 16, grid)
+            ey_above = column_of(from_above[pl.ds(MESSAGE - 8, 8), :], 0, 7, 16, grid)
             hy63, hz63 = read_planes(grid, up, 0, 1)
             c0, c1, c62, c63 = read_planes(grid, c_planes, *range(4))
-            ghost = -0.5 * ey_top
-            dhy, dhz = scale(0.5, ez64), scale(-0.5, ey64)
-            dex = mul(c63, sub(minus_y(dhz, ghost), minus_z(dhy)))
-            dey = scale(-1.0, mul(c63, dhz))
-            dez = mul(c63, dhy)
-            dex62 = mul(c62, minus_y(zero, ghost))
-            ey64_next = add(ey64_part, mul(c64, add(hz63, dhz)))
-            ez64_next = sub(ez64_part, mul(c64, add(hy63, dhy)))
-            dhx2 = scale(-0.5, sub(plus_y(dez), plus_z(dey)))
-            dhy2 = add(dhy, scale(-0.5, sub(plus_z(dex), sub(ez64_next, dez))))
-            dhz2 = add(dhz, scale(-0.5, sub(sub(ey64_next, dey), plus_y(dex))))
-            dhy62 = scale(-0.5, sub(plus_z(dex62), dez))
-            dhz62 = scale(-0.5, sub(dey, plus_y(dex62)))
-            put(h_tile, 1, 0, 63, dhx2)
-            put(h_tile, 1, 1, 63, dhy2)
-            put(h_tile, 1, 2, 63, dhz2)
-            put(h_tile, 1, 1, 62, dhy62)
-            put(h_tile, 1, 2, 62, dhz62)
-            put(e_tile, 1, 0, 63, add(dex, mul(c63, sub(minus_y(dhz2, ghost), minus_z(dhy2)))))
-            put(e_tile, 1, 1, 63, add(dey, mul(c63, sub(minus_z(dhx2), sub(dhz2, dhz62)))))
-            put(e_tile, 1, 2, 63, add(dez, mul(c63, sub(sub(dhy2, dhy62), minus_y(dhx2)))))
-            put(e_tile, 1, 0, 62, add(dex62, mul(c62, sub(minus_y(dhz62, ghost), minus_z(dhy62)))))
-            put(e_tile, 1, 1, 62, scale(-1.0, mul(c62, dhz62)))
-            put(e_tile, 1, 2, 62, mul(c62, dhy62))
-            copies = finish(1)
-
             hy_part, hz_part, next_y, next_z, cm = read_message(grid, from_below, UP[grid], gz)
             ez0, ey0, ey0_part, ez0_part = read_planes(grid, down, *range(4))
             ez0_change, ey_top = read_planes(grid, patched, 0, 1)
@@ -996,7 +970,33 @@
             put(e_tile, 0, 2, 0, add(dez, mul(c0, sub(sub(dhy2, hym2), minus_y(dhx2)))))
             put(e_tile, 0, 1, 1, mul(c1, dhz2))
             put(e_tile, 0, 2, 1, scale(-1.0, mul(c1, dhy2)))
-            copies += finish(0)
+            copies = finish(0)
+
+            ghost = -0.5 * ey_above
+            dhy, dhz = scale(0.5, ez64), scale(-0.5, ey64)
+            dex = mul(c63, sub(minus_y(dhz, ghost), minus_z(dhy)))
+            dey = scale(-1.0, mul(c63, dhz))
+            dez = mul(c63, dhy)
+            dex62 = mul(c62, minus_y(zero, ghost))
+            ey64_next = add(ey64_part, mul(c64, add(hz63, dhz)))
+            ez64_next = sub(ez64_part, mul(c64, add(hy63, dhy)))
+            dhx2 = scale(-0.5, sub(plus_y(dez), plus_z(dey)))
+            dhy2 = add(dhy, scale(-0.5, sub(plus_z(dex), sub(ez64_next, dez))))
+            dhz2 = add(dhz, scale(-0.5, sub(sub(ey64_next, dey), plus_y(dex))))
+            dhy62 = scale(-0.5, sub(plus_z(dex62), dez))
+            dhz62 = scale(-0.5, sub(dey, plus_y(dex62)))
+            put(h_tile, 1, 0, 63, dhx2)
+            put(h_tile, 1, 1, 63, dhy2)
+            put(h_tile, 1, 2, 63, dhz2)
+            put(h_tile, 1, 1, 62, dhy62)
+            put(h_tile, 1, 2, 62, dhz62)
+            put(e_tile, 1, 0, 63, add(dex, mul(c63, sub(minus_y(dhz2, ghost), minus_z(dhy2)))))
+            put(e_tile, 1, 1, 63, add(dey, mul(c63, sub(minus_z(dhx2), sub(dhz2, dhz62)))))
+            put(e_tile, 1, 2, 63, add(dez, mul(c63, sub(sub(dhy2, dhy62), minus_y(dhx2)))))
+            put(e_tile, 1, 0, 62, add(dex62, mul(c62, sub(minus_y(dhz62, ghost), minus_z(dhy62)))))
+            put(e_tile, 1, 1, 62, scale(-1.0, mul(c62, dhz62)))
+            put(e_tile, 1, 2, 62, mul(c62, dhy62))
+            copies += finish(1)
         else:
             ez32, ey32 = read_message(grid, from_above, DOWN[grid], gz)
             c0, c31 = read_planes(grid, c_planes, 0, 1)

time: 13.4 us -> 13.4 us (level)
  no operation moved by 1% of the time
where the time goes in v7:
time: 13.4 us; the launch traced here: 13.2 us
  starting transfers between devices  7.42 us (55%)
  Pallas kernels  4.24 us (32%)
  waiting for transfers between devices  0.84 us (6%)
  between operations  0.7 us (5%)
    ppermute x6, starting transfers between devices, across(): return lax.ppermute(x, ('gx', 'gy', 'gz'), pairs)  7.42 us
    pallas_call x1, Pallas kernels, fast_shards(): kernel_call(advance, [whole, whole, vmem(2, 3, 64, 128), vmem(2, 3, 64, 1...  1.33 us
    pallas_call x1, Pallas kernels, fast_shards(): kernel_call(peek, vmem(8, 128), [HBM] * 2, VM, [pltpu.VMEM((2, 3, 16, 128...  1.04 us
    ppermute x6, waiting for transfers between devices, across(): return lax.ppermute(x, ('gx', 'gy', 'gz'), pairs)  0.84 us
    pallas_call x1, Pallas kernels, fast_shards(): kernel_call(extend, [vmem(3, EXT, 128), vmem(3, EXT, 128), vmem(EXT, 128)...  0.78 us
    pallas_call x1, Pallas kernels, fast_shards(): kernel_call(correct, [whole, whole, vmem(2, 3, 64, 128), vmem(2, 3, 64, 1...  0.77 us
  transfers between devices with their start and end apart: 6, of which 4 were waited for; matrix products, arithmetic and copies ran while one was open for 0% of the time, Pallas kernels for 18%

profile of v7, /device:TPU:0, one launch (start us, length us, event | category | flops | bytes accessed | tf_op | source)
XLA Modules:
  0.0 13.2 jit_solution(7158967387448433889)
XLA Ops:
  0.6 0.0 copy-start.1
  0.6 0.0 copy-start
  0.6 1.0 %shard_map.59.after = f32[8,128]{1,0:T(8,128)S(1)} custom-call(f32[3,512,128]{2,1,0:T(8,128)} %bitcast.5, f32[3,512,128]{2,1,0:T(8,128)} %bitcast.8), custom_call_target="tpu_custom_call" | custom-call | tf_op jit(solution)/shard_map/pallas_call | solution.py:1037
  1.7 0.5 %collective-permute-start.1 = (f32[8,128]{1,0:T(8,128)S(1)}, f32[8,128]{1,0:T(8,128)S(1)}, u32[]{:S(2)}, u32[]{:S(2)}) collective-permute-start(f32[8,128]{1,0:T(8,128)S(1)} %shard_map.59.after), channel_id=1, source_target_pairs={{0,1},{1,0},{2,3},{3,2},{4,5},{5,4},{6,7},{7,6},{8,9},{9,8},{10,11... | collective-permute-start | bytes 12296 | tf_op jit(solution)/shard_map/ppermute | solution.py:1029
  2.3 0.0 copy-done.1
  2.3 0.0 copy-done
  2.3 0.2 %shard_map.61 = (f32[1088,128]{1,0:T(8,128)S(1)}, f32[8,128]{1,0:T(8,128)S(1)}, f32[192,128]{1,0:T(8,128)S(1)}) custom-call(f32[3,512,128]{2,1,0:T(8,128)S(1)} %bitcast.6, f32[3,512,128]{2,1,0:T(8,128)S(1)} %bitcast.9, s32[128,128]{1,0:T(8,128)S(1)} %get-tuple-element.24.m_face, s32[2,64,128]{2,1,0:T(8,128)S(1)} %get-tuple-element.25.m_ends), custom_call_target="tpu_custom_call" | custom-call | tf_op jit(solution)/shard_map/pallas_call | solution.py:1052
  2.5 0.3 %collective-permute-start = (f32[1088,128]{1,0:T(8,128)S(1)}, f32[1088,128]{1,0:T(8,128)S(1)}, u32[]{:S(2)}, u32[]{:S(2)}) collective-permute-start(f32[1088,128]{1,0:T(8,128)S(1)} %get-tuple-element.26), channel_id=1, source_target_pairs={{0,1},{1,0},{2,3},{3,2},{4,5},{5,4},{6,7},{7,6},{8,9},{9,8},{10,11... | collective-permute-start | bytes 1671176 | tf_op jit(solution)/shard_map/ppermute | solution.py:1029
  2.8 0.3 %collective-permute-done.1.edge_tile = f32[8,128]{1,0:T(8,128)S(1)} collective-permute-done((f32[8,128]{1,0:T(8,128)S(1)}, f32[8,128]{1,0:T(8,128)S(1)}, u32[]{:S(2)}, u32[]{:S(2)}) %collective-permute-start.1) | collective-permute-done | bytes 4128 | tf_op jit(solution)/shard_map/ppermute | solution.py:1029
  3.0 0.0 copy-start.2
  3.0 2.4 %collective-permute-start.3 = (f32[8,128]{1,0:T(8,128)S(1)}, f32[8,128]{1,0:T(8,128)S(1)}, u32[]{:S(2)}, u32[]{:S(2)}) collective-permute-start(f32[8,128]{1,0:T(8,128)S(1)} %shard_map.63), channel_id=1, source_target_pairs={{0,3},{1,2},{2,1},{3,0},{4,7},{5,6},{6,5},{7,4},{8,11},{9,10},{10,... | collective-permute-start | bytes 12296 | tf_op jit(solution)/shard_map/ppermute | solution.py:1029
  5.4 0.1 collective-permute-start.2
  5.6 0.0 collective-permute-done.zmsg.r_other
  5.6 0.0 copy-done.2
  5.6 0.8 %shard_map.62 = (f32[3,1296,128]{2,1,0:T(8,128)S(1)}, f32[3,1296,128]{2,1,0:T(8,128)S(1)}, f32[1296,128]{1,0:T(8,128)S(1)}, f32[96,128]{1,0:T(8,128)S(1)}, f32[9...) custom-call(f32[3,512,128]{2,1,0:T(8,128)S(1)} %bitcast.7, ...), custom_call_target="tpu_custom_call" | custom-call | tf_op jit(solution)/shard_map/pallas_call | solution.py:1068
  6.4 0.4 %collective-permute-done.3.yzin = f32[8,128]{1,0:T(8,128)S(1)} collective-permute-done((f32[8,128]{1,0:T(8,128)S(1)}, f32[8,128]{1,0:T(8,128)S(1)}, u32[]{:S(2)}, u32[]{:S(2)}) %collective-permute-start.3) | collective-permute-done | bytes 4128 | tf_op jit(solution)/shard_map/ppermute | solution.py:1029
  6.8 0.1 shard_map.65
  6.8 2.0 %collective-permute-start.4 = (f32[48,128]{1,0:T(8,128)S(1)}, f32[48,128]{1,0:T(8,128)S(1)}, u32[]{:S(2)}, u32[]{:S(2)}) collective-permute-start(f32[48,128]{1,0:T(8,128)S(1)} %get-tuple-element.38), channel_id=1, source_target_pairs={{0,5},{1,4},{2,7},{3,6},{4,9},{5,8},{6,11},{7,10},{8,13},{9,12},{1... | collective-permute-start | bytes 73736 | tf_op jit(solution)/shard_map/ppermute | solution.py:1029
  8.9 2.1 %collective-permute-start.5 = (f32[48,128]{1,0:T(8,128)S(1)}, f32[48,128]{1,0:T(8,128)S(1)}, u32[]{:S(2)}, u32[]{:S(2)}) collective-permute-start(f32[48,128]{1,0:T(8,128)S(1)} %get-tuple-element.39), channel_id=1, source_target_pairs={{0,13},{1,12},{2,15},{3,14},{4,1},{5,0},{6,3},{7,2},{8,5},{9,4},{1... | collective-permute-start | bytes 73736 | tf_op jit(solution)/shard_map/ppermute | solution.py:1029
  10.9 0.0 collective-permute-done.2.yin
  10.9 1.3 %shard_map.64 = (f32[3,512,128]{2,1,0:T(8,128)}, f32[3,512,128]{2,1,0:T(8,128)}, f32[2,3,64,128]{3,2,1,0:T(8,128)S(1)}, f32[2,3,64,128]{3,2,1,0:T(8,128)S(1)}, f32[32,128]{1,0:T(8,128)S(1)}) custom-call(f32[3,1296,128]{2,1,0:T(8,128)S(1)} %get-tuple-element.31.e_ext, f32[3,1296,128]{2,1,0:T(8,128)S(1)} %get-tuple-element.32.h_ext, ...), custom_call_target="tpu_custom_call" | custom-call | flops 10000000000 | bytes 100000000 | tf_op jit(solution)/shard_map/pallas_call | solution.py:1093
  12.3 0.1 collective-permute-done.4.from_below
  12.4 0.1 collective-permute-done.5.from_above
  12.4 0.8 %shard_map.66 = (f32[3,512,128]{2,1,0:T(8,128)}, f32[3,512,128]{2,1,0:T(8,128)}, f32[2,3,64,128]{3,2,1,0:T(8,128)S(1)}, f32[2,3,64,128]{3,2,1,0:T(8,128)S(1)}) custom-call(f32[96,128]{1,0:T(8,128)S(1)} %get-tuple-element.28.up, f32[96,128]{1,0:T(8,128)S(1)} %get-tuple-element.29.down, ...), custom_call_target="tpu_custom_call", output_to_operand_aliasing={{0}: (8, {}), {1}: (9, {}), {2}: (6, {}), {3}: (7, {})} | custom-call | tf_op jit(solution)/shard_map/pallas_call | solution.py:1101
  (2 shorter events, 0.0 us)
Async XLA Ops:
  0.6 1.6 %copy-start.1 = (f32[1,1,1,3,65536]{4,2,3,1,0:T(1,128)S(1)}, f32[1,1,1,3,65536]{4,2,3,1,0:T(1,128)}, u32[]{:S(2)}) copy-start(f32[1,1,1,3,65536]{4,2,3,1,0:T(1,128)} %param.5) | copy-start | bytes 2359300
  0.6 1.6 %copy-start = (f32[1,1,1,3,65536]{4,2,3,1,0:T(1,128)S(1)}, f32[1,1,1,3,65536]{4,2,3,1,0:T(1,128)}, u32[]{:S(2)}) copy-start(f32[1,1,1,3,65536]{4,2,3,1,0:T(1,128)} %param.4) | copy-start | bytes 2359300
  1.7 1.3 %collective-permute-start.1 = (f32[8,128]{1,0:T(8,128)S(1)}, f32[8,128]{1,0:T(8,128)S(1)}, u32[]{:S(2)}, u32[]{:S(2)}) collective-permute-start(f32[8,128]{1,0:T(8,128)S(1)} %shard_map.59.after), channel_id=1, source_target_pairs={{0,1},{1,0},{2,3},{3,2},{4,5},{5,4},{6,7},{7,6},{8,9},{9,8},{10,11... | collective-permute-start | bytes 12296 | tf_op jit(solution)/shard_map/ppermute | solution.py:1029
  2.5 3.1 %collective-permute-start = (f32[1088,128]{1,0:T(8,128)S(1)}, f32[1088,128]{1,0:T(8,128)S(1)}, u32[]{:S(2)}, u32[]{:S(2)}) collective-permute-start(f32[1088,128]{1,0:T(8,128)S(1)} %get-tuple-element.26), channel_id=1, source_target_pairs={{0,1},{1,0},{2,3},{3,2},{4,5},{5,4},{6,7},{7,6},{8,9},{9,8},{10,11... | collective-permute-start | bytes 1671176 | tf_op jit(solution)/shard_map/ppermute | solution.py:1029
  3.0 2.5 %copy-start.2 = (s32[1,1,1,65536]{3,2,1,0:T(1,128)S(1)}, s32[1,1,1,65536]{3,2,1,0:T(1,128)}, u32[]{:S(2)}) copy-start(s32[1,1,1,65536]{3,2,1,0:T(1,128)} %param.6) | copy-start | bytes 786436
  3.0 3.7 %collective-permute-start.3 = (f32[8,128]{1,0:T(8,128)S(1)}, f32[8,128]{1,0:T(8,128)S(1)}, u32[]{:S(2)}, u32[]{:S(2)}) collective-permute-start(f32[8,128]{1,0:T(8,128)S(1)} %shard_map.63), channel_id=1, source_target_pairs={{0,3},{1,2},{2,1},{3,0},{4,7},{5,6},{6,5},{7,4},{8,11},{9,10},{10,... | collective-permute-start | bytes 12296 | tf_op jit(solution)/shard_map/ppermute | solution.py:1029
  5.4 5.5 %collective-permute-start.2 = (f32[8,128]{1,0:T(8,128)S(1)}, f32[8,128]{1,0:T(8,128)S(1)}, u32[]{:S(2)}, u32[]{:S(2)}) collective-permute-start(f32[8,128]{1,0:T(8,128)S(1)} %shard_map.63), channel_id=1, source_target_pairs={{0,2},{1,3},{2,0},{3,1},{4,6},{5,7},{6,4},{7,5},{8,10},{9,11},{10,... | collective-permute-start | bytes 12296 | tf_op jit(solution)/shard_map/ppermute | solution.py:1029
  6.8 5.5 %collective-permute-start.4 = (f32[48,128]{1,0:T(8,128)S(1)}, f32[48,128]{1,0:T(8,128)S(1)}, u32[]{:S(2)}, u32[]{:S(2)}) collective-permute-start(f32[48,128]{1,0:T(8,128)S(1)} %get-tuple-element.38), channel_id=1, source_target_pairs={{0,5},{1,4},{2,7},{3,6},{4,9},{5,8},{6,11},{7,10},{8,13},{9,12},{1... | collective-permute-start | bytes 73736 | tf_op jit(solution)/shard_map/ppermute | solution.py:1029
  8.9 3.6 %collective-permute-start.5 = (f32[48,128]{1,0:T(8,128)S(1)}, f32[48,128]{1,0:T(8,128)S(1)}, u32[]{:S(2)}, u32[]{:S(2)}) collective-permute-start(f32[48,128]{1,0:T(8,128)S(1)} %get-tuple-element.39), channel_id=1, source_target_pairs={{0,13},{1,12},{2,15},{3,14},{4,1},{5,0},{6,3},{7,2},{8,5},{9,4},{1... | collective-permute-start | bytes 73736 | tf_op jit(solution)/shard_map/ppermute | solution.py:1029

commit v8 on v7

--- a/solution.py
+++ b/solution.py
@@ -342,7 +342,8 @@
 COARSE_M = [0, 31]
 COLUMNS = 192
 R_ROW = COLUMNS - 8
-FACE = 7 * HALO
+NEAR = 64
+FACE = 6 * HALO + NEAR
 
 
 def wanted(grid):
@@ -361,7 +362,7 @@
 
 
 def material_loads(grid, gz, m_hbm, m_face, m_ends, sems):
-    face = pl.ds((1 - gz) * (ROWS - HALO), HALO)
+    face = pl.ds((1 - gz) * (ROWS - NEAR), NEAR)
     loads = [pltpu.make_async_copy(m_hbm.at[face], m_face, sems.at[0])]
     for end, tiles in enumerate(edge_tiles(grid, m_hbm)):
         place = m_ends.at[end].reshape(8, 8, 128).at[pl.ds(0, grid.own)]
@@ -454,7 +455,7 @@
             zmsg[pl.ds(HALO * comp, HALO), :] = h_own[comp, edge, :]
             zmsg[pl.ds(HALO * (3 + comp), HALO), :] = e_own[comp, edge, :]
         if grid is Fine:
-            zmsg[pl.ds(6 * HALO, HALO), :] = m_face[...].astype(F32)
+            zmsg[pl.ds(6 * HALO, NEAR), :] = m_face[...].astype(F32)
         zmsg[pl.ds(FACE, COLUMNS), :] = columns[...]
 
     by_level(body)
@@ -688,10 +689,9 @@
                 found = jnp.where(is_material(i), parts[i], found)
             return found
 
-        for start in range(0, HALO if grid is Fine else 0, CHUNK):
-            layer, rest = divmod(start, grid.depth)
+        for start in range(0, NEAR if grid is Fine else 0, CHUNK):
             material = zmsg[pl.ds(6 * HALO + start, CHUNK), :]
-            row = layer_row(grid, halo + layer) + rest
+            row = layer_row(grid, halo + gz) + start
             c_ext[pl.ds(row, CHUNK), :] = coef(lambda i, m=material: m == float(i), CHUNK)
         for start in range(0, ROWS, CHUNK):
             layer, rest = divmod(start, grid.depth)
@@ -1043,7 +1043,7 @@
     )(far(e), far(h))
     m_face, m_ends = kernel_call(
         fine_material,
-        [vmem(HALO, 128, dtype=jnp.int32), vmem(2, 64, 128, dtype=jnp.int32)],
+        [vmem(NEAR, 128, dtype=jnp.int32), vmem(2, 64, 128, dtype=jnp.int32)],
         [HBM, VM],
         [VM] * 2,
         [dma((3,))],

time: 13.4 us -> 13.4 us (level)
  no operation moved by 1% of the time
where the time goes in v8:
time: 13.4 us; the launch traced here: 13.2 us
  starting transfers between devices  7.43 us (55%)
  Pallas kernels  4.24 us (32%)
  waiting for transfers between devices  0.84 us (6%)
  between operations  0.7 us (5%)
    ppermute x6, starting transfers between devices, across(): return lax.ppermute(x, ('gx', 'gy', 'gz'), pairs)  7.43 us
    pallas_call x1, Pallas kernels, fast_shards(): kernel_call(advance, [whole, whole, vmem(2, 3, 64, 128), vmem(2, 3, 64, 1...  1.33 us
    pallas_call x1, Pallas kernels, fast_shards(): kernel_call(peek, vmem(8, 128), [HBM] * 2, VM, [pltpu.VMEM((2, 3, 16, 128...  1.04 us
    ppermute x6, waiting for transfers between devices, across(): return lax.ppermute(x, ('gx', 'gy', 'gz'), pairs)  0.84 us
    pallas_call x1, Pallas kernels, fast_shards(): kernel_call(extend, [vmem(3, EXT, 128), vmem(3, EXT, 128), vmem(EXT, 128)...  0.78 us
    pallas_call x1, Pallas kernels, fast_shards(): kernel_call(correct, [whole, whole, vmem(2, 3, 64, 128), vmem(2, 3, 64, 1...  0.77 us
  transfers between devices with their start and end apart: 6, of which 4 were waited for; matrix products, arithmetic and copies ran while one was open for 0% of the time, Pallas kernels for 18%

profile of v8, /device:TPU:0, one launch (start us, length us, event | category | flops | bytes accessed | tf_op | source)
XLA Modules:
  0.0 13.2 jit_solution(5280626410464695664)
XLA Ops:
  0.6 0.0 copy-start.1
  0.6 0.0 copy-start
  0.6 1.0 %shard_map.59.after = f32[8,128]{1,0:T(8,128)S(1)} custom-call(f32[3,512,128]{2,1,0:T(8,128)} %bitcast.5, f32[3,512,128]{2,1,0:T(8,128)} %bitcast.8), custom_call_target="tpu_custom_call" | custom-call | tf_op jit(solution)/shard_map/pallas_call | solution.py:1037
  1.7 0.5 %collective-permute-start.1 = (f32[8,128]{1,0:T(8,128)S(1)}, f32[8,128]{1,0:T(8,128)S(1)}, u32[]{:S(2)}, u32[]{:S(2)}) collective-permute-start(f32[8,128]{1,0:T(8,128)S(1)} %shard_map.59.after), channel_id=1, source_target_pairs={{0,1},{1,0},{2,3},{3,2},{4,5},{5,4},{6,7},{7,6},{8,9},{9,8},{10,11... | collective-permute-start | bytes 12296 | tf_op jit(solution)/shard_map/ppermute | solution.py:1029
  2.3 0.0 copy-done.1
  2.3 0.0 copy-done
  2.3 0.2 %shard_map.61 = (f32[1024,128]{1,0:T(8,128)S(1)}, f32[8,128]{1,0:T(8,128)S(1)}, f32[192,128]{1,0:T(8,128)S(1)}) custom-call(f32[3,512,128]{2,1,0:T(8,128)S(1)} %bitcast.6, f32[3,512,128]{2,1,0:T(8,128)S(1)} %bitcast.9, s32[64,128]{1,0:T(8,128)S(1)} %get-tuple-element.24.m_face, s32[2,64,128]{2,1,0:T(8,128)S(1)} %get-tuple-element.25.m_ends), custom_call_target="tpu_custom_call" | custom-call | tf_op jit(solution)/shard_map/pallas_call | solution.py:1052
  2.5 0.3 %collective-permute-start = (f32[1024,128]{1,0:T(8,128)S(1)}, f32[1024,128]{1,0:T(8,128)S(1)}, u32[]{:S(2)}, u32[]{:S(2)}) collective-permute-start(f32[1024,128]{1,0:T(8,128)S(1)} %get-tuple-element.26), channel_id=1, source_target_pairs={{0,1},{1,0},{2,3},{3,2},{4,5},{5,4},{6,7},{7,6},{8,9},{9,8},{10,11... | collective-permute-start | bytes 1572872 | tf_op jit(solution)/shard_map/ppermute | solution.py:1029
  2.8 0.3 %collective-permute-done.1.edge_tile = f32[8,128]{1,0:T(8,128)S(1)} collective-permute-done((f32[8,128]{1,0:T(8,128)S(1)}, f32[8,128]{1,0:T(8,128)S(1)}, u32[]{:S(2)}, u32[]{:S(2)}) %collective-permute-start.1) | collective-permute-done | bytes 4128 | tf_op jit(solution)/shard_map/ppermute | solution.py:1029
  3.0 0.0 copy-start.2
  3.0 2.4 %collective-permute-start.3 = (f32[8,128]{1,0:T(8,128)S(1)}, f32[8,128]{1,0:T(8,128)S(1)}, u32[]{:S(2)}, u32[]{:S(2)}) collective-permute-start(f32[8,128]{1,0:T(8,128)S(1)} %shard_map.63), channel_id=1, source_target_pairs={{0,3},{1,2},{2,1},{3,0},{4,7},{5,6},{6,5},{7,4},{8,11},{9,10},{10,... | collective-permute-start | bytes 12296 | tf_op jit(solution)/shard_map/ppermute | solution.py:1029
  5.4 0.1 %collective-permute-start.2 = (f32[8,128]{1,0:T(8,128)S(1)}, f32[8,128]{1,0:T(8,128)S(1)}, u32[]{:S(2)}, u32[]{:S(2)}) collective-permute-start(f32[8,128]{1,0:T(8,128)S(1)} %shard_map.63), channel_id=1, source_target_pairs={{0,2},{1,3},{2,0},{3,1},{4,6},{5,7},{6,4},{7,5},{8,10},{9,11},{10,... | collective-permute-start | bytes 12296 | tf_op jit(solution)/shard_map/ppermute | solution.py:1029
  5.6 0.0 collective-permute-done.zmsg.r_other
  5.6 0.0 copy-done.2
  5.6 0.8 %shard_map.62 = (f32[3,1296,128]{2,1,0:T(8,128)S(1)}, f32[3,1296,128]{2,1,0:T(8,128)S(1)}, f32[1296,128]{1,0:T(8,128)S(1)}, f32[96,128]{1,0:T(8,128)S(1)}, f32[9...) custom-call(f32[3,512,128]{2,1,0:T(8,128)S(1)} %bitcast.7, ...), custom_call_target="tpu_custom_call" | custom-call | tf_op jit(solution)/shard_map/pallas_call | solution.py:1068
  6.3 0.4 %collective-permute-done.3.yzin = f32[8,128]{1,0:T(8,128)S(1)} collective-permute-done((f32[8,128]{1,0:T(8,128)S(1)}, f32[8,128]{1,0:T(8,128)S(1)}, u32[]{:S(2)}, u32[]{:S(2)}) %collective-permute-start.3) | collective-permute-done | bytes 4128 | tf_op jit(solution)/shard_map/ppermute | solution.py:1029
  6.7 0.1 shard_map.65
  6.8 2.0 %collective-permute-start.4 = (f32[48,128]{1,0:T(8,128)S(1)}, f32[48,128]{1,0:T(8,128)S(1)}, u32[]{:S(2)}, u32[]{:S(2)}) collective-permute-start(f32[48,128]{1,0:T(8,128)S(1)} %get-tuple-element.38), channel_id=1, source_target_pairs={{0,5},{1,4},{2,7},{3,6},{4,9},{5,8},{6,11},{7,10},{8,13},{9,12},{1... | collective-permute-start | bytes 73736 | tf_op jit(solution)/shard_map/ppermute | solution.py:1029
  8.9 2.1 %collective-permute-start.5 = (f32[48,128]{1,0:T(8,128)S(1)}, f32[48,128]{1,0:T(8,128)S(1)}, u32[]{:S(2)}, u32[]{:S(2)}) collective-permute-start(f32[48,128]{1,0:T(8,128)S(1)} %get-tuple-element.39), channel_id=1, source_target_pairs={{0,13},{1,12},{2,15},{3,14},{4,1},{5,0},{6,3},{7,2},{8,5},{9,4},{1... | collective-permute-start | bytes 73736 | tf_op jit(solution)/shard_map/ppermute | solution.py:1029
  10.9 0.0 collective-permute-done.2.yin
  10.9 1.3 %shard_map.64 = (f32[3,512,128]{2,1,0:T(8,128)}, f32[3,512,128]{2,1,0:T(8,128)}, f32[2,3,64,128]{3,2,1,0:T(8,128)S(1)}, f32[2,3,64,128]{3,2,1,0:T(8,128)S(1)}, f32[32,128]{1,0:T(8,128)S(1)}) custom-call(f32[3,1296,128]{2,1,0:T(8,128)S(1)} %get-tuple-element.31.e_ext, f32[3,1296,128]{2,1,0:T(8,128)S(1)} %get-tuple-element.32.h_ext, ...), custom_call_target="tpu_custom_call" | custom-call | flops 10000000000 | bytes 100000000 | tf_op jit(solution)/shard_map/pallas_call | solution.py:1093
  12.3 0.1 collective-permute-done.4.from_below
  12.4 0.1 collective-permute-done.5.from_above
  12.4 0.8 %shard_map.66 = (f32[3,512,128]{2,1,0:T(8,128)}, f32[3,512,128]{2,1,0:T(8,128)}, f32[2,3,64,128]{3,2,1,0:T(8,128)S(1)}, f32[2,3,64,128]{3,2,1,0:T(8,128)S(1)}) custom-call(f32[96,128]{1,0:T(8,128)S(1)} %get-tuple-element.28.up, f32[96,128]{1,0:T(8,128)S(1)} %get-tuple-element.29.down, ...), custom_call_target="tpu_custom_call", output_to_operand_aliasing={{0}: (8, {}), {1}: (9, {}), {2}: (6, {}), {3}: (7, {})} | custom-call | tf_op jit(solution)/shard_map/pallas_call | solution.py:1101
  (2 shorter events, 0.0 us)
Async XLA Ops:
  0.6 1.6 %copy-start.1 = (f32[1,1,1,3,65536]{4,2,3,1,0:T(1,128)S(1)}, f32[1,1,1,3,65536]{4,2,3,1,0:T(1,128)}, u32[]{:S(2)}) copy-start(f32[1,1,1,3,65536]{4,2,3,1,0:T(1,128)} %param.5) | copy-start | bytes 2359300
  0.6 1.6 %copy-start = (f32[1,1,1,3,65536]{4,2,3,1,0:T(1,128)S(1)}, f32[1,1,1,3,65536]{4,2,3,1,0:T(1,128)}, u32[]{:S(2)}) copy-start(f32[1,1,1,3,65536]{4,2,3,1,0:T(1,128)} %param.4) | copy-start | bytes 2359300
  1.7 1.3 %collective-permute-start.1 = (f32[8,128]{1,0:T(8,128)S(1)}, f32[8,128]{1,0:T(8,128)S(1)}, u32[]{:S(2)}, u32[]{:S(2)}) collective-permute-start(f32[8,128]{1,0:T(8,128)S(1)} %shard_map.59.after), channel_id=1, source_target_pairs={{0,1},{1,0},{2,3},{3,2},{4,5},{5,4},{6,7},{7,6},{8,9},{9,8},{10,11... | collective-permute-start | bytes 12296 | tf_op jit(solution)/shard_map/ppermute | solution.py:1029
  2.5 3.1 %collective-permute-start = (f32[1024,128]{1,0:T(8,128)S(1)}, f32[1024,128]{1,0:T(8,128)S(1)}, u32[]{:S(2)}, u32[]{:S(2)}) collective-permute-start(f32[1024,128]{1,0:T(8,128)S(1)} %get-tuple-element.26), channel_id=1, source_target_pairs={{0,1},{1,0},{2,3},{3,2},{4,5},{5,4},{6,7},{7,6},{8,9},{9,8},{10,11... | collective-permute-start | bytes 1572872 | tf_op jit(solution)/shard_map/ppermute | solution.py:1029
  3.0 2.5 %copy-start.2 = (s32[1,1,1,65536]{3,2,1,0:T(1,128)S(1)}, s32[1,1,1,65536]{3,2,1,0:T(1,128)}, u32[]{:S(2)}) copy-start(s32[1,1,1,65536]{3,2,1,0:T(1,128)} %param.6) | copy-start | bytes 786436
  3.0 3.7 %collective-permute-start.3 = (f32[8,128]{1,0:T(8,128)S(1)}, f32[8,128]{1,0:T(8,128)S(1)}, u32[]{:S(2)}, u32[]{:S(2)}) collective-permute-start(f32[8,128]{1,0:T(8,128)S(1)} %shard_map.63), channel_id=1, source_target_pairs={{0,3},{1,2},{2,1},{3,0},{4,7},{5,6},{6,5},{7,4},{8,11},{9,10},{10,... | collective-permute-start | bytes 12296 | tf_op jit(solution)/shard_map/ppermute | solution.py:1029
  5.4 5.5 %collective-permute-start.2 = (f32[8,128]{1,0:T(8,128)S(1)}, f32[8,128]{1,0:T(8,128)S(1)}, u32[]{:S(2)}, u32[]{:S(2)}) collective-permute-start(f32[8,128]{1,0:T(8,128)S(1)} %shard_map.63), channel_id=1, source_target_pairs={{0,2},{1,3},{2,0},{3,1},{4,6},{5,7},{6,4},{7,5},{8,10},{9,11},{10,... | collective-permute-start | bytes 12296 | tf_op jit(solution)/shard_map/ppermute | solution.py:1029
  6.8 5.6 %collective-permute-start.4 = (f32[48,128]{1,0:T(8,128)S(1)}, f32[48,128]{1,0:T(8,128)S(1)}, u32[]{:S(2)}, u32[]{:S(2)}) collective-permute-start(f32[48,128]{1,0:T(8,128)S(1)} %get-tuple-element.38), channel_id=1, source_target_pairs={{0,5},{1,4},{2,7},{3,6},{4,9},{5,8},{6,11},{7,10},{8,13},{9,12},{1... | collective-permute-start | bytes 73736 | tf_op jit(solution)/shard_map/ppermute | solution.py:1029
  8.9 3.6 %collective-permute-start.5 = (f32[48,128]{1,0:T(8,128)S(1)}, f32[48,128]{1,0:T(8,128)S(1)}, u32[]{:S(2)}, u32[]{:S(2)}) collective-permute-start(f32[48,128]{1,0:T(8,128)S(1)} %get-tuple-element.39), channel_id=1, source_target_pairs={{0,13},{1,12},{2,15},{3,14},{4,1},{5,0},{6,3},{7,2},{8,5},{9,4},{1... | collective-permute-start | bytes 73736 | tf_op jit(solution)/shard_map/ppermute | solution.py:1029

commit v9 on v8

--- a/solution.py
+++ b/solution.py
@@ -228,7 +228,7 @@
 VM = pl.BlockSpec(memory_space=pltpu.VMEM)
 HBM = pl.BlockSpec(memory_space=pltpu.HBM)
 CHUNK = 32
-SKEW = 2
+SKEW = 3
 
 
 class Fine:

time: 13.4 us -> 13.4 us (level)
  no operation moved by 1% of the time
where the time goes in v9:
time: 13.4 us; the launch traced here: 13.2 us
  starting transfers between devices  7.43 us (55%)
  Pallas kernels  4.24 us (32%)
  waiting for transfers between devices  0.84 us (6%)
  between operations  0.7 us (5%)
    ppermute x6, starting transfers between devices, across(): return lax.ppermute(x, ('gx', 'gy', 'gz'), pairs)  7.43 us
    pallas_call x1, Pallas kernels, fast_shards(): kernel_call(advance, [whole, whole, vmem(2, 3, 64, 128), vmem(2, 3, 64, 1...  1.33 us
    pallas_call x1, Pallas kernels, fast_shards(): kernel_call(peek, vmem(8, 128), [HBM] * 2, VM, [pltpu.VMEM((2, 3, 16, 128...  1.04 us
    ppermute x6, waiting for transfers between devices, across(): return lax.ppermute(x, ('gx', 'gy', 'gz'), pairs)  0.84 us
    pallas_call x1, Pallas kernels, fast_shards(): kernel_call(extend, [vmem(3, EXT, 128), vmem(3, EXT, 128), vmem(EXT, 128)...  0.78 us
    pallas_call x1, Pallas kernels, fast_shards(): kernel_call(correct, [whole, whole, vmem(2, 3, 64, 128), vmem(2, 3, 64, 1...  0.77 us
  transfers between devices with their start and end apart: 6, of which 4 were waited for; matrix products, arithmetic and copies ran while one was open for 0% of the time, Pallas kernels for 18%

profile of v9, /device:TPU:0, one launch (start us, length us, event | category | flops | bytes accessed | tf_op | source)
XLA Modules:
  0.0 13.2 jit_solution(8319184092130782629)
XLA Ops:
  0.6 0.0 copy-start.1
  0.6 0.0 copy-start
  0.6 1.0 %shard_map.59.after = f32[8,128]{1,0:T(8,128)S(1)} custom-call(f32[3,512,128]{2,1,0:T(8,128)} %bitcast.5, f32[3,512,128]{2,1,0:T(8,128)} %bitcast.8), custom_call_target="tpu_custom_call" | custom-call | tf_op jit(solution)/shard_map/pallas_call | solution.py:1037
  1.7 0.5 %collective-permute-start.1 = (f32[8,128]{1,0:T(8,128)S(1)}, f32[8,128]{1,0:T(8,128)S(1)}, u32[]{:S(2)}, u32[]{:S(2)}) collective-permute-start(f32[8,128]{1,0:T(8,128)S(1)} %shard_map.59.after), channel_id=1, source_target_pairs={{0,1},{1,0},{2,3},{3,2},{4,5},{5,4},{6,7},{7,6},{8,9},{9,8},{10,11... | collective-permute-start | bytes 12296 | tf_op jit(solution)/shard_map/ppermute | solution.py:1029
  2.3 0.0 copy-done.1
  2.3 0.0 copy-done
  2.3 0.2 %shard_map.61 = (f32[1024,128]{1,0:T(8,128)S(1)}, f32[8,128]{1,0:T(8,128)S(1)}, f32[192,128]{1,0:T(8,128)S(1)}) custom-call(f32[3,512,128]{2,1,0:T(8,128)S(1)} %bitcast.6, f32[3,512,128]{2,1,0:T(8,128)S(1)} %bitcast.9, s32[64,128]{1,0:T(8,128)S(1)} %get-tuple-element.24.m_face, s32[2,64,128]{2,1,0:T(8,128)S(1)} %get-tuple-element.25.m_ends), custom_call_target="tpu_custom_call" | custom-call | tf_op jit(solution)/shard_map/pallas_call | solution.py:1052
  2.5 0.3 %collective-permute-start = (f32[1024,128]{1,0:T(8,128)S(1)}, f32[1024,128]{1,0:T(8,128)S(1)}, u32[]{:S(2)}, u32[]{:S(2)}) collective-permute-start(f32[1024,128]{1,0:T(8,128)S(1)} %get-tuple-element.26), channel_id=1, source_target_pairs={{0,1},{1,0},{2,3},{3,2},{4,5},{5,4},{6,7},{7,6},{8,9},{9,8},{10,11... | collective-permute-start | bytes 1572872 | tf_op jit(solution)/shard_map/ppermute | solution.py:1029
  2.8 0.3 %collective-permute-done.1.edge_tile = f32[8,128]{1,0:T(8,128)S(1)} collective-permute-done((f32[8,128]{1,0:T(8,128)S(1)}, f32[8,128]{1,0:T(8,128)S(1)}, u32[]{:S(2)}, u32[]{:S(2)}) %collective-permute-start.1) | collective-permute-done | bytes 4128 | tf_op jit(solution)/shard_map/ppermute | solution.py:1029
  3.0 0.0 copy-start.2
  3.0 2.4 %collective-permute-start.3 = (f32[8,128]{1,0:T(8,128)S(1)}, f32[8,128]{1,0:T(8,128)S(1)}, u32[]{:S(2)}, u32[]{:S(2)}) collective-permute-start(f32[8,128]{1,0:T(8,128)S(1)} %shard_map.63), channel_id=1, source_target_pairs={{0,3},{1,2},{2,1},{3,0},{4,7},{5,6},{6,5},{7,4},{8,11},{9,10},{10,... | collective-permute-start | bytes 12296 | tf_op jit(solution)/shard_map/ppermute | solution.py:1029
  5.4 0.1 %collective-permute-start.2 = (f32[8,128]{1,0:T(8,128)S(1)}, f32[8,128]{1,0:T(8,128)S(1)}, u32[]{:S(2)}, u32[]{:S(2)}) collective-permute-start(f32[8,128]{1,0:T(8,128)S(1)} %shard_map.63), channel_id=1, source_target_pairs={{0,2},{1,3},{2,0},{3,1},{4,6},{5,7},{6,4},{7,5},{8,10},{9,11},{10,... | collective-permute-start | bytes 12296 | tf_op jit(solution)/shard_map/ppermute | solution.py:1029
  5.6 0.0 collective-permute-done.zmsg.r_other
  5.6 0.0 copy-done.2
  5.6 0.8 %shard_map.62 = (f32[3,1296,128]{2,1,0:T(8,128)S(1)}, f32[3,1296,128]{2,1,0:T(8,128)S(1)}, f32[1296,128]{1,0:T(8,128)S(1)}, f32[96,128]{1,0:T(8,128)S(1)}, f32[9...) custom-call(f32[3,512,128]{2,1,0:T(8,128)S(1)} %bitcast.7, ...), custom_call_target="tpu_custom_call" | custom-call | tf_op jit(solution)/shard_map/pallas_call | solution.py:1068
  6.3 0.4 %collective-permute-done.3.yzin = f32[8,128]{1,0:T(8,128)S(1)} collective-permute-done((f32[8,128]{1,0:T(8,128)S(1)}, f32[8,128]{1,0:T(8,128)S(1)}, u32[]{:S(2)}, u32[]{:S(2)}) %collective-permute-start.3) | collective-permute-done | bytes 4128 | tf_op jit(solution)/shard_map/ppermute | solution.py:1029
  6.7 0.1 shard_map.65
  6.8 2.0 %collective-permute-start.4 = (f32[48,128]{1,0:T(8,128)S(1)}, f32[48,128]{1,0:T(8,128)S(1)}, u32[]{:S(2)}, u32[]{:S(2)}) collective-permute-start(f32[48,128]{1,0:T(8,128)S(1)} %get-tuple-element.38), channel_id=1, source_target_pairs={{0,5},{1,4},{2,7},{3,6},{4,9},{5,8},{6,11},{7,10},{8,13},{9,12},{1... | collective-permute-start | bytes 73736 | tf_op jit(solution)/shard_map/ppermute | solution.py:1029
  8.9 2.1 %collective-permute-start.5 = (f32[48,128]{1,0:T(8,128)S(1)}, f32[48,128]{1,0:T(8,128)S(1)}, u32[]{:S(2)}, u32[]{:S(2)}) collective-permute-start(f32[48,128]{1,0:T(8,128)S(1)} %get-tuple-element.39), channel_id=1, source_target_pairs={{0,13},{1,12},{2,15},{3,14},{4,1},{5,0},{6,3},{7,2},{8,5},{9,4},{1... | collective-permute-start | bytes 73736 | tf_op jit(solution)/shard_map/ppermute | solution.py:1029
  10.9 0.0 collective-permute-done.2.yin
  10.9 1.3 %shard_map.64 = (f32[3,512,128]{2,1,0:T(8,128)}, f32[3,512,128]{2,1,0:T(8,128)}, f32[2,3,64,128]{3,2,1,0:T(8,128)S(1)}, f32[2,3,64,128]{3,2,1,0:T(8,128)S(1)}, f32[32,128]{1,0:T(8,128)S(1)}) custom-call(f32[3,1296,128]{2,1,0:T(8,128)S(1)} %get-tuple-element.31.e_ext, f32[3,1296,128]{2,1,0:T(8,128)S(1)} %get-tuple-element.32.h_ext, ...), custom_call_target="tpu_custom_call" | custom-call | flops 10000000000 | bytes 100000000 | tf_op jit(solution)/shard_map/pallas_call | solution.py:1093
  12.3 0.1 collective-permute-done.4.from_below
  12.4 0.1 collective-permute-done.5.from_above
  12.4 0.8 %shard_map.66 = (f32[3,512,128]{2,1,0:T(8,128)}, f32[3,512,128]{2,1,0:T(8,128)}, f32[2,3,64,128]{3,2,1,0:T(8,128)S(1)}, f32[2,3,64,128]{3,2,1,0:T(8,128)S(1)}) custom-call(f32[96,128]{1,0:T(8,128)S(1)} %get-tuple-element.28.up, f32[96,128]{1,0:T(8,128)S(1)} %get-tuple-element.29.down, ...), custom_call_target="tpu_custom_call", output_to_operand_aliasing={{0}: (8, {}), {1}: (9, {}), {2}: (6, {}), {3}: (7, {})} | custom-call | tf_op jit(solution)/shard_map/pallas_call | solution.py:1101
  (2 shorter events, 0.0 us)
Async XLA Ops:
  0.6 1.6 %copy-start.1 = (f32[1,1,1,3,65536]{4,2,3,1,0:T(1,128)S(1)}, f32[1,1,1,3,65536]{4,2,3,1,0:T(1,128)}, u32[]{:S(2)}) copy-start(f32[1,1,1,3,65536]{4,2,3,1,0:T(1,128)} %param.5) | copy-start | bytes 2359300
  0.6 1.6 %copy-start = (f32[1,1,1,3,65536]{4,2,3,1,0:T(1,128)S(1)}, f32[1,1,1,3,65536]{4,2,3,1,0:T(1,128)}, u32[]{:S(2)}) copy-start(f32[1,1,1,3,65536]{4,2,3,1,0:T(1,128)} %param.4) | copy-start | bytes 2359300
  1.7 1.3 %collective-permute-start.1 = (f32[8,128]{1,0:T(8,128)S(1)}, f32[8,128]{1,0:T(8,128)S(1)}, u32[]{:S(2)}, u32[]{:S(2)}) collective-permute-start(f32[8,128]{1,0:T(8,128)S(1)} %shard_map.59.after), channel_id=1, source_target_pairs={{0,1},{1,0},{2,3},{3,2},{4,5},{5,4},{6,7},{7,6},{8,9},{9,8},{10,11... | collective-permute-start | bytes 12296 | tf_op jit(solution)/shard_map/ppermute | solution.py:1029
  2.5 3.1 %collective-permute-start = (f32[1024,128]{1,0:T(8,128)S(1)}, f32[1024,128]{1,0:T(8,128)S(1)}, u32[]{:S(2)}, u32[]{:S(2)}) collective-permute-start(f32[1024,128]{1,0:T(8,128)S(1)} %get-tuple-element.26), channel_id=1, source_target_pairs={{0,1},{1,0},{2,3},{3,2},{4,5},{5,4},{6,7},{7,6},{8,9},{9,8},{10,11... | collective-permute-start | bytes 1572872 | tf_op jit(solution)/shard_map/ppermute | solution.py:1029
  3.0 2.5 %copy-start.2 = (s32[1,1,1,65536]{3,2,1,0:T(1,128)S(1)}, s32[1,1,1,65536]{3,2,1,0:T(1,128)}, u32[]{:S(2)}) copy-start(s32[1,1,1,65536]{3,2,1,0:T(1,128)} %param.6) | copy-start | bytes 786436
  3.0 3.7 %collective-permute-start.3 = (f32[8,128]{1,0:T(8,128)S(1)}, f32[8,128]{1,0:T(8,128)S(1)}, u32[]{:S(2)}, u32[]{:S(2)}) collective-permute-start(f32[8,128]{1,0:T(8,128)S(1)} %shard_map.63), channel_id=1, source_target_pairs={{0,3},{1,2},{2,1},{3,0},{4,7},{5,6},{6,5},{7,4},{8,11},{9,10},{10,... | collective-permute-start | bytes 12296 | tf_op jit(solution)/shard_map/ppermute | solution.py:1029
  5.4 5.5 %collective-permute-start.2 = (f32[8,128]{1,0:T(8,128)S(1)}, f32[8,128]{1,0:T(8,128)S(1)}, u32[]{:S(2)}, u32[]{:S(2)}) collective-permute-start(f32[8,128]{1,0:T(8,128)S(1)} %shard_map.63), channel_id=1, source_target_pairs={{0,2},{1,3},{2,0},{3,1},{4,6},{5,7},{6,4},{7,5},{8,10},{9,11},{10,... | collective-permute-start | bytes 12296 | tf_op jit(solution)/shard_map/ppermute | solution.py:1029
  6.8 5.6 %collective-permute-start.4 = (f32[48,128]{1,0:T(8,128)S(1)}, f32[48,128]{1,0:T(8,128)S(1)}, u32[]{:S(2)}, u32[]{:S(2)}) collective-permute-start(f32[48,128]{1,0:T(8,128)S(1)} %get-tuple-element.38), channel_id=1, source_target_pairs={{0,5},{1,4},{2,7},{3,6},{4,9},{5,8},{6,11},{7,10},{8,13},{9,12},{1... | collective-permute-start | bytes 73736 | tf_op jit(solution)/shard_map/ppermute | solution.py:1029
  8.9 3.6 %collective-permute-start.5 = (f32[48,128]{1,0:T(8,128)S(1)}, f32[48,128]{1,0:T(8,128)S(1)}, u32[]{:S(2)}, u32[]{:S(2)}) collective-permute-start(f32[48,128]{1,0:T(8,128)S(1)} %get-tuple-element.39), channel_id=1, source_target_pairs={{0,13},{1,12},{2,15},{3,14},{4,1},{5,0},{6,3},{7,2},{8,5},{9,4},{1... | collective-permute-start | bytes 73736 | tf_op jit(solution)/shard_map/ppermute | solution.py:1029
